TPU v7x, 32 devices: a whole 2x2x4 slice. The times are simulated.
32 devices in a mesh: dp: 4 (over y, x), fsdp: 8 (over z, core).
Axes of the slice: x: 2, y: 2, z: 4, core: 2. Of those that a mesh axis runs over, the one named last changes fastest.
Arguments:
- hidden_in: bfloat16 [8, 1024, 1536], P('dp', 'fsdp'), may hold values from -6 to 6
- doc_lengths: int32 [8, 1], P('dp'), may hold values from 0 to 1024, as said below
- norm_gain: bfloat16 [2, 1536], P(None, 'fsdp'), may hold values from 0.5 to 1.5
- input_proj: bfloat16 [2, 1536, 6400], P(None, 'fsdp'), may hold values from -0.15625 to 0.15625
- step_proj: bfloat16 [2, 48, 1536], P(None, None, 'fsdp'), may hold values from -0.15625 to 0.15625
- conv_weight: bfloat16 [2, 4, 3328], P(None, None, 'fsdp'), may hold values from -3 to 3
- conv_bias: bfloat16 [2, 3328], P(None, 'fsdp'), may hold values from -3 to 3
- step_bias: bfloat16 [2, 48], P(None, 'fsdp'), may hold values from -10.5 to -2.9
- decay_log: bfloat16 [2, 48], P(None, 'fsdp'), may hold values from 0 to 0.69921875
- skip_gain: bfloat16 [2, 48], P(None, 'fsdp'), may hold values from 0.5 to 1.5
- gate_gain: bfloat16 [2, 3072], P(None, 'fsdp'), may hold values from 0.5 to 1.5
- output_proj: bfloat16 [2, 3072, 1536], P(None, 'fsdp'), may hold values from -0.109375 to 0.109375
- cotangent: bfloat16 [8, 1024, 1536], P('dp', 'fsdp'), may hold values from -6 to 6
Outputs:
- hidden_out: bfloat16 [8, 1024, 1536], P('dp', 'fsdp')
- hidden_grad: float32 [8, 1024, 1536], P('dp', 'fsdp')
- norm_gain_grad: float32 [2, 1536], P(None, 'fsdp')
- input_proj_grad: float32 [2, 1536, 6400], P(None, 'fsdp')
- step_proj_grad: float32 [2, 48, 1536], P(None, None, 'fsdp')
- conv_weight_grad: float32 [2, 4, 3328], P(None, None, 'fsdp')
- conv_bias_grad: float32 [2, 3328], P(None, 'fsdp')
- step_bias_grad: float32 [2, 48], P(None, 'fsdp')
- decay_log_grad: float32 [2, 48], P(None, 'fsdp')
- skip_gain_grad: float32 [2, 48], P(None, 'fsdp')
- gate_gain_grad: float32 [2, 3072], P(None, 'fsdp')
- output_proj_grad: float32 [2, 3072, 1536], P(None, 'fsdp')
Inputs may be any that keep to these rules, and one draw needn't show every extreme that they name: `doc_lengths`: row r lists the documents of packed sequence r in order: its entries sum to 1024, each entry is 0 or at least 1024, the first is not 0; of the 2 rows of each index of dp at least one holds a single document.
All inputs are finite; a program needn't handle non-finite values.
Results may differ from a plain program's by a relative error of at most 0.022.
Values may be sent and summed in bfloat16 or wider, within the bound.
No kernel may reach another device: no remote copies, remote signals or barrier semaphores. Data moves between devices by JAX's collectives and lax.ppermute only.
A program may use at most 384 MiB of HBM per device.

v0:
```python
from functools import partial

import jax
import jax.numpy as jnp
from jax import lax
from jax.sharding import PartitionSpec as P

INNER = 3072
HEADS = 48
HEAD_DIM = 64
STATE = 128


EPSILON = 1e-05
HIGHEST = lax.Precision.HIGHEST


def from_behind(value, axis, steps):
    count = lax.axis_size(axis)
    initial, last = (max(0, -steps), min(count, count - steps))
    return lax.ppermute(value, axis, [(source, source + steps) for source in range(initial, last)])


def carried_in(value, axis, combine, identity):
    size, mine = (lax.axis_size(axis), lax.axis_index(axis))
    everything = jax.tree.map(
        lambda part, kind: lax.all_gather(part.astype(kind), axis),
        value,
        (jnp.bfloat16, jnp.bfloat16),
    )
    start = jax.tree.map(
        lambda part, zero: jnp.broadcast_to(jnp.asarray(zero, part.dtype), part.shape),
        value,
        identity,
    )

    def hop(k, before):
        reached = k < mine
        new = combine(
            before, jax.tree.map(lambda part, own: part[k].astype(own.dtype), everything, value)
        )
        return jax.tree.map(lambda a, b: jnp.where(reached, a, b), new, before)

    return lax.fori_loop(0, size, hop, start)


def carried_in_2(value, axis, combine, identity):
    size, mine = (lax.axis_size(axis), lax.axis_index(axis))
    everything = jax.tree.map(
        lambda part, kind: lax.all_gather(part.astype(kind), axis),
        value,
        jax.tree.map(lambda a: jnp.bfloat16 if a.dtype == jnp.float32 else a.dtype, value),
    )
    start = jax.tree.map(
        lambda part, zero: jnp.broadcast_to(jnp.asarray(zero, part.dtype), part.shape),
        value,
        identity,
    )

    def hop(k, before):
        at = size - 1 - k
        reached = at > mine
        new = combine(
            before, jax.tree.map(lambda part, own: part[at].astype(own.dtype), everything, value)
        )
        return jax.tree.map(lambda a, b: jnp.where(reached, a, b), new, before)

    return lax.fori_loop(0, size, hop, start)


def as_sent(value):

    def short(part):
        return part.astype(jnp.bfloat16) if part.dtype == jnp.float32 else part

    return jax.tree.map(short, value)


def rms_scale(values, weight):
    inverse_rms = lax.rsqrt(jnp.mean(values * values, axis=-1, keepdims=True) + EPSILON)
    return values * inverse_rms * weight


def gate_norm(ssd_out, gate_row, weight):
    return rms_scale(ssd_out * jax.nn.silu(gate_row), weight)


def segment_ids(lengths_row, positions):
    doc_ends = jnp.cumsum(lengths_row)
    return jnp.sum((doc_ends[None, :] <= positions[:, None]).astype(jnp.int32), axis=1)


def convolve_block(extended, weight, bias_row, segment_wide):
    kernel_width = weight.shape[0]
    row_count = extended.shape[0] - kernel_width + 1
    own_segment = segment_wide[kernel_width - 1 :]
    summed = jnp.zeros((row_count, extended.shape[1]), jnp.float32) + bias_row[None, :]
    for offset in range(kernel_width):
        same_doc = (segment_wide[offset : offset + row_count] == own_segment)[:, None]
        summed = summed + weight[offset][None, :] * jnp.where(
            same_doc, extended[offset : offset + row_count], 0.0
        )
    return jax.nn.silu(summed)


def split_inputs(xbc):
    row_count = xbc.shape[0]
    values = xbc[:, :INNER].reshape(row_count, HEADS, HEAD_DIM)
    writers = xbc[:, INNER : INNER + STATE]
    readers = xbc[:, INNER + STATE :]
    return (values, writers, readers)


def decay_sums(step_raw, step_bias, decay_log):
    step_sizes = jax.nn.softplus(step_raw + step_bias[None, :])
    log_decay = jnp.cumsum(step_sizes * (-jnp.exp(decay_log))[None, :], axis=0)
    return (step_sizes, log_decay)


def summarize(xbc, step_raw, step_bias, decay_log, starts):
    values, writers, readers = split_inputs(xbc)
    step_sizes, log_decay = decay_sums(step_raw, step_bias, decay_log)
    row_count = xbc.shape[0]
    run_counts = jnp.cumsum(starts)
    live_mask = (run_counts == run_counts[-1]).astype(jnp.float32)
    weights = jnp.exp(log_decay[-1][None, :] - log_decay) * step_sizes * live_mask[:, None]
    scaled = (values * weights[:, :, None]).reshape(row_count, INNER)
    contrib = lax.dot_general(scaled, writers, (((0,), (0,)), ((), ())), precision=HIGHEST)
    decay_end = jnp.exp(log_decay[-1]) * (run_counts[-1] == 0).astype(jnp.float32)
    return (decay_end, contrib.reshape(HEADS, HEAD_DIM, STATE))


def respond(xbc, step_raw, step_bias, decay_log, skip_row, state_in, starts):
    values, writers, readers = split_inputs(xbc)
    step_sizes, log_decay = decay_sums(step_raw, step_bias, decay_log)
    row_count = xbc.shape[0]
    run_counts = jnp.cumsum(starts)
    positions = jnp.arange(row_count, dtype=jnp.int32)
    causal = (positions[:, None] >= positions[None, :]) & (
        run_counts[:, None] == run_counts[None, :]
    )
    scores = jnp.dot(readers, writers.T, precision=HIGHEST)
    head_logs = log_decay.T
    log_gaps = jnp.where(causal[None], head_logs[:, :, None] - head_logs[:, None, :], 0.0)
    mixing = jnp.where(causal[None], jnp.exp(log_gaps), 0.0) * scores[None]
    scaled = values * step_sizes[:, :, None]
    inner_part = jnp.einsum("hts,shp->thp", mixing, scaled, precision=HIGHEST)
    entering = jnp.exp(log_decay) * (run_counts == 0).astype(jnp.float32)[:, None]
    carried = jnp.einsum("hpn,tn->thp", state_in, readers, precision=HIGHEST) * entering[:, :, None]
    summed = inner_part + carried + skip_row[None, :, None] * values
    return summed.reshape(row_count, INNER)


def combine_states(earlier, latter):
    return (earlier[0] * latter[0], latter[0][:, None, None] * earlier[1] + latter[1])


def fetch_weights(shards, layer_index):
    (
        norm_piece,
        proj_piece,
        step_piece,
        conv_piece,
        cbias_piece,
        sbias_piece,
        decay_piece,
        skip_piece,
        gate_piece,
        out_piece,
    ) = tuple((shard_item[layer_index] for shard_item in shards))
    return (
        lax.all_gather(norm_piece, "fsdp", axis=0, tiled=True),
        lax.all_gather(proj_piece, "fsdp", axis=0, tiled=True),
        lax.all_gather(step_piece, "fsdp", axis=1, tiled=True),
        lax.all_gather(conv_piece, "fsdp", axis=1, tiled=True),
        lax.all_gather(cbias_piece, "fsdp", axis=0, tiled=True),
        lax.all_gather(sbias_piece, "fsdp", axis=0, tiled=True),
        lax.all_gather(decay_piece, "fsdp", axis=0, tiled=True),
        lax.all_gather(skip_piece, "fsdp", axis=0, tiled=True),
        lax.all_gather(gate_piece, "fsdp", axis=0, tiled=True),
        lax.all_gather(out_piece, "fsdp", axis=0, tiled=True),
    )


def fetch_again(shards, layer_index):
    (
        norm_piece,
        proj_piece,
        step_piece,
        conv_piece,
        cbias_piece,
        sbias_piece,
        decay_piece,
        skip_piece,
        gate_piece,
        out_piece,
    ) = tuple((shard_item[layer_index] for shard_item in shards))
    return (
        lax.all_gather(norm_piece, "fsdp", axis=0, tiled=True),
        lax.all_gather(proj_piece, "fsdp", axis=0, tiled=True),
        lax.all_gather(step_piece, "fsdp", axis=1, tiled=True),
        lax.all_gather(conv_piece, "fsdp", axis=1, tiled=True),
        lax.all_gather(cbias_piece, "fsdp", axis=0, tiled=True),
        lax.all_gather(sbias_piece, "fsdp", axis=0, tiled=True),
        lax.all_gather(decay_piece, "fsdp", axis=0, tiled=True),
        lax.all_gather(skip_piece, "fsdp", axis=0, tiled=True),
        lax.all_gather(gate_piece, "fsdp", axis=0, tiled=True),
        lax.all_gather(out_piece, "fsdp", axis=0, tiled=True),
    )


def reduce_grads(totals):
    (
        norm_total,
        proj_total,
        step_total,
        conv_total,
        cbias_total,
        sbias_total,
        decay_total,
        skip_total,
        gate_total,
        out_total,
    ) = totals
    (
        norm_share,
        proj_share,
        step_share,
        conv_share,
        cbias_share,
        sbias_share,
        decay_share,
        skip_share,
        gate_share,
        out_share,
    ) = (
        lax.psum_scatter(
            norm_total.astype(jnp.bfloat16), "fsdp", scatter_dimension=0, tiled=True
        ).astype(jnp.float32),
        lax.psum_scatter(
            proj_total.astype(jnp.bfloat16), "fsdp", scatter_dimension=0, tiled=True
        ).astype(jnp.float32),
        lax.psum_scatter(
            step_total.astype(jnp.bfloat16), "fsdp", scatter_dimension=1, tiled=True
        ).astype(jnp.float32),
        lax.psum_scatter(
            conv_total.astype(jnp.bfloat16), "fsdp", scatter_dimension=1, tiled=True
        ).astype(jnp.float32),
        lax.psum_scatter(
            cbias_total.astype(jnp.bfloat16), "fsdp", scatter_dimension=0, tiled=True
        ).astype(jnp.float32),
        lax.psum_scatter(
            sbias_total.astype(jnp.bfloat16), "fsdp", scatter_dimension=0, tiled=True
        ).astype(jnp.float32),
        lax.psum_scatter(
            decay_total.astype(jnp.bfloat16), "fsdp", scatter_dimension=0, tiled=True
        ).astype(jnp.float32),
        lax.psum_scatter(
            skip_total.astype(jnp.bfloat16), "fsdp", scatter_dimension=0, tiled=True
        ).astype(jnp.float32),
        lax.psum_scatter(
            gate_total.astype(jnp.bfloat16), "fsdp", scatter_dimension=0, tiled=True
        ).astype(jnp.float32),
        lax.psum_scatter(
            out_total.astype(jnp.bfloat16), "fsdp", scatter_dimension=0, tiled=True
        ).astype(jnp.float32),
    )
    return (
        lax.psum(norm_share.astype(jnp.bfloat16), "dp").astype(jnp.float32),
        lax.psum(proj_share.astype(jnp.bfloat16), "dp").astype(jnp.float32),
        lax.psum(step_share.astype(jnp.bfloat16), "dp").astype(jnp.float32),
        lax.psum(conv_share.astype(jnp.bfloat16), "dp").astype(jnp.float32),
        lax.psum(cbias_share.astype(jnp.bfloat16), "dp").astype(jnp.float32),
        lax.psum(sbias_share.astype(jnp.bfloat16), "dp").astype(jnp.float32),
        lax.psum(decay_share.astype(jnp.bfloat16), "dp").astype(jnp.float32),
        lax.psum(skip_share.astype(jnp.bfloat16), "dp").astype(jnp.float32),
        lax.psum(gate_share.astype(jnp.bfloat16), "dp").astype(jnp.float32),
        lax.psum(out_share.astype(jnp.bfloat16), "dp").astype(jnp.float32),
    )


def forward_block(tokens, params, segment_wide, starts):
    (
        norm_weight,
        proj_weight,
        step_weight,
        conv_weight,
        conv_bias,
        step_bias,
        decay_log,
        skip_gain,
        gate_weight,
        out_weight,
    ) = params
    normed, norm_pull = jax.vjp(rms_scale, tokens, norm_weight.astype(jnp.float32))
    normed_low = normed.astype(jnp.bfloat16)
    mixed = jnp.dot(normed_low, proj_weight, preferred_element_type=jnp.float32)
    step_raw = lax.dot_general(
        normed_low, step_weight, (((1,), (1,)), ((), ())), preferred_element_type=jnp.float32
    )
    gate_row = mixed[:, :INNER]
    conv_in = mixed[:, INNER:]
    halo_rows = conv_weight.shape[0] - 1
    before = from_behind(
        conv_in[conv_in.shape[0] - halo_rows :].astype(jnp.bfloat16), "fsdp", 1
    ).astype(jnp.float32)
    extended = jnp.concatenate([before, conv_in], axis=0)
    conv_out, conv_pull = jax.vjp(
        partial(convolve_block, segment_wide=segment_wide),
        extended,
        conv_weight.astype(jnp.float32),
        conv_bias.astype(jnp.float32),
    )
    xbc_low = lax.optimization_barrier(conv_out.astype(jnp.bfloat16))
    xbc_float = xbc_low.astype(jnp.float32)
    bias_row = step_bias.astype(jnp.float32)
    decay_row = decay_log.astype(jnp.float32)
    skip_row = skip_gain.astype(jnp.float32)
    decay_end, contrib = summarize(xbc_float, step_raw, bias_row, decay_row, starts)
    _, state_in = carried_in(
        (decay_end, contrib),
        "fsdp",
        combine_states,
        (jnp.ones_like(decay_end), jnp.zeros_like(contrib)),
    )
    ssd_out = respond(xbc_float, step_raw, bias_row, decay_row, skip_row, state_in, starts)
    gated, gate_pull = jax.vjp(gate_norm, ssd_out, gate_row, gate_weight.astype(jnp.float32))
    gated_low = gated.astype(jnp.bfloat16)
    branch = jnp.dot(gated_low, out_weight, preferred_element_type=jnp.float32)
    kept = (norm_pull, normed_low, conv_pull, xbc_low, step_raw, state_in, gate_pull, gated_low)
    return (tokens + branch, kept)


def backward_block(upstream, params, kept, starts):
    (
        norm_weight,
        proj_weight,
        step_weight,
        conv_weight,
        conv_bias,
        step_bias,
        decay_log,
        skip_gain,
        gate_weight,
        out_weight,
    ) = params
    norm_pull, normed_low, conv_pull, xbc_low, step_raw, state_in, gate_pull, gated_low = kept
    branch_low = upstream.astype(jnp.bfloat16)
    out_grad = lax.dot_general(
        gated_low, branch_low, (((0,), (0,)), ((), ())), preferred_element_type=jnp.float32
    )
    gated_grad = lax.dot_general(
        branch_low, out_weight, (((1,), (1,)), ((), ())), preferred_element_type=jnp.float32
    )
    ssd_grad, gate_grad, gate_gain_grad = gate_pull(gated_grad)
    xbc_float = xbc_low.astype(jnp.float32)
    bias_row = step_bias.astype(jnp.float32)
    decay_row = decay_log.astype(jnp.float32)
    skip_row = skip_gain.astype(jnp.float32)
    _, respond_pull = jax.vjp(
        partial(respond, starts=starts),
        xbc_float,
        step_raw,
        bias_row,
        decay_row,
        skip_row,
        state_in,
    )
    xbc_grad_first, raw_grad_first, bias_grad_first, decay_grad_first, skip_grad, state_grad = (
        respond_pull(ssd_grad)
    )
    (decay_end, contrib), summary_pull = jax.vjp(
        partial(summarize, starts=starts), xbc_float, step_raw, bias_row, decay_row
    )
    _, later_grad = carried_in_2(
        (decay_end, state_grad),
        "fsdp",
        combine_states,
        (jnp.ones_like(decay_end), jnp.zeros_like(state_grad)),
    )
    end_grad = jnp.sum(later_grad * state_in, axis=(1, 2))
    xbc_grad_second, raw_grad_second, bias_grad_second, decay_grad_second = summary_pull(
        (end_grad, later_grad)
    )
    extended_grad, conv_weight_grad, conv_bias_grad = conv_pull(xbc_grad_first + xbc_grad_second)
    halo_rows = conv_weight.shape[0] - 1
    returned = from_behind(as_sent(extended_grad[:halo_rows]), "fsdp", -1)
    conv_in_grad = extended_grad[halo_rows:]
    row_count = conv_in_grad.shape[0]
    conv_in_grad = jnp.concatenate(
        [conv_in_grad[: row_count - halo_rows], conv_in_grad[row_count - halo_rows :] + returned],
        axis=0,
    )
    mixed_grad = jnp.concatenate([gate_grad, conv_in_grad], axis=1).astype(jnp.bfloat16)
    raw_low = (raw_grad_first + raw_grad_second).astype(jnp.bfloat16)
    proj_grad = lax.dot_general(
        normed_low, mixed_grad, (((0,), (0,)), ((), ())), preferred_element_type=jnp.float32
    )
    step_grad = lax.dot_general(
        raw_low, normed_low, (((0,), (0,)), ((), ())), preferred_element_type=jnp.float32
    )
    normed_grad = lax.dot_general(
        mixed_grad, proj_weight, (((1,), (1,)), ((), ())), preferred_element_type=jnp.float32
    )
    normed_grad = normed_grad + jnp.dot(raw_low, step_weight, preferred_element_type=jnp.float32)
    token_grad, norm_grad = norm_pull(normed_grad)
    grads = (
        norm_grad,
        proj_grad,
        step_grad,
        conv_weight_grad,
        conv_bias_grad,
        bias_grad_first + bias_grad_second,
        decay_grad_first + decay_grad_second,
        skip_grad,
        gate_gain_grad,
        out_grad,
    )
    return (upstream + token_grad, grads)


def on_device(
    hidden_in,
    doc_lengths,
    norm_gain,
    input_proj,
    step_proj,
    conv_weight,
    conv_bias,
    step_bias,
    decay_log,
    skip_gain,
    gate_gain,
    output_proj,
    cotangent,
):
    shards = (
        norm_gain,
        input_proj,
        step_proj,
        conv_weight,
        conv_bias,
        step_bias,
        decay_log,
        skip_gain,
        gate_gain,
        output_proj,
    )
    batch_count = hidden_in.shape[0]
    block_rows = hidden_in.shape[1]
    layer_count = norm_gain.shape[0]
    kernel_width = conv_weight.shape[1]
    first_row = lax.axis_index("fsdp") * block_rows
    positions = (
        jnp.arange(block_rows + kernel_width - 1, dtype=jnp.int32) + first_row - (kernel_width - 1)
    )
    segment_list = []
    start_list = []
    for batch_index in range(batch_count):
        segment_wide = segment_ids(doc_lengths[batch_index], positions)
        segment_list.append(segment_wide)
        start_list.append(
            (
                segment_wide[kernel_width - 1 :]
                != segment_wide[kernel_width - 2 : block_rows + kernel_width - 2]
            ).astype(jnp.int32)
        )
    states = [hidden_in[batch_index].astype(jnp.float32) for batch_index in range(batch_count)]
    grads_in = [cotangent[batch_index].astype(jnp.float32) for batch_index in range(batch_count)]
    owned = [None] * layer_count
    layer_totals = [None] * layer_count
    for batch_index in range(batch_count):
        kept_list = []
        for layer_index in range(layer_count):
            params = fetch_weights(shards, layer_index)
            states[batch_index], kept = forward_block(
                states[batch_index], params, segment_list[batch_index], start_list[batch_index]
            )
            kept_list.append(kept)
        for layer_index in reversed(range(layer_count)):
            params = fetch_again(shards, layer_index)
            grads_in[batch_index], grads = backward_block(
                grads_in[batch_index], params, kept_list[layer_index], start_list[batch_index]
            )
            previous = layer_totals[layer_index]
            layer_totals[layer_index] = (
                grads if previous is None else jax.tree.map(jnp.add, previous, grads)
            )
    for layer_index in range(layer_count):
        owned[layer_index] = reduce_grads(layer_totals[layer_index])
    hidden_out = jnp.stack(states).astype(jnp.bfloat16)
    hidden_grad = jnp.stack(grads_in)
    stacked = tuple(
        (
            jnp.stack([owned[layer_index][member] for layer_index in range(layer_count)])
            for member in range(10)
        )
    )
    return (hidden_out, hidden_grad) + stacked


def solution(mesh):
    in_specs = (
        P("dp", "fsdp", None),
        P("dp", None),
        P(None, "fsdp"),
        P(None, "fsdp", None),
        P(None, None, "fsdp"),
        P(None, None, "fsdp"),
        P(None, "fsdp"),
        P(None, "fsdp"),
        P(None, "fsdp"),
        P(None, "fsdp"),
        P(None, "fsdp"),
        P(None, "fsdp", None),
        P("dp", "fsdp", None),
    )
    out_specs = (
        P("dp", "fsdp", None),
        P("dp", "fsdp", None),
        P(None, "fsdp"),
        P(None, "fsdp", None),
        P(None, None, "fsdp"),
        P(None, None, "fsdp"),
        P(None, "fsdp"),
        P(None, "fsdp"),
        P(None, "fsdp"),
        P(None, "fsdp"),
        P(None, "fsdp"),
        P(None, "fsdp", None),
    )
    return jax.shard_map(
        on_device, mesh=mesh, in_specs=in_specs, out_specs=out_specs, check_vma=False
    )
```

profile of v0, /device:TPU:0, one launch (start us, length us, event | category | flops | bytes accessed | tf_op | source)
XLA Modules:
  0.0 2230.4 jit_solution(4021461565696530210)
XLA Ops:
  20.8 32.2 %all-reduce.83 = (bf16[1536]{0:T(1024)(128)(2,1)S(1)}, bf16[3328]{0:T(1024)(128)(2,1)}, bf16[48]{0:T(256)(128)(2,1)S(1)}, bf16[48]{0:T(256)(128)(2,1)S(1)}, bf16...) all-reduce(bf16[1536]{0:T(1024)(128)(2,1)S(1)} %dynamic-update-slic, ...), channel_id=4, replica_groups=mesh['dp'=4,'fsdp'=8] {'fsdp'}, use_global_device_ids=true, to_apply=%add.61 | all-reduce | flops 10016 | bytes 40064
  53.7 34.0 %all-gather.1 = bf16[1,4,3328]{1,0,2:T(2,128)(2,1)S(1)} all-gather(bf16[1,4,416]{1,0,2:T(2,128)(2,1)S(1)} %copy.787), channel_id=3, replica_groups=mesh['dp'=4,'fsdp'=8] {'fsdp'}, dimensions={2}, use_global_device_ids=true | all-gather | bytes 29952 | tf_op jit(solution)/shard_map/all_gather | solution.py:175
  90.3 27.7 %all-gather.4 = bf16[1,48,1536]{1,0,2:T(2,128)(2,1)S(1)} all-gather(bf16[1,48,192]{1,0,2:T(2,128)(2,1)S(1)} %copy.788), channel_id=6, replica_groups=mesh['dp'=4,'fsdp'=8] {'fsdp'}, dimensions={2}, use_global_device_ids=true | all-gather | bytes 165888 | tf_op jit(solution)/shard_map/all_gather | solution.py:174
  122.4 69.0 %slice_reduce_fusion.7 = (f32[3328]{0:T(1024)S(1)}, f32[3328]{0:T(1024)S(1)}, f32[3328]{0:T(1024)S(1)}, f32[3328]{0:T(1024)S(1)}) fusion(f32[1,4,3328]{1,0,2:T(1,128)S(1)} %convert_element_type.772), kind=kLoop, calls=%fused_computation.185 | loop fusion | bytes 106496 | tf_op jit(solution)/shard_map/jvp()/slice | solution.py:100
  191.5 18.9 all-gather.49.cloned.1.call-done
  306.1 32.7 %all-gather.12 = bf16[1,4,3328]{1,0,2:T(2,128)(2,1)S(1)} all-gather(bf16[1,4,416]{1,0,2:T(2,128)(2,1)S(1)} %copy.789), channel_id=14, replica_groups=mesh['dp'=4,'fsdp'=8] {'fsdp'}, dimensions={2}, use_global_device_ids=true | all-gather | bytes 29952 | tf_op jit(solution)/shard_map/all_gather | solution.py:175
  342.8 21.0 all-gather.15
  367.3 73.0 %slice_reduce_fusion.3 = (f32[3328]{0:T(1024)S(1)}, f32[3328]{0:T(1024)}, f32[3328]{0:T(1024)}, f32[3328]{0:T(1024)}) fusion(f32[1,4,3328]{1,0,2:T(1,128)} %convert_element_type.779), kind=kLoop, calls=%fused_computation.179 | loop fusion | bytes 106496 | tf_op jit(solution)/shard_map/jvp()/slice | solution.py:100
  527.4 122.3 %all-gather.55.cloned.1.call-done = bf16[1,1536,6400]{2,1,0:T(8,128)(2,1)} async-done(((bf16[1,192,6400]{2,1,0:T(8,128)(2,1)}), bf16[1,1536,6400]{2,1,0:T(8,128)(2,1)}) %all-gather.55.cloned.1.call-update) | async-done | bytes 19660816 | tf_op jit(solution)/shard_map/all_gather | solution.py:173
  781.9 25.6 %all-gather.57.cloned.1.call-done = bf16[384,64,128]{2,1,0:T(8,128)(2,1)} async-done(((bf16[48,64,128]{2,1,0:T(8,128)(2,1)}), bf16[384,64,128]{2,1,0:T(8,128)(2,1)}) %all-gather.57.cloned.1.call-update) | async-done | bytes 6291472 | tf_op jit(solution)/shard_map/all_gather | solution.py:27
  843.5 55.0 %all-gather.59.cloned.1.call-done = bf16[1,3072,1536]{2,1,0:T(8,128)(2,1)} async-done(((bf16[1,384,1536]{2,1,0:T(8,128)(2,1)}), bf16[1,3072,1536]{2,1,0:T(8,128)(2,1)}) %all-gather.59.cloned.1.call-update) | async-done | bytes 9437200 | tf_op jit(solution)/shard_map/all_gather | solution.py:181
  970.2 19.6 all-gather.69.cloned.1.call-done
  989.8 30.2 %while.126 = (s32[]{:T(128)}, f32[48,64,128]{2,1,0:T(8,128)}, s32[]{:T(128)}, bf16[8,48]{1,0:T(8,128)(2,1)}, bf16[8,48,64,128]{3,2,1,0:T(8,128)(2,1)}, /*index=5*/s32[]{:T(128)}, s32[]{:T(128)}, s32[]{:T(128)}, s32[]{:T(128)}) while((s32[]{:T(128)}, f32[48,64,128]{2,1,0:T(8,128)}, s32[]{:T(128)}, bf16[8,48]{1,0:T(8,128)(2,1)}, ...), condition=%wide.region_56.58_spmd.clone, body=%wide.region_55.57_spmd.clone.sunk | while | flops 1966136 | bytes 3932815 | solution.py:68
  1026.5 28.2 %all-gather.65.cloned.1.call-done = bf16[384,64,128]{2,1,0:T(8,128)(2,1)} async-done(((bf16[48,64,128]{2,1,0:T(8,128)(2,1)}), bf16[384,64,128]{2,1,0:T(8,128)(2,1)}) %all-gather.65.cloned.1.call-update) | async-done | bytes 6291472 | tf_op jit(solution)/shard_map/all_gather | solution.py:50
  1269.1 22.4 %add_convert_fusion = bf16[1536,6400]{1,0:T(8,128)(2,1)} fusion(f32[1536,6400]{1,0:T(8,128)} %fusion.325, bf16[128,1536]{1,0:T(8,128)(2,1)S(1)} %copy-done.76, bf16[3,3328]{1,0:T(4,128)(2,1)S(1)} %copy-done.206, bf16[125,3328]{1,0:T(8,128)(2,1)S(1)} %copy-done.108, bf16[128,3072]{1,0:T(8,128)(2,1)S(1)} %copy-done.116), kind=kOutput, calls=%fused_computation.24 | convolution fusion | flops 2541158400 | bytes 61014016 | tf_op jit(solution)/shard_map/dot_general | solution.py:396
  1331.1 30.1 %while.127 = (s32[]{:T(128)}, f32[48,64,128]{2,1,0:T(8,128)}, s32[]{:T(128)}, bf16[8,48]{1,0:T(8,128)(2,1)}, bf16[8,48,64,128]{3,2,1,0:T(8,128)(2,1)}, /*index=5*/s32[]{:T(128)}, s32[]{:T(128)}, s32[]{:T(128)}, s32[]{:T(128)}) while((s32[]{:T(128)}, f32[48,64,128]{2,1,0:T(8,128)}, s32[]{:T(128)}, bf16[8,48]{1,0:T(8,128)(2,1)}, ...), condition=%wide.region_71.73_spmd.clone, body=%wide.region_70.72_spmd.clone.sunk | while | flops 1966136 | bytes 3932815 | solution.py:68
  1447.9 22.6 %add_convert_fusion.1 = bf16[1536,6400]{1,0:T(8,128)(2,1)} fusion(f32[1536,6400]{1,0:T(8,128)} %fusion.324, bf16[3,3328]{1,0:T(4,128)(2,1)} %fusion.354, bf16[125,3328]{1,0:T(8,128)(2,1)} %slice.651, bf16[128,3072]{1,0:T(8,128)(2,1)} %get-tuple-element.1348, f32[1536]{0:T(1024)S(1)} %copy-done.133, f32[128]{0:T(128)S(1)} %copy-done.303, ...), kind=kOutput, calls=%fused_computation.25 | convolution fusion | flops 2541944832 | bytes 61047296 | tf_op jit(solution)/shard_map/dot_general | solution.py:396
  1513.2 23.4 %reduce-scatter.21.cloned.1.call-done = bf16[384,1536]{1,0:T(8,128)(2,1)} async-done(((bf16[3072,1536]{1,0:T(8,128)(2,1)}), bf16[384,1536]{1,0:T(8,128)(2,1)}) %reduce-scatter.21.cloned.1.call-update) | async-done | bytes 1179664 | tf_op jit(solution)/shard_map/reduce_scatter | solution.py:264
  1536.5 196.0 %reduce-scatter.19.cloned.1.call-done = bf16[192,6400]{1,0:T(8,128)(2,1)} async-done(((bf16[1536,6400]{1,0:T(8,128)(2,1)}), bf16[192,6400]{1,0:T(8,128)(2,1)}) %reduce-scatter.19.cloned.1.call-update) | async-done | bytes 2457616 | tf_op jit(solution)/shard_map/reduce_scatter | solution.py:240
  1732.5 196.1 %reduce-scatter.17.cloned.1.call-done = bf16[192,6400]{1,0:T(8,128)(2,1)} async-done(((bf16[1536,6400]{1,0:T(8,128)(2,1)}), bf16[192,6400]{1,0:T(8,128)(2,1)}) %reduce-scatter.17.cloned.1.call-update) | async-done | bytes 2457616 | tf_op jit(solution)/shard_map/reduce_scatter | solution.py:240
  1941.4 19.4 reduce-scatter.31.cloned.1.call-done
  1961.8 30.1 %reduce-scatter.27.cloned.1.call-done = bf16[192,48]{1,0:T(8,128)(2,1)} async-done(((bf16[1536,48]{1,0:T(8,128)(2,1)}), bf16[192,48]{1,0:T(8,128)(2,1)}) %reduce-scatter.27.cloned.1.call-update) | async-done | bytes 18448
  2017.0 26.5 %all-reduce.82 = (bf16[1536]{0:T(1024)(128)(2,1)S(1)}, bf16[1536]{0:T(1024)(128)(2,1)S(1)}, bf16[3328]{0:T(1024)(128)(2,1)S(1)}, bf16[3328]{0:T(1024)(128)(2,1)S...) all-reduce(bf16[1536]{0:T(1024)(128)(2,1)S(1)} %get-tuple-element.1, ...), channel_id=31, replica_groups=mesh['dp'=4,'fsdp'=8] {'fsdp'}, use_global_device_ids=true, to_apply=%region_88.90.clone | all-reduce | flops 16160 | bytes 64640
  2079.4 134.3 %all-reduce.88.cloned.1.call-done = (bf16[1,192,6400]{2,1,0:T(8,128)(2,1)}, bf16[1,192,6400]{2,1,0:T(8,128)(2,1)}, bf16[1,384,1536]{2,1,0:T(8,128)(2,1)}, bf16[1,384,1536]{2,1,0:T(8,128)(2,1)}) async-done(((bf16[1,192,6400]{2,1,0:T(8,128)(2,1)}, bf16[1,192,6400]{2,1,0:T(8,128)(2,1)}, bf16[1,384,1536]{2,1,0:T(8,128)(2,1)}, bf16[1,384,1536]{2,1,0:T(8,128)(2,1)}), (bf16[1,192,6400]{2,1,0:T(8,128)(2,1)}, ...) | async-done | bytes 7274512 | tf_op jit(solution)/shard_map/psum | solution.py:270
  (1459 shorter events, 1076.6 us)
Async XLA Ops:
  7.2 203.2 %all-gather.49.cloned.1.call-start = ((), (), s32[]{:S(2)}) async-start(), calls=%async_computation.12 | async-start | bytes 22118400 | tf_op jit(solution)/shard_map/all_gather | solution.py:173
  12.3 439.7 %all-gather.61.cloned.1.call-start = ((), (), s32[]{:S(2)}) async-start(), calls=%async_computation.18 | async-start | bytes 7077888 | tf_op jit(solution)/shard_map/all_gather | solution.py:27
  235.4 247.4 %all-gather.51.cloned.1.call-start = ((), (), s32[]{:S(2)}) async-start(), calls=%async_computation.13 | async-start | bytes 7077888 | tf_op jit(solution)/shard_map/all_gather | solution.py:27
  266.0 249.9 %all-gather.53.cloned.1.call-start = ((), (), s32[]{:S(2)}) async-start(), calls=%async_computation.14 | async-start | bytes 10616832 | tf_op jit(solution)/shard_map/all_gather | solution.py:181
  269.3 380.3 %all-gather.55.cloned.1.call-start = ((), (), s32[]{:S(2)}) async-start(), calls=%async_computation.15 | async-start | bytes 22118400 | tf_op jit(solution)/shard_map/all_gather | solution.py:173
  269.9 487.7 %all-gather.63.cloned.1.call-start = ((), (), s32[]{:S(2)}) async-start(), calls=%async_computation.19 | async-start | bytes 7077888 | tf_op jit(solution)/shard_map/all_gather | solution.py:27
  658.7 11.1 collective-permute-start.3
  679.0 128.5 %all-gather.57.cloned.1.call-start = ((), (), s32[]{:S(2)}) async-start(), calls=%async_computation.16 | async-start | bytes 7077888 | tf_op jit(solution)/shard_map/all_gather | solution.py:27
  708.4 190.2 %all-gather.59.cloned.1.call-start = ((), (), s32[]{:S(2)}) async-start(), calls=%async_computation.17 | async-start | bytes 10616832 | tf_op jit(solution)/shard_map/all_gather | solution.py:181
  709.1 280.7 %all-gather.69.cloned.1.call-start = ((), (), s32[]{:S(2)}) async-start(), calls=%async_computation.22 | async-start | bytes 7077888 | tf_op jit(solution)/shard_map/all_gather | solution.py:50
  926.5 128.3 %all-gather.65.cloned.1.call-start = ((), (), s32[]{:S(2)}) async-start(), calls=%async_computation.20 | async-start | bytes 7077888 | tf_op jit(solution)/shard_map/all_gather | solution.py:50
  931.1 400.1 %all-gather.71.cloned.1.call-start = ((), (), s32[]{:S(2)}) async-start(), calls=%async_computation.23 | async-start | bytes 7077888 | tf_op jit(solution)/shard_map/all_gather | solution.py:50
  1116.9 34.8 %collective-permute-start.6 = (bf16[3,3328]{1,0:T(4,128)(2,1)}, bf16[3,3328]{1,0:T(4,128)(2,1)}, u32[]{:S(2)}, u32[]{:S(2)}) collective-permute-start(bf16[3,3328]{1,0:T(4,128)(2,1)} %slice.650), channel_id=1, source_target_pairs={{1,0},{2,1},{3,2},{4,3},{5,4},{6,5},{7,6},{9,8},{10,9},{11,10},{12... | collective-permute-start | bytes 59912 | tf_op jit(solution)/shard_map/ppermute | solution.py:21
  1142.1 22.2 collective-permute-start.4
  1204.0 170.2 %all-gather.67.cloned.1.call-start = ((), (), s32[]{:S(2)}) async-start(), calls=%async_computation.21 | async-start | bytes 7077888 | tf_op jit(solution)/shard_map/all_gather | solution.py:50
  1208.8 304.4 %reduce-scatter.23.cloned.1.call-start = ((), (), s32[]{:S(2)}) async-start(), calls=%async_computation.11 | async-start | bytes 10616832 | tf_op jit(solution)/shard_map/reduce_scatter | solution.py:264
  1229.8 306.7 %reduce-scatter.21.cloned.1.call-start = ((), (), s32[]{:S(2)}) async-start(), calls=%async_computation.10 | async-start | bytes 10616832 | tf_op jit(solution)/shard_map/reduce_scatter | solution.py:264
  1251.4 481.1 %reduce-scatter.19.cloned.1.call-start = ((), (), s32[]{:S(2)}) async-start(), calls=%async_computation.9 | async-start | bytes 22118400 | tf_op jit(solution)/shard_map/reduce_scatter | solution.py:240
  1291.5 637.1 %reduce-scatter.17.cloned.1.call-start = ((), (), s32[]{:S(2)}) async-start(), calls=%async_computation.8 | async-start | bytes 22118400 | tf_op jit(solution)/shard_map/reduce_scatter | solution.py:240
  1470.5 490.3 %reduce-scatter.31.cloned.1.call-start = ((), (), s32[]{:S(2)}) async-start(), calls=%async_computation.27 | async-start | bytes 958464
  1483.6 508.2 %reduce-scatter.27.cloned.1.call-start = ((), (), s32[]{:S(2)}) async-start(), calls=%async_computation.25 | async-start | bytes 442368
  1487.4 559.9 %reduce-scatter.29.cloned.1.call-start = ((), (), s32[]{:S(2)}) async-start(), calls=%async_computation.26 | async-start | bytes 958464
  1505.3 549.9 %reduce-scatter.25.cloned.1.call-start = ((), (), s32[]{:S(2)}) async-start(), calls=%async_computation.24 | async-start | bytes 442368
  1507.6 706.1 %all-reduce.88.cloned.1.call-start = ((), (), s32[]{:S(2)}) async-start(), calls=%async_computation.28 | async-start | bytes 14548992 | tf_op jit(solution)/shard_map/psum | solution.py:270
  (418 other events, 7822.5 us)
Sparse Core Ops, SparseCore 0:
  12.4 197.8 all-gather.48
  235.5 62.9 all-gather.60
  300.1 82.9 all-gather.50
  384.7 89.6 all-gather.52
  476.4 173.1 all-gather.54
  679.2 63.0 all-gather.62
  743.9 63.5 all-gather.56
  809.1 89.3 all-gather.58
  926.6 63.1 all-gather.68
  991.3 63.3 all-gather.64
  1204.1 66.1 all-gather.70
  1271.8 63.3 all-gather.66
  1338.2 98.4 reduce-scatter.22
  1438.8 97.6 reduce-scatter.20
  1538.7 193.7 reduce-scatter.18
  1734.8 193.7 reduce-scatter.16
  1930.7 30.0 reduce-scatter.30
  1963.0 28.8 reduce-scatter.26
  1994.1 29.6 reduce-scatter.28
  2026.1 29.0 reduce-scatter.24
  2059.1 154.5 all-reduce.87
where the time goes:
time: 2240 us; the launch traced here: 2230 us
  waiting for transfers between devices  880 us (39%)
  matrix products  435 us (19%)
  other arithmetic  320 us (14%)
  local copies, waits for them, and re-layouts  296 us (13%)
  blocking collectives  256 us (11%)
  between operations  26 us (1%)
    reduce_scatter x2, waiting for transfers between devices, reduce_grads(): lax.psum_scatter(proj_total.astype(jnp.bfloat16), 'fsdp', scatter_dimensi...  392 us
    slice x2, local copies, waits for them, and re-layouts, convolve_block(): weight[offset][None, :]  142 us
    all_gather x2, waiting for transfers between devices, fetch_weights(): lax.all_gather(proj_piece, 'fsdp', axis=0, tiled=True)  141 us
    psum x1, waiting for transfers between devices, reduce_grads(): lax.psum(proj_share.astype(jnp.bfloat16), 'dp').astype(jnp.float32)  134 us
    select_n x64, other arithmetic, hop(): return jax.tree.map(lambda a, b: jnp.where(reached, a, b), new, before)  123 us
    dot_general x12, matrix products, respond(): inner_part = jnp.einsum('hts,shp->thp', mixing, scaled, precision=HIGHEST)  82.8 us
    dot_general x4, matrix products, backward_block(): lax.dot_general(normed_low, mixed_grad, (((0,), (0,)), ((), ())), preferr...  77.6 us
    all_gather x2, blocking collectives, fetch_weights(): lax.all_gather(conv_piece, 'fsdp', axis=1, tiled=True)  66.6 us
  transfers between devices with their start and end apart: 29, of which 14 were waited for; matrix products, arithmetic and copies ran while one was open for 38% of the time, Pallas kernels for 0%

commit v1 on v0

v1 whole, which is shorter than its diff:
```python
from functools import partial

import jax
import jax.numpy as jnp
from jax import lax
from jax.experimental import pallas as pl
from jax.experimental.pallas import tpu as pltpu
from jax.sharding import Mesh
from jax.sharding import PartitionSpec as P

BF = jnp.bfloat16
F32 = jnp.float32
HIGHEST = lax.Precision.HIGHEST
EPSILON = 1e-05
HEAD_DIM = 64
STATE = 128
LANES = 128
CHUNK = 128
HALO = 8
FAR = -1e30
PLANE = ("z", "core")


def mm(a, b):
    return lax.dot_general(a, b, (((1,), (0,)), ((), ())), preferred_element_type=F32)


def mm_bt(a, b):
    return lax.dot_general(a, b, (((1,), (1,)), ((), ())), preferred_element_type=F32)


def mm_at(a, b):
    return lax.dot_general(a, b, (((0,), (0,)), ((), ())), preferred_element_type=F32)


def mm_exact(a, b):
    return lax.dot_general(
        a, b, (((1,), (0,)), ((), ())), precision=HIGHEST, preferred_element_type=F32
    )


def iota2(shape, dim):
    return lax.broadcasted_iota(jnp.int32, shape, dim)


def head_spread(width):
    return (iota2((LANES, width), 1) // HEAD_DIM == iota2((LANES, width), 0)).astype(F32)


def head_gather(width):
    return (iota2((width, LANES), 0) // HEAD_DIM == iota2((width, LANES), 1)).astype(BF)


def softplus(x):
    return jnp.maximum(x, 0.0) + jnp.log1p(jnp.exp(-jnp.abs(x)))


def chunk_terms(step, age, bias_row, decay_row):
    raw = step + bias_row
    dt = softplus(raw)
    rate = -dt * decay_row
    rows = iota2((CHUNK, CHUNK), 0)
    cols = iota2((CHUNK, CHUNK), 1)
    lower = (cols <= rows).astype(F32)
    total = mm_exact(lower, rate)
    pos = iota2((CHUNK, 1), 0)
    first = pos - age
    bias = jnp.where((cols <= rows) & (cols >= first), 0.0, FAR)
    first_last = first[CHUNK - 1 :, :]
    enter = jnp.exp(total) * (first < 0).astype(F32)
    last = total[CHUNK - 1 :, :]
    leave = jnp.exp(last - total) * (pos >= first_last).astype(F32)
    through = jnp.exp(last) * (first_last < 0).astype(F32)
    return raw, dt, rate, total, bias, enter, leave, through


def to_order(refs, buf, shift, count):
    for k in range(count):
        buf[jnp.bitwise_xor(shift, k)] = refs[k][0]


def conv_sum(ext, age, weights, bias_row, rows):
    out = jnp.zeros((rows, ext.shape[1]), F32) + bias_row
    for j in range(4):
        part = ext[pl.ds(HALO - j, rows), :]
        if j:
            part = jnp.where(age >= j, part, 0.0)
        out = out + weights[3 - j : 4 - j, :] * part
    return out


def forward_kernel(shift_ref, *refs, count, cd, with_grad):
    mixed_refs, refs = refs[:count], refs[count:]
    if with_grad:
        grad_refs, refs = refs[:count], refs[count:]
    age_ref, pc_ref, ph_ref, refs = refs[0], refs[1], refs[2], refs[3:]
    gated_ref, pre_ref, ssd_ref, states_ref, refs = refs[0], refs[1], refs[2], refs[3], refs[4:]
    if with_grad:
        sums_ref, refs = refs[0], refs[1:]
    mixed_buf, gated_buf, ext, state, refs = refs[0], refs[1], refs[2], refs[3], refs[4:]
    if with_grad:
        grad_buf = refs[0]
    step_at = pl.program_id(0)
    shift = shift_ref[0]
    conv_ch = cd + 2 * STATE
    rows = mixed_buf.shape[0] * mixed_buf.shape[1]
    width = mixed_buf.shape[2]

    @pl.when(step_at == 0)
    def _():
        ext[0:HALO, :] = jnp.zeros((HALO, conv_ch), F32)
        state[...] = jnp.zeros_like(state)

    @pl.when(step_at > 0)
    def _():
        ext[0:HALO, :] = ext[rows : rows + HALO, :]

    to_order(mixed_refs, mixed_buf, shift, count)
    mixed = mixed_buf[...].reshape(rows, width)
    ext[HALO : HALO + rows, :] = mixed[:, cd : cd + conv_ch]
    age = age_ref[0][:rows, :]
    pre = conv_sum(ext, age, pc_ref[0:4, :], pc_ref[4:5, :], rows)
    pre_ref[0] = pre
    xbc = (pre * jax.nn.sigmoid(pre)).astype(BF)
    skip_row = pc_ref[5:6, :cd]
    gain_row = pc_ref[6:7, :cd]
    bias_row = ph_ref[0:1, :]
    decay_row = ph_ref[1:2, :]
    spread = head_spread(cd)
    low_half = iota2((CHUNK, LANES), 1) < HEAD_DIM
    outs = []
    for c in range(rows // CHUNK):
        at = slice(c * CHUNK, (c + 1) * CHUNK)
        raw, dt, rate, total, bias, enter, leave, through = chunk_terms(
            mixed[at, cd + conv_ch :], age[at], bias_row, decay_row
        )
        values = xbc[at, :cd]
        writers = xbc[at, cd : cd + STATE]
        readers = xbc[at, cd + STATE :]
        total_t = total.T
        dt_t = dt.T
        wide = mm_exact(
            jnp.concatenate([enter, leave * dt, jnp.broadcast_to(through, (8, LANES))], axis=0),
            spread,
        )
        scores = mm_bt(readers, writers)
        held = state[...]
        states_ref[0, c] = held.astype(BF)
        carried = mm(readers, held.astype(BF)) * wide[:CHUNK]
        values_f = values.astype(F32)
        pairs = []
        for pr in range(cd // LANES):
            mixing = []
            for h in (2 * pr, 2 * pr + 1):
                gap = total[:, h : h + 1] - total_t[h : h + 1, :] + bias
                mixing.append((jnp.exp(gap) * scores * dt_t[h : h + 1, :]).astype(BF))
            pair = values[:, pr * LANES : (pr + 1) * LANES]
            zero = jnp.zeros_like(pair)
            stacked = jnp.concatenate(
                [jnp.where(low_half, pair, zero), jnp.where(low_half, zero, pair)], axis=0
            )
            pairs.append(mm(jnp.concatenate(mixing, axis=1), stacked))
        ssd = jnp.concatenate(pairs, axis=1) + carried + skip_row * values_f
        state[...] = held * wide[2 * CHUNK : 2 * CHUNK + 1] + mm_at(
            writers, (wide[CHUNK : 2 * CHUNK] * values_f).astype(BF)
        )
        outs.append(ssd)
    ssd = jnp.concatenate(outs, axis=0)
    ssd_ref[0] = ssd
    gate = mixed[:, :cd]
    v = ssd * (gate * jax.nn.sigmoid(gate))
    squares = v * v
    partial_sums = squares[:, :LANES]
    for b in range(1, cd // LANES):
        partial_sums = partial_sums + squares[:, b * LANES : (b + 1) * LANES]
    weighted = v * gain_row
    gated_buf[:, :, :cd] = weighted.astype(BF).reshape(gated_buf.shape[0], gated_buf.shape[1], cd)
    if with_grad:
        to_order(grad_refs, grad_buf, shift, count)
        crossed = grad_buf[...].reshape(rows, cd) * weighted
        s1 = jnp.sum(partial_sums, axis=1, keepdims=True)
        s2 = jnp.sum(crossed, axis=1, keepdims=True)
        lane = iota2((rows, LANES), 1)
        sums_ref[0] = jnp.where(lane == 0, s1, jnp.where(lane == 1, s2, 0.0))
    else:
        gated_buf[:, :, cd:] = partial_sums.astype(BF).reshape(
            gated_buf.shape[0], gated_buf.shape[1], LANES
        )
    for k in range(count):
        gated_ref[k, 0] = gated_buf[jnp.bitwise_xor(shift, k)]


def backward_kernel(shift_ref, *refs, count, cd, own_scales):
    mixed_refs, grad_refs, refs = refs[:count], refs[count : 2 * count], refs[2 * count :]
    if own_scales:
        scale_ref, refs = refs[0], refs[1:]
    age_ref, pc_ref, ph_ref, pre_ref, ssd_ref, states_ref = refs[:6]
    out_ref, wide_sums, head_sums, mixed_buf, grad_buf, out_buf, ext, adjoint = refs[6:]
    step_at = pl.program_id(0)
    shift = shift_ref[0]
    conv_ch = cd + 2 * STATE
    q = mixed_buf.shape[1]
    rows = count * q
    width = mixed_buf.shape[2]

    @pl.when(step_at == 0)
    def _():
        ext[rows : rows + HALO, :] = jnp.zeros((HALO, conv_ch), F32)
        adjoint[...] = jnp.zeros_like(adjoint)
        wide_sums[...] = jnp.zeros_like(wide_sums)
        head_sums[...] = jnp.zeros_like(head_sums)

    @pl.when(step_at > 0)
    def _():
        ext[rows : rows + HALO, :] = ext[0:HALO, :]

    to_order(mixed_refs, mixed_buf, shift, count)
    to_order(grad_refs, grad_buf, shift, count)
    mixed = mixed_buf[...].reshape(rows, width)
    grad = grad_buf[...].reshape(rows, grad_buf.shape[2])
    age_ext = age_ref[0]
    age = age_ext[:rows, :]
    skip_row = pc_ref[5:6, :cd]
    gain_row = pc_ref[6:7, :cd]
    bias_row = ph_ref[0:1, :]
    decay_row = ph_ref[1:2, :]

    gate = mixed[:, :cd]
    ssd = ssd_ref[0]
    sg = jax.nn.sigmoid(gate)
    sl = gate * sg
    v = ssd * sl
    if own_scales:
        scaled = grad[:, :cd] * scale_ref[0][:, 0:1]
        mean_term = scale_ref[0][:, 1:2]
    else:
        scaled = grad[:, :cd]
        mean_term = grad[:, cd : cd + 1] + grad[:, cd + 1 : cd + 2]
    v_grad = scaled * gain_row - mean_term * v
    wide_sums[6:7, :cd] += jnp.sum(scaled * v, axis=0, keepdims=True)
    d_ssd = v_grad * sl
    d_gate = v_grad * ssd * (sg * (1.0 + gate * (1.0 - sg)))
    out_buf[:, :, :cd] = d_gate.astype(BF).reshape(count, q, cd)

    pre = pre_ref[0]
    sp = jax.nn.sigmoid(pre)
    xbc = (pre * sp).astype(BF)
    d_silu = sp * (1.0 + pre * (1.0 - sp))
    spread = head_spread(cd)
    gather = head_gather(cd)
    low_half = iota2((CHUNK, LANES), 1) < HEAD_DIM
    tri_rows = iota2((CHUNK, CHUNK), 0)
    tri_cols = iota2((CHUNK, CHUNK), 1)
    from_here = (tri_cols >= tri_rows).astype(F32)
    before = (tri_cols < tri_rows).astype(F32)
    heads = cd // HEAD_DIM
    pick = (iota2((heads * CHUNK, LANES), 0) // CHUNK == iota2((heads * CHUNK, LANES), 1)).astype(
        BF
    )

    def per_head(x):
        high = x.astype(BF)
        return mm(high, gather) + mm((x - high.astype(F32)).astype(BF), gather)

    for c in reversed(range(rows // CHUNK)):
        at = slice(c * CHUNK, (c + 1) * CHUNK)
        raw, dt, rate, total, bias, enter, leave, through = chunk_terms(
            mixed[at, cd + conv_ch :], age[at], bias_row, decay_row
        )
        values = xbc[at, :cd]
        writers = xbc[at, cd : cd + STATE]
        readers = xbc[at, cd + STATE :]
        values_f = values.astype(F32)
        dy = d_ssd[at]
        wide_sums[5:6, :cd] += jnp.sum(values_f * dy, axis=0, keepdims=True)
        total_t = total.T
        dt_t = dt.T
        wide = mm_exact(
            jnp.concatenate([enter, leave, dt, jnp.broadcast_to(through, (8, LANES))], axis=0),
            spread,
        )
        enter_w = wide[:CHUNK]
        leave_w = wide[CHUNK : 2 * CHUNK]
        dt_w = wide[2 * CHUNK : 3 * CHUNK]
        through_w = wide[3 * CHUNK : 3 * CHUNK + 1]
        held = states_ref[0, c]
        adj = adjoint[...]
        adj_b = adj.astype(BF)
        scores = mm_bt(readers, writers)
        entered = enter_w * dy
        entered_b = entered.astype(BF)
        row_enter = per_head(entered * mm(readers, held))
        d_readers = mm_bt(entered_b, held)
        from_state = leave_w * mm(writers, adj_b)
        exits = per_head(values_f * from_state * dt_w)
        d_writers = mm_bt((leave_w * dt_w * values_f).astype(BF), adj_b)
        through_sum = jnp.sum(adj * held.astype(F32), axis=0, keepdims=True) * through_w
        passing = per_head(jnp.broadcast_to(through_sum, (8, cd)))[0:1]
        adjoint[...] = adj * through_w + mm_at(readers, entered_b)
        d_scores = jnp.zeros((CHUNK, CHUNK), F32)
        pulls = []
        kernels = []
        for pr in range(cd // LANES):
            dy_pair = dy[:, pr * LANES : (pr + 1) * LANES].astype(BF)
            zero = jnp.zeros_like(dy_pair)
            stacked = jnp.concatenate(
                [jnp.where(low_half, dy_pair, zero), jnp.where(low_half, zero, dy_pair)], axis=0
            )
            d_mix = mm_bt(stacked, values[:, pr * LANES : (pr + 1) * LANES])
            mixing = []
            for i, h in enumerate((2 * pr, 2 * pr + 1)):
                gap = total[:, h : h + 1] - total_t[h : h + 1, :] + bias
                decays = jnp.exp(gap)
                mixing.append((decays * scores).astype(BF))
                pull = d_mix[i * CHUNK : (i + 1) * CHUNK] * dt_t[h : h + 1, :] * decays
                d_scores = d_scores + pull
                kernels.append((pull * scores).astype(BF))
            pulls.append(mm_at(jnp.concatenate(mixing, axis=0), stacked))
        d_scaled = jnp.concatenate(pulls, axis=1) + from_state
        row_sums = mm(jnp.concatenate(kernels, axis=1), pick)
        col_sums = mm_at(jnp.concatenate(kernels, axis=0), pick)
        d_rate = (
            mm_exact(from_here, row_sums - col_sums + row_enter)
            + mm_exact(before, exits)
            + passing
        )
        d_dt = per_head(values_f * d_scaled)
        d_raw = (d_dt - d_rate * decay_row) * jax.nn.sigmoid(raw)
        head_sums[0:1, :] += jnp.sum(d_raw, axis=0, keepdims=True)
        head_sums[1:2, :] += jnp.sum(d_rate * rate, axis=0, keepdims=True)
        d_scores_b = d_scores.astype(BF)
        d_readers = d_readers + mm(d_scores_b, writers)
        d_writers = d_writers + mm_at(d_scores_b, readers)
        d_values = dt_w * d_scaled + skip_row * dy
        ext[at, :] = jnp.concatenate([d_values, d_writers, d_readers], axis=1) * d_silu[at]
        per = CHUNK // q
        out_buf[c * per : (c + 1) * per, :, cd + conv_ch :] = d_raw.astype(BF).reshape(per, q, LANES)
    conv_in = mixed[:, cd : cd + conv_ch]
    d_conv = jnp.zeros((rows, conv_ch), F32)
    for j in range(4):
        part = ext[pl.ds(j, rows), :]
        if j:
            part = jnp.where(age_ext[j : j + rows, :] >= j, part, 0.0)
        else:
            wide_sums[4:5, :] += jnp.sum(part, axis=0, keepdims=True)
        d_conv = d_conv + pc_ref[3 - j : 4 - j, :] * part
        wide_sums[3 - j : 4 - j, :] += jnp.sum(part * conv_in, axis=0, keepdims=True)
    out_buf[:, :, cd : cd + conv_ch] = d_conv.astype(BF).reshape(count, q, conv_ch)
    for k in range(count):
        out_ref[k, 0] = out_buf[jnp.bitwise_xor(shift, k)]


def whole(shape):
    return pl.BlockSpec(shape, lambda *_: (0,) * len(shape))


def mixer_forward(shift, mixed, grads, age, pc, ph):
    count = len(mixed)
    blocks, q, width = mixed[0].shape
    conv_ch = pc.shape[1]
    cd = conv_ch - 2 * STATE
    rows = count * q
    with_grad = grads is not None
    out_width = cd if with_grad else cd + LANES
    shard = pl.BlockSpec((1, q, width), lambda i, s: (i, 0, 0))
    in_specs = [shard] * count
    args = list(mixed)
    if with_grad:
        in_specs += [pl.BlockSpec((1, q, cd), lambda i, s: (i, 0, 0))] * count
        args += list(grads)
    in_specs += [
        pl.BlockSpec((1, rows + HALO, 1), lambda i, s: (i, 0, 0)),
        whole(pc.shape),
        whole(ph.shape),
    ]
    args += [age, pc, ph]
    chunks = rows // CHUNK
    out_shape = [
        jax.ShapeDtypeStruct((count, blocks, q, out_width), BF),
        jax.ShapeDtypeStruct((blocks, rows, conv_ch), F32),
        jax.ShapeDtypeStruct((blocks, rows, cd), F32),
        jax.ShapeDtypeStruct((blocks, chunks, STATE, cd), BF),
    ]
    out_specs = [
        pl.BlockSpec((count, 1, q, out_width), lambda i, s: (0, i, 0, 0)),
        pl.BlockSpec((1, rows, conv_ch), lambda i, s: (i, 0, 0)),
        pl.BlockSpec((1, rows, cd), lambda i, s: (i, 0, 0)),
        pl.BlockSpec((1, chunks, STATE, cd), lambda i, s: (i, 0, 0, 0)),
    ]
    scratch = [
        pltpu.VMEM((count, q, width), F32),
        pltpu.VMEM((count, q, out_width), BF),
        pltpu.VMEM((rows + HALO, conv_ch), F32),
        pltpu.VMEM((STATE, cd), F32),
    ]
    if with_grad:
        out_shape.append(jax.ShapeDtypeStruct((blocks, rows, LANES), F32))
        out_specs.append(pl.BlockSpec((1, rows, LANES), lambda i, s: (i, 0, 0)))
        scratch.append(pltpu.VMEM((count, q, cd), F32))
    return pl.pallas_call(
        partial(forward_kernel, count=count, cd=cd, with_grad=with_grad),
        out_shape=out_shape,
        grid_spec=pltpu.PrefetchScalarGridSpec(
            num_scalar_prefetch=1,
            grid=(blocks,),
            in_specs=in_specs,
            out_specs=out_specs,
            scratch_shapes=scratch,
        ),
        compiler_params=pltpu.CompilerParams(vmem_limit_bytes=48 * 2**20),
        cost_estimate=pl.CostEstimate(
            flops=10**10, bytes_accessed=3 * 10**7, transcendentals=10**6
        ),
    )(shift, *args)


def mixer_backward(shift, mixed, grads, scales, age, pc, ph, pre, ssd, states):
    count = len(mixed)
    blocks, q, width = mixed[0].shape
    conv_ch = pc.shape[1]
    cd = conv_ch - 2 * STATE
    rows = count * q
    chunks = rows // CHUNK
    top = blocks - 1
    grad_width = grads[0].shape[2]
    in_specs = [pl.BlockSpec((1, q, width), lambda i, s: (top - i, 0, 0))] * count
    in_specs += [pl.BlockSpec((1, q, grad_width), lambda i, s: (top - i, 0, 0))] * count
    args = list(mixed) + list(grads)
    if scales is not None:
        in_specs.append(pl.BlockSpec((1, rows, 2), lambda i, s: (top - i, 0, 0)))
        args.append(scales)
    in_specs += [
        pl.BlockSpec((1, rows + HALO, 1), lambda i, s: (top - i, 0, 0)),
        whole(pc.shape),
        whole(ph.shape),
        pl.BlockSpec((1, rows, conv_ch), lambda i, s: (top - i, 0, 0)),
        pl.BlockSpec((1, rows, cd), lambda i, s: (top - i, 0, 0)),
        pl.BlockSpec((1, chunks, STATE, cd), lambda i, s: (top - i, 0, 0, 0)),
    ]
    args += [age, pc, ph, pre, ssd, states]
    return pl.pallas_call(
        partial(backward_kernel, count=count, cd=cd, own_scales=scales is not None),
        out_shape=[
            jax.ShapeDtypeStruct((count, blocks, q, width), BF),
            jax.ShapeDtypeStruct((8, conv_ch), F32),
            jax.ShapeDtypeStruct((8, LANES), F32),
        ],
        grid_spec=pltpu.PrefetchScalarGridSpec(
            num_scalar_prefetch=1,
            grid=(blocks,),
            in_specs=in_specs,
            out_specs=[
                pl.BlockSpec((count, 1, q, width), lambda i, s: (0, top - i, 0, 0)),
                whole((8, conv_ch)),
                whole((8, LANES)),
            ],
            scratch_shapes=[
                pltpu.VMEM((count, q, width), F32),
                pltpu.VMEM((count, q, grad_width), F32),
                pltpu.VMEM((count, q, width), BF),
                pltpu.VMEM((rows + HALO, conv_ch), F32),
                pltpu.VMEM((STATE, cd), F32),
            ],
        ),
        compiler_params=pltpu.CompilerParams(vmem_limit_bytes=48 * 2**20),
        cost_estimate=pl.CostEstimate(
            flops=2 * 10**10, bytes_accessed=5 * 10**7, transcendentals=2 * 10**6
        ),
    )(shift, *args)


def swap(value, axis, k, size):
    return lax.ppermute(value, axis, [(i, i ^ k) for i in range(size)])


def pick(value, index):
    return lax.dynamic_index_in_dim(value, index, 0, keepdims=False)


def exchange(parts, axis, size):
    mine = lax.axis_index(axis)
    return [pick(parts, mine)] + [
        swap(pick(parts, mine ^ k), axis, k, size) for k in range(1, size)
    ]


def in_order(relative, mine):
    stacked = jnp.stack(relative)
    return jnp.stack([pick(stacked, mine ^ j) for j in range(len(relative))])


def gather_rows(shard, n):
    if n != 4:
        everything = lax.all_gather(shard, "dp")
        mine = lax.axis_index("dp")
        return [pick(everything, mine ^ k) for k in range(n)]
    half = shard.shape[0] // 2
    first = swap(shard, "dp", 1, n)
    second = swap(shard, "dp", 2, n)
    low = swap(first[:half], "dp", 2, n)
    high = swap(second[half:], "dp", 1, n)
    return [shard, first, second, jnp.concatenate([low, high], axis=0)]


def reduce_rows(parts, n):
    if n != 4:
        mine = lax.axis_index("dp")
        ordered = jnp.stack([pick(parts, mine ^ j) for j in range(n)])
        return lax.psum_scatter(ordered, "dp", scatter_dimension=0, tiled=False).astype(F32)
    half = parts.shape[1] // 2
    a, b = parts[:, :half], parts[:, half:]
    got_a = swap(jnp.stack([a[1], a[3]]), "dp", 1, n)
    got_b = swap(jnp.stack([b[2], b[3]]), "dp", 2, n)
    on_a = (a[2].astype(F32) + got_a[1].astype(F32)).astype(BF)
    on_b = (b[1].astype(F32) + got_b[1].astype(F32)).astype(BF)
    last_a = swap(on_a, "dp", 2, n)
    last_b = swap(on_b, "dp", 1, n)
    sum_a = a[0].astype(F32) + got_a[0].astype(F32) + last_a.astype(F32)
    sum_b = b[0].astype(F32) + got_b[0].astype(F32) + last_b.astype(F32)
    return jnp.concatenate([sum_a, sum_b], axis=0)


def tokens_in(block, n, z_count):
    core = lax.axis_index("core")
    keep = pick(block, core)
    other = lax.ppermute(pick(block, 1 - core), "core", [(0, 1), (1, 0)])
    first = jnp.where(core == 0, keep, other)
    second = jnp.where(core == 0, other, keep)
    both = jnp.concatenate([first, second], axis=0)
    q = both.shape[0] // n
    by_group = exchange(both.reshape(n, q, -1), "dp", n)
    ordered = in_order(by_group, lax.axis_index("dp"))
    by_chunk = exchange(ordered, "z", z_count)
    return in_order(by_chunk, lax.axis_index("z"))


def tokens_out(own, n, z_count):
    core = lax.axis_index("core")
    q = own.shape[1]
    by_group = in_order(exchange(own, "z", z_count), lax.axis_index("z"))
    by_part = in_order(exchange(by_group, "dp", n), lax.axis_index("dp"))
    both = by_part.reshape(2, n * q // 2, -1)
    keep = pick(both, core)
    other = lax.ppermute(pick(both, 1 - core), "core", [(0, 1), (1, 0)])
    return jnp.stack([jnp.where(core == 0, keep, other), jnp.where(core == 0, other, keep)])


def on_device(
    hidden_in,
    doc_lengths,
    norm_gain,
    input_proj,
    step_proj,
    conv_weight,
    conv_bias,
    step_bias,
    decay_log,
    skip_gain,
    gate_gain,
    output_proj,
    cotangent,
    *,
    n,
    z_count,
):
    layers = norm_gain.shape[0]
    owners = 2 * z_count
    d_rows = norm_gain.shape[1]
    width_d = d_rows * owners
    heads_f = step_bias.shape[1]
    heads = heads_f * owners
    hd = heads // n
    cd = hd * HEAD_DIM
    inner = heads * HEAD_DIM
    conv_f = conv_bias.shape[1]
    conv_ch = cd + 2 * STATE
    gate_f = gate_gain.shape[1]
    out_rows = output_proj.shape[1]
    width_in = cd + conv_ch + LANES
    step_at = cd + conv_ch
    d = lax.axis_index("dp")
    z = lax.axis_index("z")
    core = lax.axis_index("core")
    shift = (d if n else d).astype(jnp.int32).reshape(1)

    small_len = 5 * conv_f + gate_f + 3 * heads_f
    small_cols = -(-small_len // d_rows)

    def small_pack(cw, cb, gg, sb, dl, sk):
        flat = jnp.concatenate([cw.reshape(-1), cb, gg, sb, dl, sk])
        return jnp.pad(flat, (0, small_cols * d_rows - small_len)).reshape(d_rows, small_cols)

    def small_split(flat):
        sizes = (4 * conv_f, conv_f, gate_f, heads_f, heads_f, heads_f)
        parts, at = [], 0
        for size in sizes:
            parts.append(flat[..., at : at + size])
            at += size
        return parts

    def weights_in(layer):
        block = input_proj[layer]
        pieces = jnp.concatenate(
            [
                lax.dynamic_slice_in_dim(block, d * cd, cd, 1),
                lax.dynamic_slice_in_dim(block, inner + d * cd, cd, 1),
                block[:, 2 * inner :],
                lax.dynamic_slice_in_dim(step_proj[layer], d * hd, hd, 0).T,
            ],
            axis=1,
        )
        pieces = (pieces.astype(F32) * norm_gain[layer].astype(F32)[:, None]).astype(BF)
        small = small_pack(
            conv_weight[layer],
            conv_bias[layer],
            gate_gain[layer],
            step_bias[layer],
            decay_log[layer],
            skip_gain[layer],
        )
        rest = LANES - hd - small_cols
        shard = jnp.concatenate([pieces, small, jnp.zeros((d_rows, rest), BF)], axis=1)
        full = lax.all_gather(shard, PLANE, tiled=True)
        small_all = full[:, step_at + hd : step_at + hd + small_cols].astype(F32)
        cw, cb, gg, sb, dl, sk = small_split(small_all.reshape(owners, small_cols * d_rows))
        conv = jnp.concatenate([cw, cb], axis=1).reshape(owners, 5, conv_f)
        conv = conv.transpose(1, 0, 2).reshape(5, owners * conv_f)
        conv = jnp.concatenate(
            [lax.dynamic_slice_in_dim(conv, d * cd, cd, 1), conv[:, inner:]], axis=1
        )
        gain = lax.dynamic_slice_in_dim(gg.reshape(-1), d * cd, cd, 0)
        sk = lax.dynamic_slice_in_dim(sk.reshape(-1), d * hd, hd, 0)
        sb = lax.dynamic_slice_in_dim(sb.reshape(-1), d * hd, hd, 0)
        dl = lax.dynamic_slice_in_dim(dl.reshape(-1), d * hd, hd, 0)
        skip = jnp.broadcast_to(sk[:, None], (hd, HEAD_DIM)).reshape(-1)
        wide = jnp.pad(jnp.stack([skip, gain]), ((0, 1), (0, 2 * STATE)))
        pc = jnp.concatenate([conv, wide], axis=0)
        ph = jnp.pad(jnp.stack([sb, jnp.exp(dl)]), ((0, 6), (0, LANES - hd)))
        keep = (iota2((1, width_in), 1) < step_at + hd).astype(BF)
        return full * keep, pc, ph

    out_cols = width_d // n

    def weights_out(layer):
        mine = lax.dynamic_slice_in_dim(output_proj[layer], d * out_cols, out_cols, 1)
        column = lax.all_gather(mine, PLANE, tiled=True)
        parts = exchange(column.reshape(n, cd, out_cols), "dp", n)
        full = jnp.zeros((cd, width_d), BF)
        for k in range(n):
            full = lax.dynamic_update_slice(full, parts[k], (0, (d ^ k) * out_cols))
        return full

    both = lax.ppermute(
        doc_lengths,
        ("dp", "z"),
        [(i * z_count + j, j * z_count + i) for i in range(n) for j in range(z_count)],
    )
    ends = jnp.cumsum(pick(both, core))
    tok = hidden_in.shape[1]
    block_rows = 2 * tok
    row_len = block_rows * z_count
    q = block_rows // n
    positions = jnp.arange(row_len, dtype=jnp.int32)
    begin = jnp.max(jnp.where(ends[None, :] <= positions[:, None], ends[None, :], 0), axis=1)
    age = (positions - begin).reshape(z_count, block_rows)
    after = jnp.concatenate([age[1:, :HALO], jnp.zeros((1, HALO), jnp.int32)], axis=0)
    age = jnp.concatenate([age, after], axis=1)[:, :, None]

    w_in = [None] * layers
    w_out = [None] * layers
    pcs = [None] * layers
    phs = [None] * layers
    for layer in range(layers):
        w_in[layer], pcs[layer], phs[layer] = weights_in(layer)
        w_out[layer] = weights_out(layer)

    def extended(weight):
        eye = jnp.eye(LANES, dtype=BF)
        return jnp.concatenate(
            [
                jnp.pad(weight, ((0, 0), (0, LANES))),
                jnp.pad(eye, ((0, 0), (width_d, 0))),
            ],
            axis=0,
        )

    def normalize(resid):
        inv = lax.rsqrt(jnp.mean(resid * resid, axis=-1, keepdims=True) + EPSILON)
        return inv, resid * inv

    def flat(x):
        return x.reshape(-1, x.shape[-1])

    resid = tokens_in(hidden_in, n, z_count).astype(F32)
    upstream = tokens_in(cotangent, n, z_count)
    upstream_all = gather_rows(upstream, n)

    kept = [None] * layers
    last = layers - 1
    for layer in range(layers):
        inv, u = normalize(resid)
        unit_all = gather_rows(u.astype(BF), n)
        mixed = [
            mm(flat(part), w_in[layer]).reshape(z_count, q, width_in) for part in unit_all
        ]
        if layer < last:
            weight = extended(w_out[layer])
            gated, pre, ssd, states = mixer_forward(
                shift, mixed, None, age, pcs[layer], phs[layer]
            )
            sent = mm(flat(gated), weight).astype(BF).reshape(n, z_count, q, width_d + LANES)
            got = reduce_rows(sent, n)
            squares = jnp.sum(got[..., width_d:], axis=-1, keepdims=True)
            ginv = lax.rsqrt(squares / inner + EPSILON)
            branch = got[..., :width_d] * ginv
            kept[layer] = (resid, inv, unit_all, mixed, gated, pre, ssd, states, weight, ginv, branch)
            resid = resid + branch
        else:
            weight = w_out[layer]
            gg = [mm_bt(flat(part), weight).reshape(z_count, q, cd) for part in upstream_all]
            gated, pre, ssd, states, sums = mixer_forward(
                shift, mixed, gg, age, pcs[layer], phs[layer]
            )
            totals = sums[:, :, :2].transpose(2, 0, 1).reshape(2, row_len // LANES, LANES)
            bit = 1
            while bit < n:
                totals = totals + swap(totals, "dp", bit, n)
                bit *= 2
            totals = totals.reshape(2, z_count, block_rows)
            ginv = lax.rsqrt(totals[0] / inner + EPSILON)
            scales = jnp.stack([ginv, ginv * ginv * ginv * totals[1] / inner], axis=-1)
            sent = mm(flat(gated), weight).astype(BF).reshape(n, z_count, q, width_d)
            own = lax.dynamic_index_in_dim(
                ginv.reshape(z_count, n, q), d, 1, keepdims=False
            )[..., None]
            hidden_out = (resid + reduce_rows(sent, n) * own).astype(BF)
            kept[layer] = (resid, inv, unit_all, mixed, gated, pre, ssd, states, weight, ginv, gg)
    hidden_out = tokens_out(hidden_out, n, z_count)

    back = upstream.astype(F32)
    results = [None] * layers
    for layer in reversed(range(layers)):
        resid, inv, unit_all, mixed, gated, pre, ssd, states, weight, ginv, extra = kept[layer]
        if layer == last:
            g_all = upstream_all
            gg = extra
            scale = ginv.reshape(z_count, n, q)
            scale = in_order([lax.dynamic_index_in_dim(scale, d ^ k, 1, False) for k in range(n)], 0)
            gated = (gated.astype(F32) * scale[..., None]).astype(BF)
            use = scales
        else:
            low = back.astype(BF).astype(F32)
            m = jnp.sum(low * extra, axis=-1, keepdims=True) / inner
            kappa = ginv * ginv * m
            high = kappa.astype(BF)
            rest = (kappa - high.astype(F32)).astype(BF)
            payload = jnp.concatenate(
                [(low * ginv).astype(BF), high, rest, jnp.zeros((z_count, q, LANES - 2), BF)],
                axis=-1,
            )
            g_all = gather_rows(payload, n)
            gg = [mm_bt(flat(part), weight).reshape(z_count, q, cd + LANES) for part in g_all]
            use = None
        d_mixed, wide_sums, head_sums = mixer_backward(
            shift, mixed, gg, use, age, pcs[layer], phs[layer], pre, ssd, states
        )
        sent = mm_bt(flat(d_mixed), w_in[layer]).astype(BF).reshape(n, z_count, q, width_d)
        normed_grad = reduce_rows(sent, n)
        u = resid * inv
        back = back + inv * (
            normed_grad - u * jnp.mean(normed_grad * u, axis=-1, keepdims=True)
        )
        g_cat = flat(jnp.stack(g_all))
        d_out = mm_at(flat(gated), g_cat)[:cd, :width_d].astype(BF)
        by_column = jnp.stack([d_out[:, j * out_cols : (j + 1) * out_cols] for j in range(n)])
        rows_all = in_order(exchange(by_column, "dp", n), d).reshape(n * cd, out_cols)
        own_out = lax.psum_scatter(rows_all, PLANE, scatter_dimension=0, tiled=True)
        out_grad = lax.all_gather(own_out, "dp", axis=1, tiled=True).astype(F32)

        d_in = mm_at(flat(jnp.stack(unit_all)), flat(d_mixed)).astype(BF)
        conv_full = jnp.concatenate([jnp.zeros((5, inner), F32), wide_sums[:5, cd:]], axis=1)
        conv_full = lax.dynamic_update_slice(conv_full, wide_sums[:5, :cd], (0, d * cd))
        conv_full = conv_full.reshape(5, owners, conv_f).transpose(1, 0, 2).reshape(owners, -1)
        gain_full = lax.dynamic_update_slice(jnp.zeros((inner,), F32), wide_sums[6, :cd], (d * cd,))
        skip_sum = jnp.sum(wide_sums[5, :cd].reshape(hd, HEAD_DIM), axis=1)
        head_full = lax.dynamic_update_slice(
            jnp.zeros((3, heads), F32),
            jnp.stack([head_sums[0, :hd], head_sums[1, :hd], skip_sum]),
            (0, d * hd),
        )
        head_full = head_full.reshape(3, owners, heads_f).transpose(1, 0, 2).reshape(owners, -1)
        small = jnp.concatenate([conv_full, gain_full.reshape(owners, gate_f), head_full], axis=1)
        small = jnp.pad(small, ((0, 0), (0, small_cols * d_rows - small_len)))
        small = small.reshape(owners * d_rows, small_cols).astype(BF)
        d_in = lax.dynamic_update_slice(d_in, small, (0, step_at + hd))
        own_in = lax.psum_scatter(d_in, PLANE, scatter_dimension=0, tiled=True)
        all_in = lax.all_gather(own_in, "dp").astype(F32)
        small = jnp.sum(all_in[:, :, step_at + hd : step_at + hd + small_cols], axis=0)
        small = small_split(small.reshape(-1)[:small_len])
        unit_grad = jnp.concatenate(
            [all_in[j, :, :cd] for j in range(n)]
            + [all_in[j, :, cd : 2 * cd] for j in range(n)]
            + [jnp.sum(all_in[:, :, 2 * cd : step_at], axis=0)],
            axis=1,
        )
        step_unit = jnp.concatenate(
            [all_in[j, :, step_at : step_at + hd] for j in range(n)], axis=1
        )
        gain = norm_gain[layer].astype(F32)
        norm_grad = jnp.sum(unit_grad * input_proj[layer].astype(F32), axis=1) + jnp.sum(
            step_unit.T * step_proj[layer].astype(F32), axis=0
        )
        results[layer] = (
            norm_grad,
            unit_grad * gain[:, None],
            step_unit.T * gain[None, :],
            small[0].reshape(4, conv_f),
            small[1],
            small[3],
            small[4],
            small[5],
            small[2],
            out_grad,
        )
    hidden_grad = tokens_out(back.astype(BF), n, z_count).astype(F32)
    stacked = tuple(
        jnp.stack([results[layer][member] for layer in range(layers)]) for member in range(10)
    )
    return (hidden_out, hidden_grad) + stacked


def solution(mesh):
    n = mesh.shape["dp"]
    z_count = mesh.shape["fsdp"] // 2
    assert n == z_count
    split = Mesh(mesh.devices.reshape(n, z_count, 2), ("dp", "z", "core"))
    fsdp = PLANE
    tokens = P("dp", fsdp, None)
    last = P(None, fsdp)
    weights = (
        last,
        P(None, fsdp, None),
        P(None, None, fsdp),
        P(None, None, fsdp),
        last,
        last,
        last,
        last,
        last,
        P(None, fsdp, None),
    )
    return jax.shard_map(
        partial(on_device, n=n, z_count=z_count),
        mesh=split,
        in_specs=(tokens, P("dp", None)) + weights + (tokens,),
        out_specs=(tokens, tokens) + weights,
        check_vma=False,
    )
```

time: 2240 us -> 929 us (0.41)
  waiting for transfers between devices: 880 us -> 374 us
  matrix products: 435 us -> 116 us
  blocking collectives: 256 us -> 0 us
  other arithmetic: 320 us -> 70.4 us
  local copies, waits for them, and re-layouts: 296 us -> 141 us
  Pallas kernels: 0 us -> 103 us
  starting transfers between devices: 16.4 us -> 99.7 us
    reduce_scatter x4, waiting for transfers between devices: 415 us -> 64.9 us  [the longest x2 64.9 us: on_device(): own_in = lax.psum_scatter(d_in, PLANE, scatter_dimension=0, tiled=True)]
    dot_general x84 -> x24, matrix products: 435 us -> 116 us  [the longest x10 43.3 us: mm(): lax.dot_general(a, b, (((1,), (0,)), ((), ())), preferred_element_type=F32)]
    ppermute x8 -> x75, waiting for transfers between devices: 2.19 us -> 236 us  [the longest x70 235 us: swap(): return lax.ppermute(value, axis, [(i, i ^ k) for i in range(size)])]
    all_gather x12 -> x8, waiting for transfers between devices: 270 us -> 72.5 us  [the longest x2 54.2 us: on_device(): all_in = lax.all_gather(own_in, 'dp').astype(F32)]
    all_gather x10 -> x0, blocking collectives: 179 us -> none  [the longest x2 66.6 us: fetch_weights(): lax.all_gather(conv_piece, 'fsdp', axis=1, tiled=True)]
    slice x36 -> x44, local copies, waits for them, and re-layouts: 174 us -> 19.8 us  [the longest x1 5.35 us: weights_in(): block = input_proj[layer]]
    psum x1 -> x0, waiting for transfers between devices: 134 us -> none  [reduce_grads(): lax.psum(proj_share.astype(jnp.bfloat16), 'dp').astype(jnp.float32)]
    select_n x68 -> x2, other arithmetic: 127 us -> 1.11 us  [tokens_in(): first = jnp.where(core == 0, keep, other)]
  transfers between devices with their start and end apart: 29 -> 87, of which waited for: 14 -> 48; matrix products, arithmetic and copies ran while one was open for 38% -> 27% of each run, Pallas kernels for 0% -> 10%
where the time goes in v1:
time: 929 us; the launch traced here: 921 us
  waiting for transfers between devices  374 us (40%)
  local copies, waits for them, and re-layouts  141 us (15%)
  matrix products  116 us (12%)
  Pallas kernels  103 us (11%)
  starting transfers between devices  99.7 us (11%)
  other arithmetic  70.4 us (8%)
  between operations  17 us (2%)
    ppermute x70, waiting for transfers between devices, swap(): return lax.ppermute(value, axis, [(i, i ^ k) for i in range(size)])  235 us
    ppermute x70, starting transfers between devices, swap(): return lax.ppermute(value, axis, [(i, i ^ k) for i in range(size)])  96.5 us
    unnamed x238, local copies, waits for them, and re-layouts  73.1 us
    pallas_call x2, Pallas kernels, mixer_backward(): pl.pallas_call(partial(backward_kernel, count=count, cd=cd, own_scales=sc...  72.3 us
    reduce_scatter x2, waiting for transfers between devices, on_device(): own_in = lax.psum_scatter(d_in, PLANE, scatter_dimension=0, tiled=True)  64.9 us
    all_gather x2, waiting for transfers between devices, on_device(): all_in = lax.all_gather(own_in, 'dp').astype(F32)  54.2 us
    dot_general x10, matrix products, mm(): lax.dot_general(a, b, (((1,), (0,)), ((), ())), preferred_element_type=F32)  43.3 us
    dot_general x10, matrix products, mm_bt(): lax.dot_general(a, b, (((1,), (1,)), ((), ())), preferred_element_type=F32)  39.2 us
  transfers between devices with their start and end apart: 87, of which 48 were waited for; matrix products, arithmetic and copies ran while one was open for 27% of the time, Pallas kernels for 10%

profile of v1, /device:TPU:0, one launch (start us, length us, event | category | flops | bytes accessed | tf_op | source)
XLA Modules:
  0.0 920.7 jit_solution(7151704963363068859)
XLA Ops:
  50.5 7.2 collective-permute-start.27
  57.7 19.2 %collective-permute-done.5 = bf16[64,1536]{1,0:T(8,128)(2,1)S(1)} collective-permute-done((bf16[64,1536]{1,0:T(8,128)(2,1)S(1)}, bf16[64,1536]{1,0:T(8,128)(2,1)S(1)}, u32[]{:S(2)}, u32[]{:S(2)}) %collective-permute-start.5) | collective-permute-done | bytes 196640 | tf_op jit(solution)/shard_map/ppermute | solution.py:473
  79.3 16.3 %collective-permute-done.28 = bf16[64,1536]{1,0:T(8,128)(2,1)S(1)} collective-permute-done((bf16[64,1536]{1,0:T(8,128)(2,1)S(1)}, bf16[64,1536]{1,0:T(8,128)(2,1)S(1)}, u32[]{:S(2)}, u32[]{:S(2)}) %collective-permute-start.28) | collective-permute-done | bytes 196640 | tf_op jit(solution)/shard_map/ppermute | solution.py:473
  107.7 8.6 collective-permute-done.33
  159.0 9.9 %collective-permute-done.30 = bf16[768,384]{1,0:T(8,128)(2,1)S(1)} collective-permute-done((bf16[768,384]{1,0:T(8,128)(2,1)S(1)}, bf16[768,384]{1,0:T(8,128)(2,1)S(1)}, u32[]{:S(2)}, u32[]{:S(2)}) %collective-permute-start.30) | collective-permute-done | bytes 589856 | tf_op jit(solution)/shard_map/ppermute | solution.py:473
  169.1 21.8 %collective-permute-done.31 = bf16[768,384]{1,0:T(8,128)(2,1)S(1)} collective-permute-done((bf16[768,384]{1,0:T(8,128)(2,1)S(1)}, bf16[768,384]{1,0:T(8,128)(2,1)S(1)}, u32[]{:S(2)}, u32[]{:S(2)}) %collective-permute-start.31) | collective-permute-done | bytes 589856 | tf_op jit(solution)/shard_map/ppermute | solution.py:473
  225.0 15.4 %shard_map.220 = (bf16[4,4,64,896]{3,2,1,0:T(8,128)(2,1)S(1)}, f32[4,256,1024]{2,1,0:T(8,128)}, f32[4,256,768]{2,1,0:T(8,128)}, bf16[4,2,128,768]{3,2,1,0:T(8,128)(2,1)S(1)}) custom-call(s32[1]{0:T(128)} %bitcast.15.shift_ref, f32[4,64,1920]{2,1,0:T(8,128)S(1)} %fusion.15.refs_0_, f32[4,64,1920]{2,1,0:T(8,128)} %fusion.13.refs_1_, ...), custom_call_target="tpu_custom_call" | custom-call | flops 10000000000 | bytes 30000000 | tf_op jit(solution)/shard_map/pallas_call | solution.py:400
  257.4 9.3 %collective-permute-done.15 = bf16[2,2,64,1664]{3,2,1,0:T(8,128)(2,1)} collective-permute-done((bf16[2,2,64,1664]{3,2,1,0:T(8,128)(2,1)}, bf16[2,2,64,1664]{3,2,1,0:T(8,128)(2,1)}, u32[]{:S(2)}, u32[]{:S(2)}) %collective-permute-start.15) | collective-permute-done | bytes 852000 | tf_op jit(solution)/shard_map/ppermute | solution.py:473
  286.6 9.5 %collective-permute-done.19 = bf16[4,64,1536]{2,1,0:T(8,128)(2,1)S(1)} collective-permute-done((bf16[4,64,1536]{2,1,0:T(8,128)(2,1)S(1)}, bf16[4,64,1536]{2,1,0:T(8,128)(2,1)S(1)}, u32[]{:S(2)}, u32[]{:S(2)}) %collective-permute-start.19) | collective-permute-done | bytes 786464 | tf_op jit(solution)/shard_map/ppermute | solution.py:473
  312.0 15.3 %shard_map.221 = (bf16[4,4,64,768]{3,2,1,0:T(8,128)(2,1)S(1)}, f32[4,256,1024]{2,1,0:T(8,128)}, f32[4,256,768]{2,1,0:T(8,128)}, bf16[4,2,128,768]{3,2,1,0:T(8,128)(2,1)}, f32[4,256,128]{2,1,0:T(8,128)S(1)}) custom-call(s32[1]{0:T(128)} %bitcast.15.shift_ref, f32[4,64,1920]{2,1,0:T(8,128)} %fusion.7.refs_0_, f32[4,64,1920]{2,1,0:T(8,128)} %fusion.5.refs_1_, ...), custom_call_target="tpu_custom_call" | custom-call | flops 10000000000 | bytes 30000000 | tf_op jit(solution)/shard_map/pallas_call | solution.py:400
  346.3 36.3 %shard_map.222 = (bf16[4,4,64,1920]{3,2,1,0:T(8,128)(2,1)}, f32[8,1024]{1,0:T(8,128)S(1)}, f32[8,128]{1,0:T(8,128)S(1)}) custom-call(s32[1]{0:T(128)} %bitcast.15.shift_ref, f32[4,64,1920]{2,1,0:T(8,128)} %fusion.7.refs_0_, f32[4,64,1920]{2,1,0:T(8,128)} %fusion.5.refs_1_, f32[4,64,1920]{2,1,0:T(8,128)} %fusion.3.refs_2_, f32[4,64,1920]{2,1,0:T(8,128)} %fusion.1.refs_3_, ...), custom_call_target="tpu_custom_call" | custom-call | flops 20000000000 | bytes 50000000 | tf_op jit(solution)/shard_map/pallas_call | solution.py:441
  382.6 10.2 %convolution_convert_fusion.1 = bf16[1024,1536]{1,0:T(8,128)(2,1)S(1)} fusion(bf16[1024,1920]{1,0:T(8,128)(2,1)} %bitcast.578, bf16[1536,1920]{1,0:T(8,128)(2,1)} %all-gather.15.cloned.1.call-done, bf16[1920]{0:T(1024)(128)(2,1)S(1)} %fusion.115), kind=kOutput, calls=%fused_computation.26 | convolution fusion | flops 6044319744 | bytes 12979968 | tf_op jit(solution)/shard_map/dot_general | solution.py:29
  418.2 10.8 %collective-permute-done.52 = bf16[2,2,64,1536]{3,2,1,0:T(8,128)(2,1)S(1)} collective-permute-done((bf16[2,2,64,1536]{3,2,1,0:T(8,128)(2,1)}, bf16[2,2,64,1536]{3,2,1,0:T(8,128)(2,1)S(1)}, u32[]{:S(2)}, u32[]{:S(2)}) %collective-permute-start.52) | collective-permute-done | bytes 786464 | tf_op jit(solution)/shard_map/ppermute | solution.py:473
  431.7 14.7 %collective-permute-done.38 = bf16[2,64,1536]{2,1,0:T(8,128)(2,1)S(1)} collective-permute-done((bf16[2,64,1536]{2,1,0:T(8,128)(2,1)S(1)}, bf16[2,64,1536]{2,1,0:T(8,128)(2,1)S(1)}, u32[]{:S(2)}, u32[]{:S(2)}) %collective-permute-start.38) | collective-permute-done | bytes 393248 | tf_op jit(solution)/shard_map/ppermute | solution.py:473
  470.2 10.4 %collective-permute-done.54 = bf16[4,64,1664]{2,1,0:T(8,128)(2,1)} collective-permute-done((bf16[4,64,1664]{2,1,0:T(8,128)(2,1)}, bf16[4,64,1664]{2,1,0:T(8,128)(2,1)}, u32[]{:S(2)}, u32[]{:S(2)}) %collective-permute-start.54) | collective-permute-done | bytes 852000 | tf_op jit(solution)/shard_map/ppermute | solution.py:473
  504.3 7.7 collective-permute-done.71
  523.7 11.3 %bitcast_convert_fusion = bf16[1536,1920]{1,0:T(8,128)(2,1)} fusion(bf16[4,4,64,1920]{3,2,1,0:T(8,128)(2,1)} %get-tuple-element.33, bf16[1,4,64,1536]{3,2,1,0:T(8,128)(2,1)} %bitcast.544, bf16[1,4,64,1536]{3,2,1,0:T(8,128)(2,1)} %bitcast.542, bf16[1,4,64,1536]{3,2,1,0:T(8,128)(2,1)} %bitcast.541, bf16[1,4,64,1536]{3,2,1,0:T(8,128)(2,1)} %fusion.169), kind=kOutput, calls=%fused_computation | convolution fusion | flops 6047465472 | bytes 12976128 | tf_op jit(solution)/shard_map/dot_general | solution.py:33
  554.3 36.0 %shard_map.223 = (bf16[4,4,64,1920]{3,2,1,0:T(8,128)(2,1)}, f32[8,1024]{1,0:T(8,128)S(1)}, f32[8,128]{1,0:T(8,128)S(1)}) custom-call(s32[1]{0:T(128)} %bitcast.15.shift_ref, f32[4,64,1920]{2,1,0:T(8,128)} %copy-done.7, f32[4,64,1920]{2,1,0:T(8,128)} %fusion.13.refs_1_, f32[4,64,1920]{2,1,0:T(8,128)} %fusion.11.refs_2_, f32[4,64,1920]{2,1,0:T(8,128)} %fusion.9.refs_3_, ...), custom_call_target="tpu_custom_call" | custom-call | flops 20000000000 | bytes 50000000 | tf_op jit(solution)/shard_map/pallas_call | solution.py:441
  590.6 11.4 %bitcast_convert_fusion.1 = bf16[1536,1920]{1,0:T(8,128)(2,1)} fusion(bf16[4,4,64,1920]{3,2,1,0:T(8,128)(2,1)} %get-tuple-element.37, bf16[1,4,64,1536]{3,2,1,0:T(8,128)(2,1)} %bitcast.140, bf16[1,4,64,1536]{3,2,1,0:T(8,128)(2,1)} %bitcast.139, bf16[1,4,64,1536]{3,2,1,0:T(8,128)(2,1)} %bitcast.138, bf16[1,4,64,1536]{3,2,1,0:T(8,128)(2,1)} %multiply_convert_fusion.2), kind=kOutput, calls=%fused_computation.1 | convolution fusion | flops 6047465472 | bytes 12976128 | tf_op jit(solution)/shard_map/dot_general | solution.py:33
  614.2 10.0 %convolution_convert_fusion = bf16[1024,1536]{1,0:T(8,128)(2,1)S(1)} fusion(bf16[1024,1920]{1,0:T(8,128)(2,1)} %bitcast.579, bf16[1536,1920]{1,0:T(8,128)(2,1)} %all-gather.13.cloned.1.call-done, bf16[1920]{0:T(1024)(128)(2,1)S(1)} %fusion.115), kind=kOutput, calls=%fused_computation.25 | convolution fusion | flops 6044319744 | bytes 12979968 | tf_op jit(solution)/shard_map/dot_general | solution.py:29
  682.6 18.3 %all-gather.17.cloned.1.call-done = bf16[384,1536]{1,0:T(8,128)(2,1)} async-done(((bf16[384,384]{1,0:T(8,128)(2,1)}), bf16[384,1536]{1,0:T(8,128)(2,1)}) %all-gather.17.cloned.1.call-update) | async-done | bytes 1179664 | tf_op jit(solution)/shard_map/all_gather | solution.py:778
  704.9 64.9 %reduce-scatter.5.cloned.1.call-done = bf16[192,1920]{1,0:T(8,128)(2,1)} async-done(((bf16[1536,1920]{1,0:T(8,128)(2,1)}), bf16[192,1920]{1,0:T(8,128)(2,1)}) %reduce-scatter.5.cloned.1.call-update) | async-done | bytes 737296 | tf_op jit(solution)/shard_map/reduce_scatter | solution.py:796
  769.8 42.6 %all-gather.27.cloned.1.call-done = bf16[768,1920]{1,0:T(8,128)(2,1)} async-done(((bf16[192,1920]{1,0:T(8,128)(2,1)}), bf16[768,1920]{1,0:T(8,128)(2,1)}) %all-gather.27.cloned.1.call-update) | async-done | bytes 2949136 | tf_op jit(solution)/shard_map/all_gather | solution.py:797
  844.8 11.7 %all-gather.25.cloned.1.call-done = bf16[768,1920]{1,0:T(8,128)(2,1)} async-done(((bf16[192,1920]{1,0:T(8,128)(2,1)}), bf16[768,1920]{1,0:T(8,128)(2,1)}) %all-gather.25.cloned.1.call-update) | async-done | bytes 2949136 | tf_op jit(solution)/shard_map/all_gather | solution.py:797
  (746 shorter events, 475.0 us)
Async XLA Ops:
  7.2 129.9 %all-gather.21.cloned.1.call-start = ((), (), s32[]{:S(2)}) async-start(), calls=%async_computation.12 | async-start | bytes 2654208 | tf_op jit(solution)/shard_map/all_gather | solution.py:646
  9.8 132.0 %all-gather.23.cloned.1.call-start = ((), (), s32[]{:S(2)}) async-start(), calls=%async_computation.13 | async-start | bytes 2654208 | tf_op jit(solution)/shard_map/all_gather | solution.py:646
  10.7 189.8 %all-gather.13.cloned.1.call-start = ((), (), s32[]{:S(2)}) async-start(), calls=%async_computation.4 | async-start | bytes 6635520 | tf_op jit(solution)/shard_map/all_gather | solution.py:623
  20.2 232.6 %all-gather.15.cloned.1.call-start = ((), (), s32[]{:S(2)}) async-start(), calls=%async_computation.5 | async-start | bytes 6635520 | tf_op jit(solution)/shard_map/all_gather | solution.py:623
  42.8 34.0 %collective-permute-start.5 = (bf16[64,1536]{1,0:T(8,128)(2,1)S(1)}, bf16[64,1536]{1,0:T(8,128)(2,1)S(1)}, u32[]{:S(2)}, u32[]{:S(2)}) collective-permute-start(bf16[64,1536]{1,0:T(8,128)(2,1)S(1)} %get-tuple-element.195), channel_id=1, source_target_pairs={{0,4},{2,6},{4,0},{6,2},{1,5},{3,7},{5,1},{7,3},{8,12},{10,14},{12... | collective-permute-start | bytes 589832 | tf_op jit(solution)/shard_map/ppermute | solution.py:473
  50.5 45.1 %collective-permute-start.28 = (bf16[64,1536]{1,0:T(8,128)(2,1)S(1)}, bf16[64,1536]{1,0:T(8,128)(2,1)S(1)}, u32[]{:S(2)}, u32[]{:S(2)}) collective-permute-start(bf16[64,1536]{1,0:T(8,128)(2,1)S(1)} %get-tuple-element.179), channel_id=1, source_target_pairs={{0,4},{2,6},{4,0},{6,2},{1,5},{3,7},{5,1},{7,3},{8,12},{10,14},{12... | collective-permute-start | bytes 589832 | tf_op jit(solution)/shard_map/ppermute | solution.py:473
  50.5 45.1 %collective-permute-start.27 = (bf16[64,1536]{1,0:T(8,128)(2,1)S(1)}, bf16[64,1536]{1,0:T(8,128)(2,1)S(1)}, u32[]{:S(2)}, u32[]{:S(2)}) collective-permute-start(bf16[64,1536]{1,0:T(8,128)(2,1)S(1)} %get-tuple-element.180), channel_id=1, source_target_pairs={{0,2},{2,0},{4,6},{6,4},{1,3},{3,1},{5,7},{7,5},{8,10},{10,8},{12,... | collective-permute-start | bytes 589832 | tf_op jit(solution)/shard_map/ppermute | solution.py:473
  79.2 41.4 %collective-permute-start.8 = (bf16[4,64,1536]{2,1,0:T(8,128)(2,1)S(1)}, bf16[4,64,1536]{2,1,0:T(8,128)(2,1)}, u32[]{:S(2)}, u32[]{:S(2)}) collective-permute-start(bf16[4,64,1536]{2,1,0:T(8,128)(2,1)S(1)} %fusion.84), channel_id=1, source_target_pairs={{0,16},{8,24},{16,0},{24,8},{1,17},{9,25},{17,1},{25,9},{2,18},{10... | collective-permute-start | bytes 2359304 | tf_op jit(solution)/shard_map/ppermute | solution.py:473
  102.0 449.6 %reduce-scatter.11.cloned.1.call-start = ((), (), s32[]{:S(2)}) async-start(), calls=%async_computation.10 | async-start | bytes 2654208 | tf_op jit(solution)/shard_map/reduce_scatter | solution.py:777
  146.4 44.6 %collective-permute-start.14 = (bf16[768,384]{1,0:T(8,128)(2,1)S(1)}, bf16[768,384]{1,0:T(8,128)(2,1)S(1)}, u32[]{:S(2)}, u32[]{:S(2)}) collective-permute-start(bf16[768,384]{1,0:T(8,128)(2,1)S(1)} %copy-done.61), channel_id=1, source_target_pairs={{0,24},{8,16},{16,8},{24,0},{1,25},{9,17},{17,9},{25,1},{2,26},{10... | collective-permute-start | bytes 1769480 | tf_op jit(solution)/shard_map/ppermute | solution.py:473
  146.6 44.4 %collective-permute-start.31 = (bf16[768,384]{1,0:T(8,128)(2,1)S(1)}, bf16[768,384]{1,0:T(8,128)(2,1)S(1)}, u32[]{:S(2)}, u32[]{:S(2)}) collective-permute-start(bf16[768,384]{1,0:T(8,128)(2,1)S(1)} %get-tuple-element.123), channel_id=1, source_target_pairs={{0,16},{8,24},{16,0},{24,8},{1,17},{9,25},{17,1},{25,9},{2,18},{10... | collective-permute-start | bytes 1769480 | tf_op jit(solution)/shard_map/ppermute | solution.py:473
  156.4 36.5 %collective-permute-start.32 = (bf16[768,384]{1,0:T(8,128)(2,1)S(1)}, bf16[768,384]{1,0:T(8,128)(2,1)S(1)}, u32[]{:S(2)}, u32[]{:S(2)}) collective-permute-start(bf16[768,384]{1,0:T(8,128)(2,1)S(1)} %get-tuple-element.122), channel_id=1, source_target_pairs={{0,24},{8,16},{16,8},{24,0},{1,25},{9,17},{17,9},{25,1},{2,26},{10... | collective-permute-start | bytes 1769480 | tf_op jit(solution)/shard_map/ppermute | solution.py:473
  337.7 69.8 %collective-permute-start.37 = (bf16[2,2,64,1536]{3,2,1,0:T(8,128)(2,1)}, bf16[2,2,64,1536]{3,2,1,0:T(8,128)(2,1)}, u32[]{:S(2)}, u32[]{:S(2)}) collective-permute-start(bf16[2,2,64,1536]{3,2,1,0:T(8,128)(2,1)} %pad_maximum_fusion.20), channel_id=1, source_target_pairs={{0,8},{8,0},{16,24},{24,16},{1,9},{9,1},{17,25},{25,17},{2,10},{10... | collective-permute-start | bytes 2359304 | tf_op jit(solution)/shard_map/ppermute | solution.py:473
  339.1 69.5 %collective-permute-start.39 = (bf16[2,2,64,1536]{3,2,1,0:T(8,128)(2,1)}, bf16[2,2,64,1536]{3,2,1,0:T(8,128)(2,1)}, u32[]{:S(2)}, u32[]{:S(2)}) collective-permute-start(bf16[2,2,64,1536]{3,2,1,0:T(8,128)(2,1)} %stack.635), channel_id=1, source_target_pairs={{0,16},{8,24},{16,0},{24,8},{1,17},{9,25},{17,1},{25,9},{2,18},{10... | collective-permute-start | bytes 2359304 | tf_op jit(solution)/shard_map/ppermute | solution.py:473
  405.7 58.7 %collective-permute-start.74 = (bf16[768,384]{1,0:T(8,128)(2,1)}, bf16[768,384]{1,0:T(8,128)(2,1)}, u32[]{:S(2)}, u32[]{:S(2)}) collective-permute-start(bf16[768,384]{1,0:T(8,128)(2,1)} %get-tuple-element.115), channel_id=1, source_target_pairs={{0,24},{8,16},{16,8},{24,0},{1,25},{9,17},{17,9},{25,1},{2,26},{10... | collective-permute-start | bytes 1769480 | tf_op jit(solution)/shard_map/ppermute | solution.py:473
  407.5 56.9 %collective-permute-start.73 = (bf16[768,384]{1,0:T(8,128)(2,1)}, bf16[768,384]{1,0:T(8,128)(2,1)}, u32[]{:S(2)}, u32[]{:S(2)}) collective-permute-start(bf16[768,384]{1,0:T(8,128)(2,1)} %get-tuple-element.116), channel_id=1, source_target_pairs={{0,16},{8,24},{16,0},{24,8},{1,17},{9,25},{17,1},{25,9},{2,18},{10... | collective-permute-start | bytes 1769480 | tf_op jit(solution)/shard_map/ppermute | solution.py:473
  408.6 55.8 %collective-permute-start.72 = (bf16[768,384]{1,0:T(8,128)(2,1)}, bf16[768,384]{1,0:T(8,128)(2,1)}, u32[]{:S(2)}, u32[]{:S(2)}) collective-permute-start(bf16[768,384]{1,0:T(8,128)(2,1)} %get-tuple-element.117), channel_id=1, source_target_pairs={{0,8},{8,0},{16,24},{24,16},{1,9},{9,1},{17,25},{25,17},{2,10},{10... | collective-permute-start | bytes 1769480 | tf_op jit(solution)/shard_map/ppermute | solution.py:473
  469.7 120.6 %reduce-scatter.9.cloned.1.call-start = ((), (), s32[]{:S(2)}) async-start(), calls=%async_computation.8 | async-start | bytes 2654208 | tf_op jit(solution)/shard_map/reduce_scatter | solution.py:777
  520.6 136.7 %reduce-scatter.7.cloned.1.call-start = ((), (), s32[]{:S(2)}) async-start(), calls=%async_computation.7 | async-start | bytes 6635520 | tf_op jit(solution)/shard_map/reduce_scatter | solution.py:796
  539.5 143.0 %all-gather.19.cloned.1.call-start = ((), (), s32[]{:S(2)}) async-start(), calls=%async_computation.11 | async-start | bytes 1474560 | tf_op jit(solution)/shard_map/all_gather | solution.py:778
  551.6 149.2 %all-gather.17.cloned.1.call-start = ((), (), s32[]{:S(2)}) async-start(), calls=%async_computation.9 | async-start | bytes 1474560 | tf_op jit(solution)/shard_map/all_gather | solution.py:778
  590.3 179.5 %reduce-scatter.5.cloned.1.call-start = ((), (), s32[]{:S(2)}) async-start(), calls=%async_computation.6 | async-start | bytes 6635520 | tf_op jit(solution)/shard_map/reduce_scatter | solution.py:796
  608.5 203.8 %all-gather.27.cloned.1.call-start = ((), (), s32[]{:S(2)}) async-start(), calls=%async_computation.15 | async-start | bytes 3686400 | tf_op jit(solution)/shard_map/all_gather | solution.py:797
  657.3 199.2 %all-gather.25.cloned.1.call-start = ((), (), s32[]{:S(2)}) async-start(), calls=%async_computation.14 | async-start | bytes 3686400 | tf_op jit(solution)/shard_map/all_gather | solution.py:797
  (163 other events, 3100.4 us)
Sparse Core Ops, SparseCore 0:
  9.9 34.3 all-gather.20
  46.0 48.9 all-gather.22
  97.2 61.5 all-gather.12
  160.3 60.1 all-gather.14
  469.9 33.2 reduce-scatter.10
  520.7 33.2 reduce-scatter.8
  556.3 76.2 reduce-scatter.6
  634.6 36.6 all-gather.18
  673.2 27.5 all-gather.16
  703.7 66.0 reduce-scatter.4
  771.6 40.6 all-gather.26
  814.1 42.3 all-gather.24

commit v2 on v1

v2 whole, which is shorter than its diff:
```python
from functools import partial

import jax
import jax.numpy as jnp
from jax import lax
from jax.experimental import pallas as pl
from jax.experimental.pallas import tpu as pltpu
from jax.sharding import Mesh
from jax.sharding import PartitionSpec as P

BF = jnp.bfloat16
F32 = jnp.float32
HIGHEST = lax.Precision.HIGHEST
EPSILON = 1e-05
HEAD_DIM = 64
STATE = 128
LANES = 128
CHUNK = 128
HALO = 8
FAR = -1e30
PLANE = ("z", "core")


def mm(a, b):
    return lax.dot_general(a, b, (((1,), (0,)), ((), ())), preferred_element_type=F32)


def mm_bt(a, b):
    return lax.dot_general(a, b, (((1,), (1,)), ((), ())), preferred_element_type=F32)


def mm_at(a, b):
    return lax.dot_general(a, b, (((0,), (0,)), ((), ())), preferred_element_type=F32)


def halves(x, count):
    out = []
    for _ in range(count):
        part = x.astype(BF)
        out.append(part)
        x = x - part.astype(F32)
    return out


def mm_fine(a, b, count):
    return sum(mm(part, b) for part in halves(a, count))


def mm_fine_right(a, b, count):
    return sum(mm(a, part) for part in halves(b, count))


def iota2(shape, dim):
    return lax.broadcasted_iota(jnp.int32, shape, dim)


def head_spread(width):
    return (iota2((LANES, width), 1) // HEAD_DIM == iota2((LANES, width), 0)).astype(BF)


def head_gather(width):
    return (iota2((width, LANES), 0) // HEAD_DIM == iota2((width, LANES), 1)).astype(BF)


def softplus(x):
    return jnp.maximum(x, 0.0) + jnp.log1p(jnp.exp(-jnp.abs(x)))


def chunk_terms(step, age, bias_row, decay_row):
    raw = step + bias_row
    dt = softplus(raw)
    rate = -dt * decay_row
    rows = iota2((CHUNK, CHUNK), 0)
    cols = iota2((CHUNK, CHUNK), 1)
    lower = (cols <= rows).astype(BF)
    total = mm_fine_right(lower, rate, 3)
    pos = iota2((CHUNK, 1), 0)
    first = pos - age
    bias = jnp.where((cols <= rows) & (cols >= first), 0.0, FAR)
    first_last = first[CHUNK - 1 :, :]
    enter = jnp.exp(total) * (first < 0).astype(F32)
    last = total[CHUNK - 1 :, :]
    leave = jnp.exp(last - total) * (pos >= first_last).astype(F32)
    through = jnp.exp(last) * (first_last < 0).astype(F32)
    return raw, dt, rate, total, bias, enter, leave, through


def shard_refs(refs, count):
    used = count + 1 if count == 4 else count
    return refs[:used], refs[used:]


def to_order(refs, buf, shift, count, at):
    for k in range(count):
        place = jnp.bitwise_xor(shift, k)
        if count == 4 and k == 3:
            low, high, blocks = refs[3], refs[4], at[1]

            @pl.when(at[0] < blocks // 2)
            def _():
                buf[place] = low[0]

            @pl.when(at[0] >= blocks // 2)
            def _():
                buf[place] = high[0]

        else:
            buf[place] = refs[k][0]


def shard_specs(count, blocks, q, width, place):
    one = pl.BlockSpec((1, q, width), lambda i, s: (place(i, s), 0, 0))
    if count != 4:
        return [one] * count
    half = blocks // 2
    low = pl.BlockSpec((1, q, width), lambda i, s: (jnp.minimum(place(i, s), half - 1), 0, 0))
    high = pl.BlockSpec((1, q, width), lambda i, s: (jnp.maximum(place(i, s) - half, 0), 0, 0))
    return [one, one, one, low, high]


def conv_sum(ext, age, weights, bias_row, rows):
    out = jnp.zeros((rows, ext.shape[1]), F32) + bias_row
    for j in range(4):
        part = ext[pl.ds(HALO - j, rows), :]
        if j:
            part = jnp.where(age >= j, part, 0.0)
        out = out + weights[3 - j : 4 - j, :] * part
    return out


def forward_kernel(shift_ref, *refs, count, cd, ordered):
    unit_refs, refs = shard_refs(refs, count)
    weight_ref, age_ref, pc_ref, ph_ref, refs = *refs[:4], refs[4:]
    unit_ref, mixed_ref, gated_ref, pre_ref, ssd_ref, states_ref, sums_ref, refs = *refs[:7], refs[7:]
    unit_buf, gated_buf, ext, state, sums_buf = refs
    grid_at = pl.program_id(0)
    blocks = pl.num_programs(0)
    shift = shift_ref[0]
    conv_ch = cd + 2 * STATE
    q = unit_buf.shape[1]
    rows = count * q

    @pl.when(grid_at == 0)
    def _():
        ext[0:HALO, :] = jnp.zeros((HALO, conv_ch), F32)
        state[...] = jnp.zeros_like(state)

    @pl.when(grid_at > 0)
    def _():
        ext[0:HALO, :] = ext[rows : rows + HALO, :]

    to_order(unit_refs, unit_buf, shift, count, (jnp.bitwise_xor(grid_at, shift_ref[1]), blocks))
    unit = unit_buf[...].reshape(rows, unit_buf.shape[2])
    unit_ref[0] = unit
    mixed_ref[0] = mm(unit, weight_ref[...].reshape(-1, weight_ref.shape[2]))
    ext[HALO : HALO + rows, :] = mixed_ref[0, :, cd : cd + conv_ch]
    age = age_ref[0][:rows, :]
    pre = conv_sum(ext, age, pc_ref[0:4, :], pc_ref[4:5, :], rows)
    pre_ref[0] = pre
    xbc = (pre * jax.nn.sigmoid(pre)).astype(BF)
    skip_row = pc_ref[5:6, :cd]
    gain_row = pc_ref[6:7, :cd]
    bias_row = ph_ref[0:1, :]
    decay_row = ph_ref[1:2, :]
    spread = head_spread(cd)
    low_half = iota2((CHUNK, LANES), 1) < HEAD_DIM
    for c in range(rows // CHUNK):
        at = slice(c * CHUNK, (c + 1) * CHUNK)
        raw, dt, rate, total, bias, enter, leave, through = chunk_terms(
            mixed_ref[0, at, cd + conv_ch :], age[at], bias_row, decay_row
        )
        values = xbc[at, :cd]
        writers = xbc[at, cd : cd + STATE]
        readers = xbc[at, cd + STATE :]
        total_t = total.T
        dt_t = dt.T
        wide = mm_fine(
            jnp.concatenate([enter, leave * dt, jnp.broadcast_to(through, (8, LANES))], axis=0),
            spread,
            2,
        )
        scores = mm_bt(readers, writers)
        held = state[...]
        states_ref[0, c] = held.astype(BF)
        carried = mm(readers, held.astype(BF)) * wide[:CHUNK]
        values_f = values.astype(F32)
        pairs = []
        for pr in range(cd // LANES):
            mixing = []
            for h in (2 * pr, 2 * pr + 1):
                gap = total[:, h : h + 1] - total_t[h : h + 1, :] + bias
                mixing.append((jnp.exp(gap) * scores * dt_t[h : h + 1, :]).astype(BF))
            pair = values[:, pr * LANES : (pr + 1) * LANES]
            zero = jnp.zeros_like(pair)
            stacked = jnp.concatenate(
                [jnp.where(low_half, pair, zero), jnp.where(low_half, zero, pair)], axis=0
            )
            pairs.append(mm(jnp.concatenate(mixing, axis=1), stacked))
        ssd = jnp.concatenate(pairs, axis=1) + carried + skip_row * values_f
        ssd_ref[0, at, :] = ssd
        state[...] = held * wide[2 * CHUNK : 2 * CHUNK + 1] + mm_at(
            writers, (wide[CHUNK : 2 * CHUNK] * values_f).astype(BF)
        )
    ssd = ssd_ref[0]
    gate = mixed_ref[0, :, :cd]
    v = ssd * (gate * jax.nn.sigmoid(gate))
    squares = v * v
    partial_sums = squares[:, :LANES]
    for b in range(1, cd // LANES):
        partial_sums = partial_sums + squares[:, b * LANES : (b + 1) * LANES]
    weighted = v * gain_row
    gated = weighted.astype(BF).reshape(count, q, cd)
    sums = partial_sums.astype(BF).reshape(count, q, LANES)
    if ordered:
        gated_ref[:, 0] = gated
        sums_ref[:, 0] = sums
        return
    gated_buf[...] = gated
    sums_buf[...] = sums
    for k in range(count):
        gated_ref[k, 0] = gated_buf[jnp.bitwise_xor(shift, k)]
        sums_ref[k, 0] = sums_buf[jnp.bitwise_xor(shift, k)]


def backward_kernel(shift_ref, *refs, count, cd, own_scales):
    shift = shift_ref[0]
    grid_at = pl.program_id(0)
    blocks = pl.num_programs(0)
    if own_scales:
        grad_ref, scale_ref, refs = refs[0], refs[1], refs[2:]
    else:
        grad_refs, refs = shard_refs(refs, count)
        weight_out_ref, refs = refs[0], refs[1:]
    weight_ref, mixed_ref, age_ref, pc_ref, ph_ref, pre_ref, ssd_ref, states_ref = refs[:8]
    mixed_grad_ref, unit_grad_ref, wide_sums, head_sums = refs[8:12]
    out_buf, ext, adjoint = refs[12:15]
    conv_ch = cd + 2 * STATE
    rows = mixed_ref.shape[1]
    q = rows // count

    @pl.when(grid_at == 0)
    def _():
        ext[rows : rows + HALO, :] = jnp.zeros((HALO, conv_ch), F32)
        adjoint[...] = jnp.zeros_like(adjoint)
        wide_sums[...] = jnp.zeros_like(wide_sums)
        head_sums[...] = jnp.zeros_like(head_sums)

    @pl.when(grid_at > 0)
    def _():
        ext[rows : rows + HALO, :] = ext[0:HALO, :]

    age_ext = age_ref[0]
    age = age_ext[:rows, :]
    skip_row = pc_ref[5:6, :cd]
    gain_row = pc_ref[6:7, :cd]
    bias_row = ph_ref[0:1, :]
    decay_row = ph_ref[1:2, :]

    if own_scales:
        extra = scale_ref[:, 0].reshape(rows, 2)
        scaled = grad_ref[:, 0].reshape(rows, cd) * extra[:, 0:1]
        mean_term = extra[:, 1:2]
    else:
        grad_buf = refs[15]
        at = jnp.bitwise_xor(blocks - 1 - grid_at, shift_ref[1])
        to_order(grad_refs, grad_buf, shift, count, (at, blocks))
        grad = grad_buf[...].reshape(rows, grad_buf.shape[2])
        model = weight_out_ref.shape[1]
        scaled = mm_bt(grad[:, :model], weight_out_ref[...])
        extra = grad[:, model:].astype(F32)
        mean_term = extra[:, 0:1] + extra[:, 1:2]
    gate = mixed_ref[0, :, :cd]
    ssd = ssd_ref[0]
    sg = jax.nn.sigmoid(gate)
    sl = gate * sg
    v = ssd * sl
    v_grad = scaled * gain_row - mean_term * v
    wide_sums[6:7, :cd] += jnp.sum(scaled * v, axis=0, keepdims=True)
    d_ssd = v_grad * sl
    d_gate = v_grad * ssd * (sg * (1.0 + gate * (1.0 - sg)))
    out_buf[:, :cd] = d_gate.astype(BF)

    pre = pre_ref[0]
    sp = jax.nn.sigmoid(pre)
    xbc = (pre * sp).astype(BF)
    d_silu = sp * (1.0 + pre * (1.0 - sp))
    spread = head_spread(cd)
    gather = head_gather(cd)
    low_half = iota2((CHUNK, LANES), 1) < HEAD_DIM
    tri_rows = iota2((CHUNK, CHUNK), 0)
    tri_cols = iota2((CHUNK, CHUNK), 1)
    from_here = (tri_cols >= tri_rows).astype(BF)
    before = (tri_cols < tri_rows).astype(BF)
    heads = cd // HEAD_DIM
    pick_shape = (heads * CHUNK, LANES)
    pick_head = (iota2(pick_shape, 0) // CHUNK == iota2(pick_shape, 1)).astype(BF)

    for c in reversed(range(rows // CHUNK)):
        at = slice(c * CHUNK, (c + 1) * CHUNK)
        raw, dt, rate, total, bias, enter, leave, through = chunk_terms(
            mixed_ref[0, at, cd + conv_ch :], age[at], bias_row, decay_row
        )
        values = xbc[at, :cd]
        writers = xbc[at, cd : cd + STATE]
        readers = xbc[at, cd + STATE :]
        values_f = values.astype(F32)
        dy = d_ssd[at]
        wide_sums[5:6, :cd] += jnp.sum(values_f * dy, axis=0, keepdims=True)
        total_t = total.T
        dt_t = dt.T
        wide = mm_fine(
            jnp.concatenate([enter, leave, dt, jnp.broadcast_to(through, (8, LANES))], axis=0),
            spread,
            2,
        )
        enter_w = wide[:CHUNK]
        leave_w = wide[CHUNK : 2 * CHUNK]
        dt_w = wide[2 * CHUNK : 3 * CHUNK]
        through_w = wide[3 * CHUNK : 3 * CHUNK + 1]
        held = states_ref[0, c]
        adj = adjoint[...]
        adj_b = adj.astype(BF)
        scores = mm_bt(readers, writers)
        entered = enter_w * dy
        entered_b = entered.astype(BF)
        row_enter = entered * mm(readers, held)
        d_readers = mm_bt(entered_b, held)
        from_state = leave_w * mm(writers, adj_b)
        exits = values_f * from_state * dt_w
        d_writers = mm_bt((leave_w * dt_w * values_f).astype(BF), adj_b)
        through_sum = jnp.sum(adj * held.astype(F32), axis=0, keepdims=True) * through_w
        adjoint[...] = adj * through_w + mm_at(readers, entered_b)
        d_scores = jnp.zeros((CHUNK, CHUNK), F32)
        pulls = []
        kernels = []
        for pr in range(cd // LANES):
            dy_pair = dy[:, pr * LANES : (pr + 1) * LANES].astype(BF)
            zero = jnp.zeros_like(dy_pair)
            stacked = jnp.concatenate(
                [jnp.where(low_half, dy_pair, zero), jnp.where(low_half, zero, dy_pair)], axis=0
            )
            d_mix = mm_bt(stacked, values[:, pr * LANES : (pr + 1) * LANES])
            mixing = []
            for i, h in enumerate((2 * pr, 2 * pr + 1)):
                gap = total[:, h : h + 1] - total_t[h : h + 1, :] + bias
                decays = jnp.exp(gap)
                mixing.append((decays * scores).astype(BF))
                pull = d_mix[i * CHUNK : (i + 1) * CHUNK] * dt_t[h : h + 1, :] * decays
                d_scores = d_scores + pull
                kernels.append((pull * scores).astype(BF))
            pulls.append(mm_at(jnp.concatenate(mixing, axis=0), stacked))
        d_scaled = jnp.concatenate(pulls, axis=1) + from_state
        per_head = mm_fine(
            jnp.concatenate(
                [row_enter, exits, values_f * d_scaled, jnp.broadcast_to(through_sum, (8, cd))],
                axis=0,
            ),
            gather,
            2,
        )
        row_enter = per_head[:CHUNK]
        exits = per_head[CHUNK : 2 * CHUNK]
        d_dt = per_head[2 * CHUNK : 3 * CHUNK]
        passing = per_head[3 * CHUNK : 3 * CHUNK + 1]
        row_sums = mm(jnp.concatenate(kernels, axis=1), pick_head)
        col_sums = mm_at(jnp.concatenate(kernels, axis=0), pick_head)
        d_rate = (
            mm_fine_right(from_here, row_sums - col_sums + row_enter, 3)
            + mm_fine_right(before, exits, 3)
            + passing
        )
        d_raw = (d_dt - d_rate * decay_row) * jax.nn.sigmoid(raw)
        head_sums[0:1, :] += jnp.sum(d_raw, axis=0, keepdims=True)
        head_sums[1:2, :] += jnp.sum(d_rate * rate, axis=0, keepdims=True)
        d_scores_b = d_scores.astype(BF)
        d_readers = d_readers + mm(d_scores_b, writers)
        d_writers = d_writers + mm_at(d_scores_b, readers)
        d_values = dt_w * d_scaled + skip_row * dy
        ext[at, :] = jnp.concatenate([d_values, d_writers, d_readers], axis=1) * d_silu[at]
        out_buf[at, cd + conv_ch :] = d_raw.astype(BF)
    conv_in = mixed_ref[0, :, cd : cd + conv_ch]
    d_conv = jnp.zeros((rows, conv_ch), F32)
    for j in range(4):
        part = ext[pl.ds(j, rows), :]
        if j:
            part = jnp.where(age_ext[j : j + rows, :] >= j, part, 0.0)
        else:
            wide_sums[4:5, :] += jnp.sum(part, axis=0, keepdims=True)
        d_conv = d_conv + pc_ref[3 - j : 4 - j, :] * part
        wide_sums[3 - j : 4 - j, :] += jnp.sum(part * conv_in, axis=0, keepdims=True)
    out_buf[:, cd : cd + conv_ch] = d_conv.astype(BF)
    mixed_grad_ref[0] = out_buf[...]
    weight = weight_ref[...].reshape(-1, weight_ref.shape[2])
    unit_grad = mm_bt(out_buf[...], weight).astype(BF)
    unit_grad_buf = refs[-1]
    unit_grad_buf[...] = unit_grad.reshape(unit_grad_buf.shape)
    for k in range(count):
        unit_grad_ref[k, 0] = unit_grad_buf[jnp.bitwise_xor(shift, k)]


def whole(shape):
    return pl.BlockSpec(shape, lambda *_: (0,) * len(shape), pipeline_mode=pl.Buffered(1))


def mixer_forward(shift, units, weight, ordered, age, pc, ph):
    count = len(units)
    blocks, q, model = units[0].shape
    width = weight.shape[2]
    weight_block = (weight.shape[0], model // weight.shape[0], width)
    conv_ch = pc.shape[1]
    cd = conv_ch - 2 * STATE
    rows = count * q
    chunks = rows // CHUNK
    in_specs = shard_specs(count, blocks, q, model, lambda i, s: i ^ s[1]) + [
        whole(weight_block),
        pl.BlockSpec((1, rows + HALO, 1), lambda i, s: (i, 0, 0)),
        whole(pc.shape),
        whole(ph.shape),
    ]

    def in_order(*shape):
        return pl.BlockSpec((1,) + shape, lambda i, s: (i,) + (0,) * len(shape))

    def relative(last):
        return pl.BlockSpec((count, 1, q, last), lambda i, s: (0, i ^ s[1], 0, 0))

    return pl.pallas_call(
        partial(forward_kernel, count=count, cd=cd, ordered=ordered),
        out_shape=[
            jax.ShapeDtypeStruct((blocks, rows, model), BF),
            jax.ShapeDtypeStruct((blocks, rows, width), F32),
            jax.ShapeDtypeStruct((count, blocks, q, cd), BF),
            jax.ShapeDtypeStruct((blocks, rows, conv_ch), F32),
            jax.ShapeDtypeStruct((blocks, rows, cd), F32),
            jax.ShapeDtypeStruct((blocks, chunks, STATE, cd), BF),
            jax.ShapeDtypeStruct((count, blocks, q, LANES), BF),
        ],
        grid_spec=pltpu.PrefetchScalarGridSpec(
            num_scalar_prefetch=1,
            grid=(blocks,),
            in_specs=in_specs,
            out_specs=[
                in_order(rows, model),
                in_order(rows, width),
                relative(cd),
                in_order(rows, conv_ch),
                in_order(rows, cd),
                in_order(chunks, STATE, cd),
                relative(LANES),
            ],
            scratch_shapes=[
                pltpu.VMEM((count, q, model), BF),
                pltpu.VMEM((count, q, cd), BF),
                pltpu.VMEM((rows + HALO, conv_ch), F32),
                pltpu.VMEM((STATE, cd), F32),
                pltpu.VMEM((count, q, LANES), BF),
            ],
        ),
        compiler_params=pltpu.CompilerParams(vmem_limit_bytes=52 * 2**20),
        cost_estimate=pl.CostEstimate(
            flops=2 * 10**10, bytes_accessed=4 * 10**7, transcendentals=10**6
        ),
    )(shift, *flat_shards(units), weight, age, pc, ph)


def flat_shards(shards):
    out = []
    for shard in shards:
        out += list(shard) if isinstance(shard, tuple) else [shard]
    return out


def mixer_backward(
    shift, grads, scales, weight_out, weight, mixed, age, pc, ph, pre, ssd, states, model
):
    blocks, rows, width = mixed.shape
    weight_block = (weight.shape[0], model // weight.shape[0], width)
    conv_ch = pc.shape[1]
    cd = conv_ch - 2 * STATE
    chunks = rows // CHUNK
    top = blocks - 1
    if scales is not None:
        count, _, q, _ = grads.shape
        in_specs = [
            pl.BlockSpec((count, 1, q, cd), lambda i, s: (0, (top - i) ^ s[1], 0, 0)),
            pl.BlockSpec((count, 1, q, 2), lambda i, s: (0, (top - i) ^ s[1], 0, 0)),
        ]
        args = [grads, scales]
    else:
        count = len(grads)
        _, q, grad_width = grads[0].shape
        in_specs = shard_specs(count, blocks, q, grad_width, lambda i, s: (top - i) ^ s[1])
        in_specs.append(whole(weight_out.shape))
        args = flat_shards(grads) + [weight_out]

    def in_order(*shape):
        return pl.BlockSpec((1,) + shape, lambda i, s: (top - i,) + (0,) * len(shape))

    in_specs += [
        whole(weight_block),
        in_order(rows, width),
        in_order(rows + HALO, 1),
        whole(pc.shape),
        whole(ph.shape),
        in_order(rows, conv_ch),
        in_order(rows, cd),
        in_order(chunks, STATE, cd),
    ]
    args += [weight, mixed, age, pc, ph, pre, ssd, states]
    scratch = [
        pltpu.VMEM((rows, width), BF),
        pltpu.VMEM((rows + HALO, conv_ch), F32),
        pltpu.VMEM((STATE, cd), F32),
    ]
    if scales is None:
        scratch.append(pltpu.VMEM((count, q, grad_width), BF))
    scratch.append(pltpu.VMEM((count, q, model), BF))
    return pl.pallas_call(
        partial(backward_kernel, count=count, cd=cd, own_scales=scales is not None),
        out_shape=[
            jax.ShapeDtypeStruct((blocks, rows, width), BF),
            jax.ShapeDtypeStruct((count, blocks, q, model), BF),
            jax.ShapeDtypeStruct((8, conv_ch), F32),
            jax.ShapeDtypeStruct((8, LANES), F32),
        ],
        grid_spec=pltpu.PrefetchScalarGridSpec(
            num_scalar_prefetch=1,
            grid=(blocks,),
            in_specs=in_specs,
            out_specs=[
                in_order(rows, width),
                pl.BlockSpec((count, 1, q, model), lambda i, s: (0, (top - i) ^ s[1], 0, 0)),
                pl.BlockSpec((8, conv_ch), lambda i, s: (0, 0)),
                pl.BlockSpec((8, LANES), lambda i, s: (0, 0)),
            ],
            scratch_shapes=scratch,
        ),
        compiler_params=pltpu.CompilerParams(vmem_limit_bytes=52 * 2**20),
        cost_estimate=pl.CostEstimate(
            flops=4 * 10**10, bytes_accessed=5 * 10**7, transcendentals=2 * 10**6
        ),
    )(shift, *args)


SMALL_ROWS = 16


def shard_kernel(at_ref, *refs, cd, hd, small):
    gate_ref, values_ref, rest_ref, step_ref, gain_ref, refs = *refs[:5], refs[5:]
    gain = gain_ref[...]
    rows = gain.shape[0]
    conv_ch = cd + 2 * STATE

    def scaled(ref):
        return (ref[0].astype(F32) * gain).astype(BF)

    out_ref = refs[small]
    out_ref[0:rows, :cd] = scaled(gate_ref)
    out_ref[0:rows, cd : 2 * cd] = scaled(values_ref)
    out_ref[0:rows, 2 * cd : cd + conv_ch] = scaled(rest_ref)
    steps = step_ref[0]
    shape = (steps.shape[0], LANES)
    heads, cols = iota2(shape, 0), iota2(shape, 1)
    chosen = ((heads == at_ref[0] * hd + cols) & (cols < hd)).astype(BF)
    out_ref[0:rows, cd + conv_ch :] = (mm_at(steps, chosen) * gain).astype(BF)
    if small:
        buf = refs[small + 1]
        buf[...] = jnp.zeros_like(buf)
        at, lane = 0, 0
        for ref in refs[:small]:
            count, lanes = ref.shape
            buf[at : at + count, lane : lane + lanes] = ref[...].astype(F32)
            if lanes < LANES:
                lane += LANES
            else:
                at += count
        out_ref[rows : rows + SMALL_ROWS, :] = buf[...].astype(BF)


def weight_shard(shift, layer, input_proj, step_proj, gain, cd, hd, small=()):
    _, rows, columns = input_proj.shape
    heads = step_proj.shape[1]
    parts = heads // hd
    at_rest = (columns - 2 * STATE) // (2 * STATE)
    width = 2 * cd + 2 * STATE + LANES
    full = rows + SMALL_ROWS if small else rows
    return pl.pallas_call(
        partial(shard_kernel, cd=cd, hd=hd, small=len(small)),
        out_shape=jax.ShapeDtypeStruct((full, width), BF),
        grid_spec=pltpu.PrefetchScalarGridSpec(
            num_scalar_prefetch=1,
            grid=(1,),
            in_specs=[
                pl.BlockSpec((1, rows, cd), lambda i, s: (layer, 0, s[0])),
                pl.BlockSpec((1, rows, cd), lambda i, s: (layer, 0, parts + s[0])),
                pl.BlockSpec((1, rows, 2 * STATE), lambda i, s: (layer, 0, at_rest)),
                pl.BlockSpec((1, heads, rows), lambda i, s: (layer, 0, 0)),
                whole((rows, 1)),
            ]
            + [whole(x.shape) for x in small],
            out_specs=pl.BlockSpec((full, width), lambda i, s: (0, 0)),
            scratch_shapes=[pltpu.VMEM((SMALL_ROWS, width), F32)] if small else [],
        ),
        cost_estimate=pl.CostEstimate(flops=10**6, bytes_accessed=2 * 10**6, transcendentals=0),
    )(shift, input_proj, input_proj, input_proj, step_proj, gain[:, None], *small)


def place_kernel(shift_ref, *refs, count, dim):
    out_ref = refs[count]
    for k in range(count):
        at = (slice(None),) * dim + (jnp.bitwise_xor(shift_ref[0], k),)
        out_ref[at] = refs[k][...]


def place(shift, parts, dim):
    shape = parts[0].shape
    full = shape[:dim] + (len(parts),) + shape[dim:]
    return pl.pallas_call(
        partial(place_kernel, count=len(parts), dim=dim),
        out_shape=jax.ShapeDtypeStruct(full, parts[0].dtype),
        grid_spec=pltpu.PrefetchScalarGridSpec(
            num_scalar_prefetch=1,
            grid=(1,),
            in_specs=[whole(part.shape) for part in parts],
            out_specs=whole(full),
        ),
        compiler_params=pltpu.CompilerParams(vmem_limit_bytes=40 * 2**20),
        cost_estimate=pl.CostEstimate(flops=0, bytes_accessed=5 * 10**6, transcendentals=0),
    )(shift, *parts)


def finish_kernel(shift_ref, *refs, count, cd, inner, rows, out_part, apart):
    part_refs, refs = refs[:count], refs[count:]
    own_refs, refs = (refs[:count], refs[count:]) if apart else (None, refs)
    weight_ref, gain_ref, refs = refs[0], refs[1], refs[2:]
    grad_ref, out_ref, norm_ref = refs[-3:]
    gain = gain_ref[...]
    norm = jnp.zeros((rows, 1), F32)

    def put(at, value, norm):
        cols = pl.ds(at, value.shape[1])
        grad_ref[0, :, cols] = value * gain
        return norm + jnp.sum(
            value * weight_ref[0, :, cols].astype(F32), axis=1, keepdims=True
        )

    rest = jnp.zeros((rows, 2 * STATE), F32)
    for k in range(count):
        j = jnp.bitwise_xor(shift_ref[0], k)
        part = part_refs[k][:rows, :].astype(F32)
        norm = put(pl.multiple_of(j * cd, LANES), part[:, :cd], norm)
        norm = put(pl.multiple_of(inner + j * cd, LANES), part[:, cd : 2 * cd], norm)
        rest = rest + part[:, 2 * cd : 2 * cd + 2 * STATE]
        own = (own_refs[k][...] if apart else part_refs[k][rows:, :]).astype(F32)
        out_ref[0, pl.ds(pl.multiple_of(j * out_part, 8), out_part), :] = own[
            :out_part, : out_ref.shape[2]
        ]
    norm_ref[...] = put(2 * inner, rest, norm)


def finish(layer, shift, parts, apart, weight, gain, out_part, out_cols, before, cd, inner):
    count = len(parts)
    layers, rows, columns = weight.shape
    in_specs = [whole(part.shape) for part in parts + (apart or [])] + [
        pl.BlockSpec((1, rows, columns), lambda i, s: (layer, 0, 0)),
        whole((rows, 1)),
    ]
    args = parts + (apart or []) + [weight, gain[:, None]]
    aliases = {}
    if before is not None:
        aliases = {len(args) + 1: 0, len(args) + 2: 1}
        in_specs += [pl.BlockSpec(memory_space=pl.ANY)] * 2
        args += list(before)
    return pl.pallas_call(
        partial(
            finish_kernel,
            count=count,
            cd=cd,
            inner=inner,
            rows=rows,
            out_part=out_part,
            apart=apart is not None,
        ),
        out_shape=[
            jax.ShapeDtypeStruct((layers, rows, columns), F32),
            jax.ShapeDtypeStruct((layers, count * out_part, out_cols), F32),
            jax.ShapeDtypeStruct((rows, 1), F32),
        ],
        grid_spec=pltpu.PrefetchScalarGridSpec(
            num_scalar_prefetch=1,
            grid=(1,),
            in_specs=in_specs,
            out_specs=[
                pl.BlockSpec((1, rows, columns), lambda i, s: (layer, 0, 0)),
                pl.BlockSpec((1, count * out_part, out_cols), lambda i, s: (layer, 0, 0)),
                whole((rows, 1)),
            ],
        ),
        input_output_aliases=aliases,
        compiler_params=pltpu.CompilerParams(vmem_limit_bytes=48 * 2**20),
        cost_estimate=pl.CostEstimate(flops=10**7, bytes_accessed=2 * 10**7, transcendentals=0),
    )(shift, *args)


def swap(value, axis, k, size):
    return lax.ppermute(value, axis, [(i, i ^ k) for i in range(size)])


def pick(value, index):
    return lax.dynamic_index_in_dim(value, index, 0, keepdims=False)


def tie(*values):
    return lax.optimization_barrier(values)


def after(value, *first):
    return lax.optimization_barrier((value, first))[0]


def sends(parts, base, size):
    return [pick(parts, base ^ k) for k in range(size)]


def moved(items, axis, what):
    size = len(items)
    with jax.named_scope(what):
        return [items[0]] + [swap(items[k], axis, k, size) for k in range(1, size)]


def gather_rows(shard, n, what, arrived=None):
    if n != 4:
        everything = lax.all_gather(shard, "dp")
        mine = lax.axis_index("dp")
        return [pick(everything, mine ^ k) for k in range(n)], arrived
    half = shard.shape[0] // 2
    with jax.named_scope(what):
        first = swap(shard, "dp", 1, n)
        second = swap(shard, "dp", 2, n)
        if arrived is not None:
            first, second, arrived = tie(first, second, arrived)
        low = swap(first[:half], "dp", 2, n)
        high = swap(second[half:], "dp", 1, n)
    return [shard, first, second, (low, high)], arrived


def joined(shards):
    return [
        jnp.concatenate(shard, axis=0) if isinstance(shard, tuple) else shard for shard in shards
    ]


def reduce_rows(parts, n, what, during=None):
    with jax.named_scope(what):
        return reduce_parts(parts, n, during)


def reduce_parts(parts, n, during=None):
    if n != 4:
        mine = lax.axis_index("dp")
        ordered = jnp.stack([pick(parts, mine ^ j) for j in range(n)])
        total = lax.psum_scatter(ordered, "dp", scatter_dimension=0, tiled=False).astype(F32)
        return (total, None if during is None else during[0](*during[1]))
    half = parts.shape[1] // 2
    a, b = parts[:, :half], parts[:, half:]
    send_a, send_b = tie(jnp.stack([a[1], a[3]]), jnp.stack([b[2], b[3]]))
    got_a = swap(send_a, "dp", 1, n)
    got_b = swap(send_b, "dp", 2, n)
    work = None
    if during is not None:
        function, args = during
        work = function(*after(args, send_a, send_b))
        got_a, got_b, work = tie(got_a, got_b, work)
    on_a = (a[2].astype(F32) + got_a[1].astype(F32)).astype(BF)
    on_b = (b[1].astype(F32) + got_b[1].astype(F32)).astype(BF)
    last_a = swap(on_a, "dp", 2, n)
    last_b = swap(on_b, "dp", 1, n)
    sum_a = a[0].astype(F32) + got_a[0].astype(F32) + last_a.astype(F32)
    sum_b = b[0].astype(F32) + got_b[0].astype(F32) + last_b.astype(F32)
    return jnp.concatenate([sum_a, sum_b], axis=0), work


def both_cores(block, what):
    core = lax.axis_index("core")
    keep = pick(block, core)
    with jax.named_scope(what):
        other = lax.ppermute(pick(block, 1 - core), "core", [(0, 1), (1, 0)])
    first = jnp.where(core == 0, keep, other)
    second = jnp.where(core == 0, other, keep)
    return jnp.concatenate([first, second], axis=0)


def to_groups(both, n, what):
    q = both.shape[0] // n
    d = lax.axis_index("dp")
    return jnp.stack(moved(sends(both.reshape(n, q, -1), d, n), "dp", what))


def to_chunks(groups, z_count, what):
    d, z = lax.axis_index("dp"), lax.axis_index("z")
    return jnp.stack(moved(sends(groups, z ^ d, z_count), "z", what))


def from_groups(groups, n, what):
    d, z = lax.axis_index("dp"), lax.axis_index("z")
    return jnp.stack(moved(sends(groups, z ^ d, n), "dp", what))


def from_both(parts, what):
    n = parts.shape[0]
    d, core = lax.axis_index("dp"), lax.axis_index("core")
    half = n // 2

    def side(c):
        return jnp.concatenate([pick(parts, (half * c + i) ^ d) for i in range(half)], axis=0)

    with jax.named_scope(what):
        other = lax.ppermute(side(1 - core), "core", [(0, 1), (1, 0)])
    keep = side(core)
    return jnp.stack([jnp.where(core == 0, keep, other), jnp.where(core == 0, other, keep)])


def on_device(
    hidden_in,
    doc_lengths,
    norm_gain,
    input_proj,
    step_proj,
    conv_weight,
    conv_bias,
    step_bias,
    decay_log,
    skip_gain,
    gate_gain,
    output_proj,
    cotangent,
    *,
    n,
    z_count,
):
    layers = norm_gain.shape[0]
    owners = 2 * z_count
    d_rows = norm_gain.shape[1]
    width_d = d_rows * owners
    heads_f = step_bias.shape[1]
    heads = heads_f * owners
    hd = heads // n
    cd = hd * HEAD_DIM
    inner = heads * HEAD_DIM
    conv_f = conv_bias.shape[1]
    conv_ch = cd + 2 * STATE
    gate_f = gate_gain.shape[1]
    out_rows = output_proj.shape[1]
    width_in = cd + conv_ch + LANES
    step_at = cd + conv_ch
    d = lax.axis_index("dp")
    z = lax.axis_index("z")
    core = lax.axis_index("core")
    shift = jnp.stack([d, z]).astype(jnp.int32)

    small_len = 5 * conv_f + gate_f + 3 * heads_f
    small_cols = -(-small_len // d_rows)

    def small_split(flat):
        sizes = (4 * conv_f, conv_f, gate_f, heads_f, heads_f, heads_f)
        parts, at = [], 0
        for size in sizes:
            parts.append(flat[..., at : at + size])
            at += size
        return parts

    small_lanes = max(-(-max(conv_f, gate_f) // LANES), 3) * LANES

    def small_unpack(everything):
        everything = everything.astype(F32)

        def rows(at, count, lanes):
            part = everything[:, at : at + count, lanes]
            return part.transpose(1, 0, 2).reshape(count, -1)

        def mine(x):
            width = x.shape[1] // n
            return lax.dynamic_slice_in_dim(x, d * width, width, 1)

        conv = rows(0, 5 * layers, slice(0, conv_f))
        conv = jnp.concatenate([mine(conv[:, :inner]), conv[:, inner:]], axis=1)
        gain = mine(rows(5 * layers, layers, slice(0, gate_f)))
        at = 6 * layers
        bias, decay, skip = (
            mine(rows(at, layers, slice(i * LANES, i * LANES + heads_f))) for i in range(3)
        )
        skip = jnp.broadcast_to(skip[:, :, None], (layers, hd, HEAD_DIM)).reshape(layers, cd)
        wide = jnp.pad(jnp.stack([skip, gain], axis=1), ((0, 0), (0, 1), (0, 2 * STATE)))
        head = jnp.stack([bias, jnp.exp(decay)], axis=1)
        head = jnp.pad(head, ((0, 0), (0, 6), (0, LANES - hd)))
        pcs = [
            jnp.concatenate(
                [conv[4 * l : 4 * l + 4], conv[4 * layers + l : 4 * layers + l + 1], wide[l]],
                axis=0,
            )
            for l in range(layers)
        ]
        return pcs, [head[l] for l in range(layers)]

    out_part = out_rows // n

    def shard_out(layer):
        return lax.dynamic_slice_in_dim(output_proj[layer], d * out_part, out_part, 0)

    def column_sends(column):
        return sends(column.reshape(n, 2, out_part, width_d), d, n)

    def weight_out(parts):
        return place(shift, parts, 1).reshape(cd, width_d)

    def grad_out_sends(d_out):
        return sends(d_out.reshape(2, n, out_part, width_d).transpose(1, 0, 2, 3), d, n)

    def grad_out_owned(by_rows):
        rows_all = place(shift, by_rows, 0).reshape(owners, out_part, width_d)
        return lax.psum_scatter(rows_all, PLANE, scatter_dimension=0)

    def small_out(wide_sums, head_sums):
        conv_full = jnp.concatenate([jnp.zeros((5, inner), F32), wide_sums[:5, cd:]], axis=1)
        conv_full = lax.dynamic_update_slice(conv_full, wide_sums[:5, :cd], (0, d * cd))
        conv_full = conv_full.reshape(5, owners, conv_f).transpose(1, 0, 2).reshape(owners, -1)
        gain_full = lax.dynamic_update_slice(jnp.zeros((inner,), F32), wide_sums[6, :cd], (d * cd,))
        skip_sum = jnp.sum(wide_sums[5, :cd].reshape(hd, HEAD_DIM), axis=1)
        head_full = lax.dynamic_update_slice(
            jnp.zeros((3, heads), F32),
            jnp.stack([head_sums[0, :hd], head_sums[1, :hd], skip_sum]),
            (0, d * hd),
        )
        head_full = head_full.reshape(3, owners, heads_f).transpose(1, 0, 2).reshape(owners, -1)
        small = jnp.concatenate([conv_full, gain_full.reshape(owners, gate_f), head_full], axis=1)
        small = jnp.pad(small, ((0, 0), (0, small_cols * d_rows - small_len)))
        return small.reshape(owners * d_rows, small_cols)

    def grad_in(unit_cat, d_mixed, wide_sums, head_sums):
        small = small_out(wide_sums, head_sums)
        product = mm_at(flat(unit_cat), flat(d_mixed))
        return (
            product + jnp.pad(small, ((0, 0), (step_at + hd, LANES - hd - small_cols)))
        ).astype(BF)

    out_padded = -(-out_part // 16) * 16

    def owned_parts(own_in, own_out, what):
        own_out = jnp.pad(own_out, ((0, out_padded - out_part), (0, 0)))
        if width_in < width_d:
            return joined(gather_rows(own_in, n, what)[0]), joined(gather_rows(own_out, n, what)[0])
        own_out = jnp.pad(own_out, ((0, 0), (0, width_in - width_d)))
        return joined(gather_rows(jnp.concatenate([own_in, own_out], axis=0), n, what)[0]), None

    def finished_layer(layer, owned, before):
        parts, apart = owned
        at = slice(step_at + hd, step_at + hd + small_cols)
        small = sum(part[:d_rows, at].astype(F32) for part in parts)
        small = small_split(small.reshape(-1)[:small_len])
        steps = jnp.stack([part[:d_rows, step_at : step_at + hd] for part in parts])
        steps = jnp.stack([pick(steps, d ^ j) for j in range(n)]).astype(F32)
        steps = steps.transpose(0, 2, 1).reshape(heads, d_rows)
        gain = norm_gain[layer].astype(F32)
        in_all, out_all, norm_grad = finish(
            layer, shift, parts, apart, input_proj, gain, out_part, width_d, before, cd, inner
        )
        norm_grad = norm_grad[:, 0] + jnp.sum(steps * step_proj[layer].astype(F32), axis=0)
        rest = (
            norm_grad,
            steps * gain[None, :],
            small[0].reshape(4, conv_f),
            small[1],
            small[3],
            small[4],
            small[5],
            small[2],
        )
        return (in_all, out_all), rest

    both = lax.ppermute(
        doc_lengths,
        ("dp", "z"),
        [(i * z_count + j, j * z_count + i) for i in range(n) for j in range(z_count)],
    )
    ends = jnp.cumsum(pick(both, core))
    tok = hidden_in.shape[1]
    block_rows = 2 * tok
    row_len = block_rows * z_count
    q = block_rows // n
    positions = jnp.arange(row_len, dtype=jnp.int32)
    begin = jnp.max(jnp.where(ends[None, :] <= positions[:, None], ends[None, :], 0), axis=1)
    age = (positions - begin).reshape(z_count, block_rows)
    follow = jnp.concatenate([age[1:, :HALO], jnp.zeros((1, HALO), jnp.int32)], axis=0)
    age = jnp.concatenate([age, follow], axis=1)[:, :, None]

    def normalize(resid):
        inv = lax.rsqrt(jnp.mean(resid * resid, axis=-1, keepdims=True) + EPSILON)
        return inv, resid * inv

    def flat(x):
        return x.reshape(-1, x.shape[-1])

    def norm_back(back, resid, inv, normed_grad):
        u = resid * inv
        return back + inv * (
            normed_grad - u * jnp.mean(normed_grad * u, axis=-1, keepdims=True)
        )

    both = both_cores(hidden_in, "hidden_cores")
    small = (
        conv_weight.reshape(layers * 4, conv_f),
        conv_bias,
        gate_gain,
        step_bias,
        decay_log,
        skip_gain,
    )
    shard0 = weight_shard(
        shift, 0, input_proj, step_proj, norm_gain[0].astype(F32), cd, hd, small
    )
    both, shard0 = tie(both, shard0)
    w_in0 = lax.all_gather(shard0, PLANE)
    groups = to_groups(both, n, "hidden_groups")
    resid0 = to_chunks(groups, z_count, "hidden_chunks").astype(F32)
    inv0, unit = normalize(resid0)
    unit = unit.astype(BF)
    shard1 = weight_shard(shift, 1, input_proj, step_proj, norm_gain[1].astype(F32), cd, hd)
    shard_out0, shard1, shard_out1, unit = tie(shard_out(0), shard1, shard_out(1), unit)
    column0 = lax.all_gather(shard_out0, PLANE)
    w_in1 = lax.all_gather(shard1, PLANE)
    column1 = lax.all_gather(shard_out1, PLANE)
    units0, w_in0 = gather_rows(unit, n, "unit0", w_in0)
    pcs, phs = small_unpack(w_in0[:, d_rows:, :small_lanes])

    items, w_in0 = tie(column_sends(after(column0, *flat_shards(units0))), w_in0)
    parts = moved(items, "dp", "weight_out0")
    _, mixed0, gated0, pre0, ssd0, states0, sums0 = layer0 = mixer_forward(
        shift, units0, w_in0, False, age, pcs[0], phs[0]
    )
    unit_cat0 = layer0[0]
    parts, gated0 = tie(parts, gated0)
    w_out0 = weight_out(parts)
    sent = mm(flat(gated0), w_out0).astype(BF).reshape(n, z_count, q, width_d)
    sent = jnp.concatenate([sent, sums0], axis=-1)
    cot_both = both_cores(after(cotangent, sent), "cot_cores")
    cot_items = sends(cot_both.reshape(n, q, width_d), d, n)
    cot_groups = moved(cot_items, "dp", "cot_groups")
    got, _ = reduce_rows(sent, n, "product0")
    squares = jnp.sum(got[..., width_d:], axis=-1, keepdims=True)
    ginv0 = lax.rsqrt(squares / inner + EPSILON)
    branch0 = got[..., :width_d] * ginv0
    resid1 = resid0 + branch0

    inv1, unit = normalize(resid1)
    unit, *cot_groups = tie(unit.astype(BF), *cot_groups)
    cot_chunks = moved(sends(jnp.stack(cot_groups), z ^ d, z_count), "z", "cot_chunks")
    units1, _ = gather_rows(unit, n, "unit1")
    cot_chunks, units1 = tie(cot_chunks, units1)
    upstream = jnp.stack(cot_chunks)
    items, w_in1 = tie(column_sends(after(column1, *flat_shards(units1))), w_in1)
    parts = moved(items, "dp", "weight_out1")
    unit_cat1, mixed1, gated1, pre1, ssd1, states1, sums1 = mixer_forward(
        shift, units1, w_in1, True, age, pcs[1], phs[1]
    )
    upstream_parts, gated1 = gather_rows(upstream, n, "upstream", gated1)
    parts, gated1 = tie(parts, gated1)
    upstream_all = place(shift, joined(upstream_parts), 0)
    w_out1 = weight_out(parts)
    gg1 = mm_bt(flat(upstream_all), w_out1).reshape(n, z_count, q, cd)
    s1 = jnp.sum(sums1.astype(F32), axis=-1)
    s2 = jnp.sum(gg1 * gated1.astype(F32), axis=-1)
    totals = jnp.stack([s1, s2]).reshape(2, row_len // LANES, LANES)
    bit = 1
    while bit < n:
        with jax.named_scope("totals"):
            totals = totals + swap(totals, "dp", bit, n)
        bit *= 2
    totals = totals.reshape(2, n, z_count, q)
    ginv1 = lax.rsqrt(totals[0] / inner + EPSILON)
    scales = jnp.stack([ginv1, ginv1 * ginv1 * ginv1 * totals[1] / inner], axis=-1)
    relative1 = jnp.stack([pick(gated1, d ^ k) for k in range(n)])
    sent1 = mm(flat(relative1), w_out1).astype(BF).reshape(n, z_count, q, width_d)
    own = pick(ginv1, d)[..., None]

    weighted = (gated1.astype(F32) * ginv1[..., None]).astype(BF)
    d_out1 = mm_at(flat(weighted), flat(upstream_all)).astype(BF)
    items, sent1, gg1 = tie(grad_out_sends(d_out1), sent1, gg1)
    by_rows = moved(items, "dp", "grad_out1")

    def backward1(gg1):
        return mixer_backward(
            shift, gg1, scales, None, w_in1, mixed1, age, pcs[1], phs[1], pre1, ssd1, states1,
            width_d,
        )

    total1, (d_mixed, sent, wide_sums, head_sums) = reduce_rows(
        sent1, n, "product1", (backward1, (gg1,))
    )
    by_rows, sent = tie(by_rows, sent)
    own_out1 = grad_out_owned(by_rows)
    normed_grad, d_in1 = reduce_rows(
        sent, n, "back1", (grad_in, (unit_cat1, d_mixed, wide_sums, head_sums))
    )
    own_in1 = lax.psum_scatter(d_in1, PLANE, scatter_dimension=0, tiled=True)
    back1 = norm_back(upstream.astype(F32), resid1, inv1, normed_grad)

    low = back1.astype(BF).astype(F32)
    mean = jnp.sum(low * branch0, axis=-1, keepdims=True) / inner
    kappa = ginv0 * ginv0 * mean
    high = kappa.astype(BF)
    rest = (kappa - high.astype(F32)).astype(BF)
    payload = jnp.concatenate(
        [(low * ginv0).astype(BF), high, rest, jnp.zeros((z_count, q, LANES - 2), BF)], axis=-1
    )
    hidden_out = (resid1 + after(total1, payload) * own).astype(BF)
    out_chunks = moved([hidden_out[k] for k in range(z_count)], "z", "hidden_out_chunks")
    g_all, _ = gather_rows(payload, n, "branch_grad0")
    out_chunks, g_all = tie(out_chunks, g_all)
    d_out0 = mm_at(flat(gated0), flat(jnp.stack(joined(g_all)))[:, :width_d]).astype(BF)
    items, g_all = tie(grad_out_sends(d_out0), g_all)
    by_rows = moved(items, "dp", "grad_out0")
    d_mixed, sent, wide_sums, head_sums = mixer_backward(
        shift, g_all, None, w_out0, w_in0, mixed0, age, pcs[0], phs[0], pre0, ssd0, states0,
        width_d,
    )
    by_rows, sent = tie(by_rows, sent)
    own_out0 = grad_out_owned(by_rows)
    normed_grad, d_in0 = reduce_rows(
        sent, n, "back0", (grad_in, (unit_cat0, d_mixed, wide_sums, head_sums))
    )
    own_in0 = lax.psum_scatter(d_in0, PLANE, scatter_dimension=0, tiled=True)
    back0 = norm_back(back1, resid0, inv0, normed_grad).astype(BF)
    own_in1, own_out1, back0 = tie(own_in1, own_out1, back0)
    back_chunks = moved([back0[k] for k in range(z_count)], "z", "back_chunks")
    owned1 = owned_parts(own_in1, own_out1, "owned1")
    back_chunks, owned1 = tie(back_chunks, owned1)
    back_groups = from_groups(jnp.stack(back_chunks), n, "back_groups")
    buffers, rest1 = finished_layer(1, owned1, None)
    back_groups, buffers = tie(back_groups, buffers)
    hidden_grad = from_both(back_groups, "back_cores").astype(F32)
    out_groups = from_groups(jnp.stack(after(out_chunks, back_groups)), n, "hidden_out_groups")
    hidden_out = from_both(out_groups, "hidden_out_cores")
    own_in0, own_out0, buffers, out_groups = tie(own_in0, own_out0, buffers, out_groups)
    owned0 = owned_parts(own_in0, own_out0, "owned0")
    buffers, rest0 = finished_layer(0, owned0, buffers)
    stacked = tuple(jnp.stack([first, second]) for first, second in zip(rest0, rest1))
    return (hidden_out, hidden_grad, stacked[0], buffers[0], *stacked[1:], buffers[1])


def solution(mesh):
    n = mesh.shape["dp"]
    z_count = mesh.shape["fsdp"] // 2
    assert n == z_count
    split = Mesh(mesh.devices.reshape(n, z_count, 2), ("dp", "z", "core"))
    fsdp = PLANE
    tokens = P("dp", fsdp, None)
    last = P(None, fsdp)
    weights = (
        last,
        P(None, fsdp, None),
        P(None, None, fsdp),
        P(None, None, fsdp),
        last,
        last,
        last,
        last,
        last,
        P(None, fsdp, None),
    )
    return jax.shard_map(
        partial(on_device, n=n, z_count=z_count),
        mesh=split,
        in_specs=(tokens, P("dp", None)) + weights + (tokens,),
        out_specs=(tokens, tokens) + weights,
        check_vma=False,
    )
```

time: 929 us -> 741 us (0.80)
  waiting for transfers between devices: 374 us -> 276 us
  matrix products: 116 us -> 41.5 us
  local copies, waits for them, and re-layouts: 141 us -> 84.1 us
  Pallas kernels: 103 us -> 146 us
  other arithmetic: 70.4 us -> 56.9 us
  starting transfers between devices: 99.7 us -> 111 us
    reduce_scatter x4, waiting for transfers between devices: 64.9 us -> 0.04 us  [the longest x2 0.02 us: grad_out_owned(): return lax.psum_scatter(rows_all, PLANE, scatter_dimension=0)]
    unnamed x238 -> x198, local copies, waits for them, and re-layouts: 73.1 us -> 22.5 us
    dot_general x10 -> x2, matrix products: 43.3 us -> 6.88 us  [mm(): lax.dot_general(a, b, (((1,), (0,)), ((), ())), preferred_element_type=F32)]
    pallas_call x2 -> x11, Pallas kernels: 30.8 us -> 66.3 us  [the longest x2 40.3 us: mixer_forward(): pl.pallas_call(partial(forward_kernel, count=count, cd=cd, ordered=ordere...]
    dot_general x10 -> x1, matrix products: 39.2 us -> 4.4 us  [mm_bt(): lax.dot_general(a, b, (((1,), (1,)), ((), ())), preferred_element_type=F32)]
    all_gather x8 -> x4, waiting for transfers between devices: 72.5 us -> 41 us  [the longest x1 23.1 us: on_device(): column0 = lax.all_gather(shard_out0, PLANE)]
    ppermute x70 -> x78, starting transfers between devices: 96.5 us -> 109 us  [swap(): return lax.ppermute(value, axis, [(i, i ^ k) for i in range(size)])]
    dynamic_update_slice x16 -> x6, local copies, waits for them, and re-layouts: 13.8 us -> 1.09 us  [the longest x2 0.61 us: small_out(): lax.dynamic_update_slice(jnp.zeros((inner,), F32), wide_sums[6, :cd], (d...]
  transfers between devices with their start and end apart: 87 -> 91, of which waited for: 48 -> 42; matrix products, arithmetic and copies ran while one was open for 27% -> 18% of each run, Pallas kernels for 10% -> 19%
where the time goes in v2:
time: 741 us; the launch traced here: 733 us
  waiting for transfers between devices  276 us (37%)
  Pallas kernels  146 us (20%)
  starting transfers between devices  111 us (15%)
  local copies, waits for them, and re-layouts  84.1 us (11%)
  other arithmetic  56.9 us (8%)
  matrix products  41.5 us (6%)
  between operations  16.4 us (2%)
    ppermute x78, waiting for transfers between devices, swap(): return lax.ppermute(value, axis, [(i, i ^ k) for i in range(size)])  234 us
    ppermute x78, starting transfers between devices, swap(): return lax.ppermute(value, axis, [(i, i ^ k) for i in range(size)])  109 us
    pallas_call x2, Pallas kernels, mixer_backward(): pl.pallas_call(partial(backward_kernel, count=count, cd=cd, own_scales=sc...  80.1 us
    pallas_call x2, Pallas kernels, mixer_forward(): pl.pallas_call(partial(forward_kernel, count=count, cd=cd, ordered=ordere...  40.3 us
    dot_general x4, matrix products, mm_at(): lax.dot_general(a, b, (((0,), (0,)), ((), ())), preferred_element_type=F32)  30.3 us
    all_gather x1, waiting for transfers between devices, on_device(): column0 = lax.all_gather(shard_out0, PLANE)  23.1 us
    unnamed x198, local copies, waits for them, and re-layouts  22.5 us
    all_gather x1, waiting for transfers between devices, on_device(): w_in0 = lax.all_gather(shard0, PLANE)  17.9 us
  transfers between devices with their start and end apart: 91, of which 42 were waited for; matrix products, arithmetic and copies ran while one was open for 18% of the time, Pallas kernels for 19%

profile of v2, /device:TPU:0, one launch (start us, length us, event | category | flops | bytes accessed | tf_op | source)
XLA Modules:
  0.0 732.6 jit_solution(17906467639449002099)
XLA Ops:
  37.2 15.1 %collective-permute-done.4 = bf16[64,1536]{1,0:T(8,128)(2,1)S(1)} collective-permute-done((bf16[64,1536]{1,0:T(8,128)(2,1)S(1)}, bf16[64,1536]{1,0:T(8,128)(2,1)S(1)}, u32[]{:S(2)}, u32[]{:S(2)}) %collective-permute-start.4) | collective-permute-done | bytes 196640 | tf_op jit(solution)/shard_map/hidden_chunks/ppermute | solution.py:706
  68.8 12.6 %collective-permute-done.7.refs_1_ = bf16[4,64,1536]{2,1,0:T(8,128)(2,1)} collective-permute-done((bf16[4,64,1536]{2,1,0:T(8,128)(2,1)S(1)}, bf16[4,64,1536]{2,1,0:T(8,128)(2,1)}, u32[]{:S(2)}, u32[]{:S(2)}) %collective-permute-start.7) | collective-permute-done | bytes 786464 | tf_op jit(solution)/shard_map/unit0/ppermute | solution.py:706
  82.8 17.9 %all-gather.11.cloned.1.call-done = bf16[1664,1920]{1,0:T(8,128)(2,1)} async-done(((bf16[208,1920]{1,0:T(8,128)(2,1)}), bf16[1664,1920]{1,0:T(8,128)(2,1)}) %all-gather.11.cloned.1.call-update) | async-done | bytes 6389776 | tf_op jit(solution)/shard_map/all_gather | solution.py:1022
  109.4 23.1 %all-gather.9.cloned.1.call-done = bf16[768,1536]{1,0:T(8,128)(2,1)} async-done(((bf16[96,1536]{1,0:T(8,128)(2,1)}), bf16[768,1536]{1,0:T(8,128)(2,1)}) %all-gather.9.cloned.1.call-update) | async-done | bytes 2359312 | tf_op jit(solution)/shard_map/all_gather | solution.py:1029
  137.8 20.2 %shard_map.222 = (bf16[4,256,1536]{2,1,0:T(8,128)(2,1)}, f32[4,256,1920]{2,1,0:T(8,128)}, bf16[4,4,64,768]{3,2,1,0:T(8,128)(2,1)}, f32[4,256,1024]{2,1,0:T(8,128...) custom-call(s32[2]{0:T(128)S(1)} %copy-done.14, ...), custom_call_target="tpu_custom_call" | custom-call | flops 20000000000 | bytes 40000000 | tf_op jit(solution)/shard_map/pallas_call | solution.py:427
  170.3 18.0 %collective-permute-done.15 = bf16[2,2,64,1664]{3,2,1,0:T(8,128)(2,1)S(1)} collective-permute-done((bf16[2,2,64,1664]{3,2,1,0:T(8,128)(2,1)S(1)}, bf16[2,2,64,1664]{3,2,1,0:T(8,128)(2,1)S(1)}, u32[]{:S(2)}, u32[]{:S(2)}) %collective-permute-start.15) | collective-permute-done | bytes 852000 | tf_op jit(solution)/shard_map/product0/ppermute | solution.py:706
  195.4 6.6 collective-permute-done.16
  211.3 15.0 %collective-permute-done.26.refs_1_ = bf16[4,64,1536]{2,1,0:T(8,128)(2,1)S(1)} collective-permute-done((bf16[4,64,1536]{2,1,0:T(8,128)(2,1)S(1)}, bf16[4,64,1536]{2,1,0:T(8,128)(2,1)S(1)}, u32[]{:S(2)}, u32[]{:S(2)}) %collective-permute-start.26) | collective-permute-done | bytes 786464 | tf_op jit(solution)/shard_map/unit1/ppermute | solution.py:706
  257.4 20.1 %shard_map.224 = (bf16[4,256,1536]{2,1,0:T(8,128)(2,1)}, f32[4,256,1920]{2,1,0:T(8,128)}, bf16[4,4,64,768]{3,2,1,0:T(8,128)(2,1)}, f32[4,256,1024]{2,1,0:T(8,128...) custom-call(s32[2]{0:T(128)S(1)} %copy-done.14, ...), custom_call_target="tpu_custom_call" | custom-call | flops 20000000000 | bytes 40000000 | tf_op jit(solution)/shard_map/pallas_call | solution.py:427
  323.3 39.0 %product1.1 = (bf16[4,256,1920]{2,1,0:T(8,128)(2,1)}, bf16[4,4,64,1536]{3,2,1,0:T(8,128)(2,1)}, f32[8,1024]{1,0:T(8,128)S(1)}, f32[8,128]{1,0:T(8,128)S(1)}) custom-call(s32[2]{0:T(128)S(1)} %copy-done.14, f32[4,4,64,768]{3,2,1,0:T(8,128)} %get-tuple-element.234.refs_0_, f32[4,4,64,2]{3,2,1,0:T(8,128)S(1)} %pad_maximum_fusion.23.refs_1_, ...), custom_call_target="tpu_custom_call" | custom-call | flops 40000000000 | bytes 50000000 | tf_op jit(solution)/shard_map/product1/pallas_call | solution.py:518
  371.6 11.2 %fusion.1 = bf16[1536,1920]{1,0:T(8,128)(2,1)} fusion(f32[1536,13]{1,0:T(8,128)S(1)} %reshape.546, bf16[4,256,1536]{2,1,0:T(8,128)(2,1)} %get-tuple-element.257, bf16[4,256,1920]{2,1,0:T(8,128)(2,1)} %get-tuple-element.258), kind=kOutput, calls=%fused_computation.3 | convolution fusion | flops 6045696000 | bytes 13056000 | tf_op jit(solution)/shard_map/back1/dot_general | solution.py:33
  412.4 13.8 %collective-permute-done.53.refs_1_ = bf16[4,64,1664]{2,1,0:T(8,128)(2,1)S(1)} collective-permute-done((bf16[4,64,1664]{2,1,0:T(8,128)(2,1)S(1)}, bf16[4,64,1664]{2,1,0:T(8,128)(2,1)S(1)}, u32[]{:S(2)}, u32[]{:S(2)}) %collective-permute-start.53) | collective-permute-done | bytes 852000 | tf_op jit(solution)/shard_map/branch_grad0/ppermute | solution.py:706
  429.2 15.5 %collective-permute-start.50 = (bf16[64,1536]{1,0:T(8,128)(2,1)S(1)}, bf16[64,1536]{1,0:T(8,128)(2,1)S(1)}, u32[]{:S(2)}, u32[]{:S(2)}) collective-permute-start(bf16[64,1536]{1,0:T(8,128)(2,1)S(1)} %get-tuple-element.424), channel_id=1, source_target_pairs={{0,2},{2,0},{4,6},{6,4},{1,3},{3,1},{5,7},{7,5},{8,10},{10,8},{12,... | collective-permute-start | bytes 589832 | tf_op jit(solution)/shard_map/hidden_out_chunks/ppermute | solution.py:706
  447.0 9.3 %collective-permute-done.50 = bf16[64,1536]{1,0:T(8,128)(2,1)S(1)} collective-permute-done((bf16[64,1536]{1,0:T(8,128)(2,1)S(1)}, bf16[64,1536]{1,0:T(8,128)(2,1)S(1)}, u32[]{:S(2)}, u32[]{:S(2)}) %collective-permute-start.50) | collective-permute-done | bytes 196640 | tf_op jit(solution)/shard_map/hidden_out_chunks/ppermute | solution.py:706
  456.3 7.8 %collective-permute-done.51 = bf16[64,1536]{1,0:T(8,128)(2,1)S(1)} collective-permute-done((bf16[64,1536]{1,0:T(8,128)(2,1)S(1)}, bf16[64,1536]{1,0:T(8,128)(2,1)S(1)}, u32[]{:S(2)}, u32[]{:S(2)}) %collective-permute-start.51) | collective-permute-done | bytes 196640 | tf_op jit(solution)/shard_map/hidden_out_chunks/ppermute | solution.py:706
  475.6 41.1 %shard_map.228 = (bf16[4,256,1920]{2,1,0:T(8,128)(2,1)}, bf16[4,4,64,1536]{3,2,1,0:T(8,128)(2,1)}, f32[8,1024]{1,0:T(8,128)S(1)}, f32[8,128]{1,0:T(8,128)S(1)}) custom-call(s32[2]{0:T(128)S(1)} %copy-done.14, bf16[4,64,1664]{2,1,0:T(8,128)(2,1)} %copy-done.39, bf16[4,64,1664]{2,1,0:T(8,128)(2,1)} %copy-done.43, bf16[4,64,1664]{2,1,0:T(8,128)(2,1)} %copy-done.44, ...), custom_call_target="tpu_custom_call" | custom-call | flops 40000000000 | bytes 50000000 | tf_op jit(solution)/shard_map/pallas_call | solution.py:518
  527.0 11.4 %fusion = bf16[1536,1920]{1,0:T(8,128)(2,1)} fusion(f32[1536,13]{1,0:T(8,128)S(1)} %reshape.555, bf16[4,256,1536]{2,1,0:T(8,128)(2,1)} %get-tuple-element.299, bf16[4,256,1920]{2,1,0:T(8,128)(2,1)} %get-tuple-element.300), kind=kOutput, calls=%fused_computation.1 | convolution fusion | flops 6045696000 | bytes 13056000 | tf_op jit(solution)/shard_map/back0/dot_general | solution.py:33
  544.9 7.4 %collective-permute-done.62 = bf16[2,64,1536]{2,1,0:T(8,128)(2,1)S(1)} collective-permute-done((bf16[2,64,1536]{2,1,0:T(8,128)(2,1)S(1)}, bf16[2,64,1536]{2,1,0:T(8,128)(2,1)S(1)}, u32[]{:S(2)}, u32[]{:S(2)}) %collective-permute-start.62) | collective-permute-done | bytes 393248 | tf_op jit(solution)/shard_map/back0/ppermute | solution.py:706
  562.0 18.6 %collective-permute-done.67.refs_1_ = bf16[288,1920]{1,0:T(8,128)(2,1)S(1)} collective-permute-done((bf16[288,1920]{1,0:T(8,128)(2,1)S(1)}, bf16[288,1920]{1,0:T(8,128)(2,1)S(1)}, u32[]{:S(2)}, u32[]{:S(2)}) %collective-permute-start.67) | collective-permute-done | bytes 1105952 | tf_op jit(solution)/shard_map/owned1/ppermute | solution.py:706
  590.2 7.0 collective-permute-start.64
  611.0 6.7 collective-permute-done.66
  660.7 20.1 %collective-permute-done.79.refs_1_ = bf16[288,1920]{1,0:T(8,128)(2,1)S(1)} collective-permute-done((bf16[288,1920]{1,0:T(8,128)(2,1)S(1)}, bf16[288,1920]{1,0:T(8,128)(2,1)S(1)}, u32[]{:S(2)}, u32[]{:S(2)}) %collective-permute-start.79) | collective-permute-done | bytes 1105952 | tf_op jit(solution)/shard_map/owned0/ppermute | solution.py:706
  687.0 9.2 %collective-permute-done.81 = bf16[144,1920]{1,0:T(8,128)(2,1)} collective-permute-done((bf16[144,1920]{1,0:T(8,128)(2,1)}, bf16[144,1920]{1,0:T(8,128)(2,1)}, u32[]{:S(2)}, u32[]{:S(2)}) %collective-permute-start.81) | collective-permute-done | bytes 552992 | tf_op jit(solution)/shard_map/owned0/ppermute | solution.py:706
  710.0 6.2 shard_map.231
  (647 shorter events, 343.3 us)
Async XLA Ops:
  7.2 93.5 %all-gather.11.cloned.1.call-start = ((), (), s32[]{:S(2)}) async-start(), calls=%async_computation.9 | async-start | bytes 7188480 | tf_op jit(solution)/shard_map/all_gather | solution.py:1022
  16.0 116.4 %all-gather.9.cloned.1.call-start = ((), (), s32[]{:S(2)}) async-start(), calls=%async_computation.8 | async-start | bytes 2654208 | tf_op jit(solution)/shard_map/all_gather | solution.py:1029
  62.0 185.3 %all-gather.13.cloned.1.call-start = ((), (), s32[]{:S(2)}) async-start(), calls=%async_computation.10 | async-start | bytes 2654208 | tf_op jit(solution)/shard_map/all_gather | solution.py:1031
  62.7 187.4 %all-gather.15.cloned.1.call-start = ((), (), s32[]{:S(2)}) async-start(), calls=%async_computation.11 | async-start | bytes 6635520 | tf_op jit(solution)/shard_map/all_gather | solution.py:1030
  67.2 103.0 %collective-permute-start.19 = (bf16[128,1536]{1,0:T(8,128)(2,1)}, bf16[128,1536]{1,0:T(8,128)(2,1)S(1)}, u32[]{:S(2)}, u32[]{:S(2)}) collective-permute-start(bf16[128,1536]{1,0:T(8,128)(2,1)} %dynamic-slice_bitcast_fusion.16), channel_id=1, source_target_pairs={{0,1},{1,0},{2,3},{3,2},{4,5},{5,4},{6,7},{7,6},{8,9},{9,8},{10,11... | collective-permute-start | bytes 1179656 | tf_op jit(solution)/shard_map/cot_cores/ppermute | solution.py:787
  68.8 488.6 %reduce-scatter.7.cloned.1.call-start = ((), (), s32[]{:S(2)}) async-start(), calls=%async_computation.5 | async-start | bytes 2654208 | tf_op jit(solution)/shard_map/reduce_scatter | solution.py:921
  245.3 32.1 %collective-permute-start.33 = (bf16[4,64,1536]{2,1,0:T(8,128)(2,1)S(1)}, bf16[4,64,1536]{2,1,0:T(8,128)(2,1)S(1)}, u32[]{:S(2)}, u32[]{:S(2)}) collective-permute-start(bf16[4,64,1536]{2,1,0:T(8,128)(2,1)S(1)} %pad_maximum_fusion.13.refs_0_), channel_id=1, source_target_pairs={{0,8},{8,0},{16,24},{24,16},{1,9},{9,1},{17,25},{25,17},{2,10},{10... | collective-permute-start | bytes 2359304 | tf_op jit(solution)/shard_map/upstream/ppermute | solution.py:706
  246.6 30.8 %collective-permute-start.34 = (bf16[4,64,1536]{2,1,0:T(8,128)(2,1)S(1)}, bf16[4,64,1536]{2,1,0:T(8,128)(2,1)S(1)}, u32[]{:S(2)}, u32[]{:S(2)}) collective-permute-start(bf16[4,64,1536]{2,1,0:T(8,128)(2,1)S(1)} %pad_maximum_fusion.13.refs_0_), channel_id=1, source_target_pairs={{0,16},{8,24},{16,0},{24,8},{1,17},{9,25},{17,1},{25,9},{2,18},{10... | collective-permute-start | bytes 2359304 | tf_op jit(solution)/shard_map/upstream/ppermute | solution.py:706
  250.1 34.6 %collective-permute-start.30 = (bf16[2,96,1536]{2,1,0:T(8,128)(2,1)}, bf16[2,96,1536]{2,1,0:T(8,128)(2,1)S(1)}, u32[]{:S(2)}, u32[]{:S(2)}) collective-permute-start(bf16[2,96,1536]{2,1,0:T(8,128)(2,1)} %get-tuple-element.212), channel_id=1, source_target_pairs={{0,8},{8,0},{16,24},{24,16},{1,9},{9,1},{17,25},{25,17},{2,10},{10... | collective-permute-start | bytes 1769480 | tf_op jit(solution)/shard_map/weight_out1/ppermute | solution.py:706
  250.9 37.2 %collective-permute-start.31 = (bf16[2,96,1536]{2,1,0:T(8,128)(2,1)}, bf16[2,96,1536]{2,1,0:T(8,128)(2,1)}, u32[]{:S(2)}, u32[]{:S(2)}) collective-permute-start(bf16[2,96,1536]{2,1,0:T(8,128)(2,1)} %get-tuple-element.213), channel_id=1, source_target_pairs={{0,16},{8,24},{16,0},{24,8},{1,17},{9,25},{17,1},{25,9},{2,18},{10... | collective-permute-start | bytes 1769480 | tf_op jit(solution)/shard_map/weight_out1/ppermute | solution.py:706
  252.3 35.8 %collective-permute-start.32 = (bf16[2,96,1536]{2,1,0:T(8,128)(2,1)}, bf16[2,96,1536]{2,1,0:T(8,128)(2,1)}, u32[]{:S(2)}, u32[]{:S(2)}) collective-permute-start(bf16[2,96,1536]{2,1,0:T(8,128)(2,1)} %get-tuple-element.214), channel_id=1, source_target_pairs={{0,24},{8,16},{16,8},{24,0},{1,25},{9,17},{17,9},{25,1},{2,26},{10... | collective-permute-start | bytes 1769480 | tf_op jit(solution)/shard_map/weight_out1/ppermute | solution.py:706
  317.3 45.0 %collective-permute-start.39 = (bf16[2,2,64,1536]{3,2,1,0:T(8,128)(2,1)S(1)}, bf16[2,2,64,1536]{3,2,1,0:T(8,128)(2,1)S(1)}, u32[]{:S(2)}, u32[]{:S(2)}) collective-permute-start(bf16[2,2,64,1536]{3,2,1,0:T(8,128)(2,1)S(1)} %pad_maximum_fusion.15), channel_id=1, source_target_pairs={{0,8},{8,0},{16,24},{24,16},{1,9},{9,1},{17,25},{25,17},{2,10},{10... | collective-permute-start | bytes 2359304 | tf_op jit(solution)/shard_map/product1/ppermute | solution.py:706
  318.1 44.2 %collective-permute-start.40 = (bf16[2,2,64,1536]{3,2,1,0:T(8,128)(2,1)S(1)}, bf16[2,2,64,1536]{3,2,1,0:T(8,128)(2,1)S(1)}, u32[]{:S(2)}, u32[]{:S(2)}) collective-permute-start(bf16[2,2,64,1536]{3,2,1,0:T(8,128)(2,1)S(1)} %copy-done.51), channel_id=1, source_target_pairs={{0,16},{8,24},{16,0},{24,8},{1,17},{9,25},{17,1},{25,9},{2,18},{10... | collective-permute-start | bytes 2359304 | tf_op jit(solution)/shard_map/product1/ppermute | solution.py:706
  319.8 42.6 %collective-permute-start.43 = (bf16[2,96,1536]{2,1,0:T(8,128)(2,1)S(1)}, bf16[2,96,1536]{2,1,0:T(8,128)(2,1)S(1)}, u32[]{:S(2)}, u32[]{:S(2)}) collective-permute-start(bf16[2,96,1536]{2,1,0:T(8,128)(2,1)S(1)} %copy-done.69), channel_id=1, source_target_pairs={{0,8},{8,0},{16,24},{24,16},{1,9},{9,1},{17,25},{25,17},{2,10},{10... | collective-permute-start | bytes 1769480 | tf_op jit(solution)/shard_map/grad_out1/ppermute | solution.py:706
  321.1 41.3 %collective-permute-start.44 = (bf16[2,96,1536]{2,1,0:T(8,128)(2,1)S(1)}, bf16[2,96,1536]{2,1,0:T(8,128)(2,1)S(1)}, u32[]{:S(2)}, u32[]{:S(2)}) collective-permute-start(bf16[2,96,1536]{2,1,0:T(8,128)(2,1)S(1)} %copy-done.68), channel_id=1, source_target_pairs={{0,16},{8,24},{16,0},{24,8},{1,17},{9,25},{17,1},{25,9},{2,18},{10... | collective-permute-start | bytes 1769480 | tf_op jit(solution)/shard_map/grad_out1/ppermute | solution.py:706
  321.4 41.8 %collective-permute-start.45 = (bf16[2,96,1536]{2,1,0:T(8,128)(2,1)S(1)}, bf16[2,96,1536]{2,1,0:T(8,128)(2,1)S(1)}, u32[]{:S(2)}, u32[]{:S(2)}) collective-permute-start(bf16[2,96,1536]{2,1,0:T(8,128)(2,1)S(1)} %copy-done.67), channel_id=1, source_target_pairs={{0,24},{8,16},{16,8},{24,0},{1,25},{9,17},{17,9},{25,1},{2,26},{10... | collective-permute-start | bytes 1769480 | tf_op jit(solution)/shard_map/grad_out1/ppermute | solution.py:706
  365.4 192.1 %reduce-scatter.5.cloned.1.call-start = ((), (), s32[]{:S(2)}) async-start(), calls=%async_computation.4 | async-start | bytes 6635520 | tf_op jit(solution)/shard_map/reduce_scatter | solution.py:1104
  382.9 269.8 %reduce-scatter.11.cloned.1.call-start = ((), (), s32[]{:S(2)}) async-start(), calls=%async_computation.7 | async-start | bytes 2654208 | tf_op jit(solution)/shard_map/reduce_scatter | solution.py:921
  426.2 41.1 %collective-permute-start.55 = (bf16[2,64,1664]{2,1,0:T(8,128)(2,1)S(1)}, bf16[2,64,1664]{2,1,0:T(8,128)(2,1)S(1)}, u32[]{:S(2)}, u32[]{:S(2)}) collective-permute-start(bf16[2,64,1664]{2,1,0:T(8,128)(2,1)S(1)} %slice.626), channel_id=1, source_target_pairs={{0,16},{8,24},{16,0},{24,8},{1,17},{9,25},{17,1},{25,9},{2,18},{10... | collective-permute-start | bytes 1277960 | tf_op jit(solution)/shard_map/branch_grad0/ppermute | solution.py:706
  427.1 40.2 %collective-permute-start.56 = (bf16[2,64,1664]{2,1,0:T(8,128)(2,1)S(1)}, bf16[2,64,1664]{2,1,0:T(8,128)(2,1)S(1)}, u32[]{:S(2)}, u32[]{:S(2)}) collective-permute-start(bf16[2,64,1664]{2,1,0:T(8,128)(2,1)S(1)} %slice.627), channel_id=1, source_target_pairs={{0,8},{8,0},{16,24},{24,16},{1,9},{9,1},{17,25},{25,17},{2,10},{10... | collective-permute-start | bytes 1277960 | tf_op jit(solution)/shard_map/branch_grad0/ppermute | solution.py:706
  472.0 44.6 %collective-permute-start.57 = (bf16[2,96,1536]{2,1,0:T(8,128)(2,1)S(1)}, bf16[2,96,1536]{2,1,0:T(8,128)(2,1)S(1)}, u32[]{:S(2)}, u32[]{:S(2)}) collective-permute-start(bf16[2,96,1536]{2,1,0:T(8,128)(2,1)S(1)} %get-tuple-element.279), channel_id=1, source_target_pairs={{0,8},{8,0},{16,24},{24,16},{1,9},{9,1},{17,25},{25,17},{2,10},{10... | collective-permute-start | bytes 1769480 | tf_op jit(solution)/shard_map/grad_out0/ppermute | solution.py:706
  473.6 43.1 %collective-permute-start.58 = (bf16[2,96,1536]{2,1,0:T(8,128)(2,1)S(1)}, bf16[2,96,1536]{2,1,0:T(8,128)(2,1)S(1)}, u32[]{:S(2)}, u32[]{:S(2)}) collective-permute-start(bf16[2,96,1536]{2,1,0:T(8,128)(2,1)S(1)} %get-tuple-element.280), channel_id=1, source_target_pairs={{0,16},{8,24},{16,0},{24,8},{1,17},{9,25},{17,1},{25,9},{2,18},{10... | collective-permute-start | bytes 1769480 | tf_op jit(solution)/shard_map/grad_out0/ppermute | solution.py:706
  473.8 42.8 %collective-permute-start.59 = (bf16[2,96,1536]{2,1,0:T(8,128)(2,1)S(1)}, bf16[2,96,1536]{2,1,0:T(8,128)(2,1)S(1)}, u32[]{:S(2)}, u32[]{:S(2)}) collective-permute-start(bf16[2,96,1536]{2,1,0:T(8,128)(2,1)S(1)} %get-tuple-element.281), channel_id=1, source_target_pairs={{0,24},{8,16},{16,8},{24,0},{1,25},{9,17},{17,9},{25,1},{2,26},{10... | collective-permute-start | bytes 1769480 | tf_op jit(solution)/shard_map/grad_out0/ppermute | solution.py:706
  518.8 133.9 %reduce-scatter.9.cloned.1.call-start = ((), (), s32[]{:S(2)}) async-start(), calls=%async_computation.6 | async-start | bytes 6635520 | tf_op jit(solution)/shard_map/reduce_scatter | solution.py:1131
  (165 other events, 2413.7 us)
Sparse Core Ops, SparseCore 0:
  16.2 84.4 all-gather.10
  102.3 30.0 all-gather.8
  134.1 30.7 all-gather.12
  166.4 60.6 all-gather.14
  365.5 41.7 reduce-scatter.6
  409.5 78.0 reduce-scatter.4
  518.9 39.4 reduce-scatter.10
  560.8 77.8 reduce-scatter.8

commit v3 on v2

--- a/solution.py
+++ b/solution.py
@@ -118,6 +118,45 @@
     return [one, one, one, low, high]
 
 
+QUARTERS = (((1, 3), (0, 2)), ((2, 3), (0, 1)))
+
+
+def sum_shapes(count, blocks, q, width):
+    if count != 4:
+        return [jax.ShapeDtypeStruct((count, blocks, q, width), BF)]
+    return [jax.ShapeDtypeStruct((2, blocks // 2, q, width), BF)] * 4
+
+
+def sum_specs(count, blocks, q, width, step):
+    if count != 4:
+        return [pl.BlockSpec((count, 1, q, width), lambda i, s: (0, step(i) ^ s[1], 0, 0))]
+    half = blocks // 2
+
+    def lower(i, s):
+        start = jnp.where(s[1] < half, 0, half)
+        return (0, jnp.clip(step(i), start, start + half - 1) ^ s[1], 0, 0)
+
+    def upper(i, s):
+        start = jnp.where(s[1] < half, half, 0)
+        return (0, (jnp.clip(step(i), start, start + half - 1) ^ s[1]) - half, 0, 0)
+
+    return [pl.BlockSpec((2, 1, q, width), which) for which in (lower, lower, upper, upper)]
+
+
+def sum_store(refs, buf, shift, at, blocks, count):
+    if count != 4:
+        for k in range(count):
+            refs[0][k, 0] = buf[jnp.bitwise_xor(shift, k)]
+        return
+    for upper in range(2):
+
+        @pl.when((at >= blocks // 2) == (upper == 1))
+        def _():
+            for which in range(2):
+                for i, k in enumerate(QUARTERS[upper][which]):
+                    refs[2 * upper + which][i, 0] = buf[jnp.bitwise_xor(shift, k)]
+
+
 def conv_sum(ext, age, weights, bias_row, rows):
     out = jnp.zeros((rows, ext.shape[1]), F32) + bias_row
     for j in range(4):
@@ -131,8 +170,14 @@
 def forward_kernel(shift_ref, *refs, count, cd, ordered):
     unit_refs, refs = shard_refs(refs, count)
     weight_ref, age_ref, pc_ref, ph_ref, refs = *refs[:4], refs[4:]
-    unit_ref, mixed_ref, gated_ref, pre_ref, ssd_ref, states_ref, sums_ref, refs = *refs[:7], refs[7:]
-    unit_buf, gated_buf, ext, state, sums_buf = refs
+    if not ordered:
+        weight_out_ref, refs = refs[0], refs[1:]
+    unit_ref, mixed_ref, gated_ref, pre_ref, ssd_ref, states_ref, refs = *refs[:6], refs[6:]
+    if ordered:
+        sums_ref, unit_buf, ext, state = refs
+    else:
+        used = 4 if count == 4 else 1
+        sum_refs, (unit_buf, ext, state, gated_buf, sent_buf) = refs[:used], refs[used:]
     grid_at = pl.program_id(0)
     blocks = pl.num_programs(0)
     shift = shift_ref[0]
@@ -216,10 +261,14 @@
         sums_ref[:, 0] = sums
         return
     gated_buf[...] = gated
-    sums_buf[...] = sums
     for k in range(count):
         gated_ref[k, 0] = gated_buf[jnp.bitwise_xor(shift, k)]
-        sums_ref[k, 0] = sums_buf[jnp.bitwise_xor(shift, k)]
+    model = weight_out_ref.shape[1]
+    product = mm(gated.reshape(rows, cd), weight_out_ref[...]).astype(BF)
+    sent_buf[:, :, :model] = product.reshape(count, q, model)
+    sent_buf[:, :, model:] = sums
+    at = jnp.bitwise_xor(grid_at, shift_ref[1])
+    sum_store(sum_refs, sent_buf, shift, at, blocks, count)
 
 
 def backward_kernel(shift_ref, *refs, count, cd, own_scales):
@@ -232,8 +281,9 @@
         grad_refs, refs = shard_refs(refs, count)
         weight_out_ref, refs = refs[0], refs[1:]
     weight_ref, mixed_ref, age_ref, pc_ref, ph_ref, pre_ref, ssd_ref, states_ref = refs[:8]
-    mixed_grad_ref, unit_grad_ref, wide_sums, head_sums = refs[8:12]
-    out_buf, ext, adjoint = refs[12:15]
+    used = 4 if count == 4 else 1
+    mixed_grad_ref, wide_sums, head_sums, sum_refs = *refs[8:11], refs[11 : 11 + used]
+    out_buf, ext, adjoint, sent_buf = refs[11 + used : 15 + used]
     conv_ch = cd + 2 * STATE
     rows = mixed_ref.shape[1]
     q = rows // count
@@ -261,7 +311,7 @@
         scaled = grad_ref[:, 0].reshape(rows, cd) * extra[:, 0:1]
         mean_term = extra[:, 1:2]
     else:
-        grad_buf = refs[15]
+        grad_buf = refs[15 + used]
         at = jnp.bitwise_xor(blocks - 1 - grid_at, shift_ref[1])
         to_order(grad_refs, grad_buf, shift, count, (at, blocks))
         grad = grad_buf[...].reshape(rows, grad_buf.shape[2])
@@ -392,17 +442,16 @@
     mixed_grad_ref[0] = out_buf[...]
     weight = weight_ref[...].reshape(-1, weight_ref.shape[2])
     unit_grad = mm_bt(out_buf[...], weight).astype(BF)
-    unit_grad_buf = refs[-1]
-    unit_grad_buf[...] = unit_grad.reshape(unit_grad_buf.shape)
-    for k in range(count):
-        unit_grad_ref[k, 0] = unit_grad_buf[jnp.bitwise_xor(shift, k)]
+    sent_buf[...] = unit_grad.reshape(sent_buf.shape)
+    at = jnp.bitwise_xor(blocks - 1 - grid_at, shift_ref[1])
+    sum_store(sum_refs, sent_buf, shift, at, blocks, count)
 
 
 def whole(shape):
     return pl.BlockSpec(shape, lambda *_: (0,) * len(shape), pipeline_mode=pl.Buffered(1))
 
 
-def mixer_forward(shift, units, weight, ordered, age, pc, ph):
+def mixer_forward(shift, units, weight, weight_out, age, pc, ph):
     count = len(units)
     blocks, q, model = units[0].shape
     width = weight.shape[2]
@@ -417,6 +466,11 @@
         whole(pc.shape),
         whole(ph.shape),
     ]
+    ordered = weight_out is None
+    args = flat_shards(units) + [weight, age, pc, ph]
+    if not ordered:
+        in_specs.append(whole(weight_out.shape))
+        args.append(weight_out)
 
     def in_order(*shape):
         return pl.BlockSpec((1,) + shape, lambda i, s: (i,) + (0,) * len(shape))
@@ -424,6 +478,21 @@
     def relative(last):
         return pl.BlockSpec((count, 1, q, last), lambda i, s: (0, i ^ s[1], 0, 0))
 
+    scratch = [
+        pltpu.VMEM((count, q, model), BF),
+        pltpu.VMEM((rows + HALO, conv_ch), F32),
+        pltpu.VMEM((STATE, cd), F32),
+    ]
+    if ordered:
+        last_shapes = [jax.ShapeDtypeStruct((count, blocks, q, LANES), BF)]
+        last_specs = [relative(LANES)]
+    else:
+        last_shapes = sum_shapes(count, blocks, q, model + LANES)
+        last_specs = sum_specs(count, blocks, q, model + LANES, lambda i: i)
+        scratch += [
+            pltpu.VMEM((count, q, cd), BF),
+            pltpu.VMEM((count, q, model + LANES), BF),
+        ]
     return pl.pallas_call(
         partial(forward_kernel, count=count, cd=cd, ordered=ordered),
         out_shape=[
@@ -433,8 +502,8 @@
             jax.ShapeDtypeStruct((blocks, rows, conv_ch), F32),
             jax.ShapeDtypeStruct((blocks, rows, cd), F32),
             jax.ShapeDtypeStruct((blocks, chunks, STATE, cd), BF),
-            jax.ShapeDtypeStruct((count, blocks, q, LANES), BF),
-        ],
+        ]
+        + last_shapes,
         grid_spec=pltpu.PrefetchScalarGridSpec(
             num_scalar_prefetch=1,
             grid=(blocks,),
@@ -446,21 +515,13 @@
                 in_order(rows, conv_ch),
                 in_order(rows, cd),
                 in_order(chunks, STATE, cd),
-                relative(LANES),
-            ],
-            scratch_shapes=[
-                pltpu.VMEM((count, q, model), BF),
-                pltpu.VMEM((count, q, cd), BF),
-                pltpu.VMEM((rows + HALO, conv_ch), F32),
-                pltpu.VMEM((STATE, cd), F32),
-                pltpu.VMEM((count, q, LANES), BF),
-            ],
+            ]
+            + last_specs,
+            scratch_shapes=scratch,
         ),
         compiler_params=pltpu.CompilerParams(vmem_limit_bytes=52 * 2**20),
-        cost_estimate=pl.CostEstimate(
-            flops=2 * 10**10, bytes_accessed=4 * 10**7, transcendentals=10**6
-        ),
-    )(shift, *flat_shards(units), weight, age, pc, ph)
+        cost_estimate=pl.CostEstimate(flops=10**6, bytes_accessed=10**5, transcendentals=0),
+    )(shift, *args)
 
 
 def flat_shards(shards):
@@ -511,28 +572,28 @@
         pltpu.VMEM((rows, width), BF),
         pltpu.VMEM((rows + HALO, conv_ch), F32),
         pltpu.VMEM((STATE, cd), F32),
+        pltpu.VMEM((count, q, model), BF),
     ]
     if scales is None:
         scratch.append(pltpu.VMEM((count, q, grad_width), BF))
-    scratch.append(pltpu.VMEM((count, q, model), BF))
     return pl.pallas_call(
         partial(backward_kernel, count=count, cd=cd, own_scales=scales is not None),
         out_shape=[
             jax.ShapeDtypeStruct((blocks, rows, width), BF),
-            jax.ShapeDtypeStruct((count, blocks, q, model), BF),
             jax.ShapeDtypeStruct((8, conv_ch), F32),
             jax.ShapeDtypeStruct((8, LANES), F32),
-        ],
+        ]
+        + sum_shapes(count, blocks, q, model),
         grid_spec=pltpu.PrefetchScalarGridSpec(
             num_scalar_prefetch=1,
             grid=(blocks,),
             in_specs=in_specs,
             out_specs=[
                 in_order(rows, width),
-                pl.BlockSpec((count, 1, q, model), lambda i, s: (0, (top - i) ^ s[1], 0, 0)),
                 pl.BlockSpec((8, conv_ch), lambda i, s: (0, 0)),
                 pl.BlockSpec((8, LANES), lambda i, s: (0, 0)),
-            ],
+            ]
+            + sum_specs(count, blocks, q, model, lambda i: top - i),
             scratch_shapes=scratch,
         ),
         compiler_params=pltpu.CompilerParams(vmem_limit_bytes=52 * 2**20),
@@ -601,7 +662,8 @@
             out_specs=pl.BlockSpec((full, width), lambda i, s: (0, 0)),
             scratch_shapes=[pltpu.VMEM((SMALL_ROWS, width), F32)] if small else [],
         ),
-        cost_estimate=pl.CostEstimate(flops=10**6, bytes_accessed=2 * 10**6, transcendentals=0),
+        compiler_params=pltpu.CompilerParams(vmem_limit_bytes=40 * 2**20),
+        cost_estimate=pl.CostEstimate(flops=10**6, bytes_accessed=10**5, transcendentals=0),
     )(shift, input_proj, input_proj, input_proj, step_proj, gain[:, None], *small)
 
 
@@ -625,15 +687,157 @@
             out_specs=whole(full),
         ),
         compiler_params=pltpu.CompilerParams(vmem_limit_bytes=40 * 2**20),
-        cost_estimate=pl.CostEstimate(flops=0, bytes_accessed=5 * 10**6, transcendentals=0),
+        cost_estimate=pl.CostEstimate(flops=10**6, bytes_accessed=10**5, transcendentals=0),
     )(shift, *parts)
 
 
-def finish_kernel(shift_ref, *refs, count, cd, inner, rows, out_part, apart):
+def term_specs(terms, q):
+    specs, kinds = [], []
+    for array, kind in terms:
+        lead = array.ndim - 3
+        blocks, width = array.shape[lead], array.shape[-1]
+        half = blocks // 2 if kind == "all" else blocks
+
+        def place(i, lead=lead, kind=kind):
+            return (0,) * lead + (i if kind == "all" else 0, 0, 0)
+
+        specs.append(pl.BlockSpec((1,) * lead + (half, q, width), place))
+        kinds.append(kind)
+    return specs, kinds
+
+
+def add_terms(refs, kinds, buf):
+    at = pl.program_id(0)
+
+    def total(kind):
+        out = None
+        for ref, own in zip(refs, kinds):
+            if own == kind:
+                part = ref[...].reshape(buf.shape).astype(F32)
+                out = part if out is None else out + part
+        return out
+
+    if "all" in kinds:
+        buf[...] = total("all")
+        return
+
+    @pl.when(at == 0)
+    def _():
+        buf[...] = total("lower")
+
+    @pl.when(at == 1)
+    def _():
+        buf[...] = total("upper")
+
+
+def settle_forward_kernel(*refs, kinds, inner):
+    term_refs, refs = refs[: len(kinds)], refs[len(kinds) :]
+    resid_ref, out_ref, branch_ref, ginv_ref, inv_ref, unit_ref, buf = refs
+    add_terms(term_refs, kinds, buf)
+    model = resid_ref.shape[2]
+    squares = jnp.sum(buf[:, model:], axis=1, keepdims=True)
+    ginv = lax.rsqrt(squares / inner + EPSILON)
+    branch = buf[:, :model] * ginv
+    resid = resid_ref[...].reshape(branch.shape) + branch
+    inv = lax.rsqrt(jnp.mean(resid * resid, axis=1, keepdims=True) + EPSILON)
+    out_ref[...] = resid.reshape(out_ref.shape)
+    branch_ref[...] = branch.reshape(branch_ref.shape)
+    ginv_ref[...] = ginv.reshape(ginv_ref.shape)
+    inv_ref[...] = inv.reshape(inv_ref.shape)
+    unit_ref[...] = (resid * inv).astype(BF).reshape(unit_ref.shape)
+
+
+def settle_forward(terms, resid, inner):
+    blocks, q, model = resid.shape
+    specs, kinds = term_specs(terms, q)
+    half = blocks // 2
+    wide = pl.BlockSpec((half, q, model), lambda i: (i, 0, 0))
+    thin = pl.BlockSpec((half, q, 1), lambda i: (i, 0, 0))
+    return pl.pallas_call(
+        partial(settle_forward_kernel, kinds=kinds, inner=inner),
+        grid=(2,),
+        out_shape=[
+            jax.ShapeDtypeStruct(resid.shape, F32),
+            jax.ShapeDtypeStruct(resid.shape, F32),
+            jax.ShapeDtypeStruct((blocks, q, 1), F32),
+            jax.ShapeDtypeStruct((blocks, q, 1), F32),
+            jax.ShapeDtypeStruct(resid.shape, BF),
+        ],
+        in_specs=specs + [wide],
+        out_specs=[wide, wide, thin, thin, wide],
+        compiler_params=pltpu.CompilerParams(vmem_limit_bytes=40 * 2**20),
+        scratch_shapes=[pltpu.VMEM((half * q, terms[0][0].shape[-1]), F32)],
+        cost_estimate=pl.CostEstimate(flops=10**6, bytes_accessed=10**5, transcendentals=0),
+    )(*[array for array, _ in terms], resid)
+
+
+def settle_backward_kernel(*refs, kinds, inner, onward):
+    term_refs, refs = refs[: len(kinds)], refs[len(kinds) :]
+    resid_ref, inv_ref, back_ref, refs = refs[0], refs[1], refs[2], refs[3:]
+    buf = refs[-1]
+    add_terms(term_refs, kinds, buf)
+    grad = buf[...]
+    inv = inv_ref[...].reshape(grad.shape[0], 1)
+    u = resid_ref[...].reshape(grad.shape) * inv
+    back = back_ref[...].astype(F32).reshape(grad.shape) + inv * (
+        grad - u * jnp.mean(grad * u, axis=1, keepdims=True)
+    )
+    if not onward:
+        refs[0][...] = back.astype(BF).reshape(refs[0].shape)
+        return
+    branch_ref, ginv_ref, out_ref, payload_ref = refs[:4]
+    out_ref[...] = back.reshape(out_ref.shape)
+    model = back.shape[1]
+    low = back.astype(BF).astype(F32)
+    ginv = ginv_ref[...].reshape(inv.shape)
+    mean = jnp.sum(low * branch_ref[...].reshape(low.shape), axis=1, keepdims=True) / inner
+    kappa = ginv * ginv * mean
+    high = kappa.astype(BF).astype(F32)
+    lane = iota2((back.shape[0], LANES), 1)
+    front = payload_ref.shape[:2]
+    payload_ref[:, :, :model] = (low * ginv).astype(BF).reshape(*front, model)
+    tail = jnp.where(lane == 0, high, jnp.where(lane == 1, kappa - high, 0.0))
+    payload_ref[:, :, model:] = tail.astype(BF).reshape(*front, LANES)
+
+
+def settle_backward(terms, resid, inv, back, inner, branch=None, ginv=None):
+    blocks, q, model = resid.shape
+    specs, kinds = term_specs(terms, q)
+    onward = branch is not None
+    half = blocks // 2
+    wide = pl.BlockSpec((half, q, model), lambda i: (i, 0, 0))
+    thin = pl.BlockSpec((half, q, 1), lambda i: (i, 0, 0))
+    args = [array for array, _ in terms] + [resid, inv, back]
+    in_specs = specs + [wide, thin, wide]
+    if onward:
+        args += [branch, ginv]
+        in_specs += [wide, thin]
+        out_shape = [
+            jax.ShapeDtypeStruct(resid.shape, F32),
+            jax.ShapeDtypeStruct((blocks, q, model + LANES), BF),
+        ]
+        out_specs = [wide, pl.BlockSpec((half, q, model + LANES), lambda i: (i, 0, 0))]
+    else:
+        out_shape = [jax.ShapeDtypeStruct(resid.shape, BF)]
+        out_specs = [wide]
+    limit = 40 if onward else 60
+    return pl.pallas_call(
+        partial(settle_backward_kernel, kinds=kinds, inner=inner, onward=onward),
+        grid=(2,),
+        out_shape=out_shape,
+        in_specs=in_specs,
+        out_specs=out_specs,
+        compiler_params=pltpu.CompilerParams(vmem_limit_bytes=limit * 2**20),
+        scratch_shapes=[pltpu.VMEM((half * q, model), F32)],
+        cost_estimate=pl.CostEstimate(flops=10**6, bytes_accessed=10**5, transcendentals=0),
+    )(*args)
+
+
+def finish_kernel(shift_ref, *refs, count, cd, hd, inner, rows, out_part, apart):
     part_refs, refs = refs[:count], refs[count:]
     own_refs, refs = (refs[:count], refs[count:]) if apart else (None, refs)
-    weight_ref, gain_ref, refs = refs[0], refs[1], refs[2:]
-    grad_ref, out_ref, norm_ref = refs[-3:]
+    weight_ref, step_ref, gain_ref, gain_row_ref = refs[:4]
+    grad_ref, out_ref, steps_ref, norm_ref, norm_row_ref = refs[-5:]
     gain = gain_ref[...]
     norm = jnp.zeros((rows, 1), F32)
 
@@ -645,9 +849,15 @@
         )
 
     rest = jnp.zeros((rows, 2 * STATE), F32)
+    heads = step_ref.shape[1]
+    steps = jnp.zeros((heads, rows), F32)
+    head, lane = iota2((heads, LANES), 0), iota2((heads, LANES), 1)
     for k in range(count):
         j = jnp.bitwise_xor(shift_ref[0], k)
-        part = part_refs[k][:rows, :].astype(F32)
+        part = part_refs[k][:rows, :]
+        chosen = ((head == j * hd + lane) & (lane < hd)).astype(BF)
+        steps = steps + mm_bt(chosen, part[:, 2 * cd + 2 * STATE :])
+        part = part.astype(F32)
         norm = put(pl.multiple_of(j * cd, LANES), part[:, :cd], norm)
         norm = put(pl.multiple_of(inner + j * cd, LANES), part[:, cd : 2 * cd], norm)
         rest = rest + part[:, 2 * cd : 2 * cd + 2 * STATE]
@@ -656,26 +866,32 @@
             :out_part, : out_ref.shape[2]
         ]
     norm_ref[...] = put(2 * inner, rest, norm)
-
-
-def finish(layer, shift, parts, apart, weight, gain, out_part, out_cols, before, cd, inner):
+    norm_row_ref[...] = jnp.sum(steps * step_ref[0].astype(F32), axis=0, keepdims=True)
+    steps_ref[0] = steps * gain_row_ref[...]
+
+
+def finish(layer, shift, parts, apart, weight, step, gain, out_part, out_cols, before, cd, inner):
     count = len(parts)
     layers, rows, columns = weight.shape
+    heads = step.shape[1]
     in_specs = [whole(part.shape) for part in parts + (apart or [])] + [
         pl.BlockSpec((1, rows, columns), lambda i, s: (layer, 0, 0)),
+        pl.BlockSpec((1, heads, rows), lambda i, s: (layer, 0, 0)),
         whole((rows, 1)),
+        whole((1, rows)),
     ]
-    args = parts + (apart or []) + [weight, gain[:, None]]
+    args = parts + (apart or []) + [weight, step, gain[:, None], gain[None, :]]
     aliases = {}
     if before is not None:
-        aliases = {len(args) + 1: 0, len(args) + 2: 1}
-        in_specs += [pl.BlockSpec(memory_space=pl.ANY)] * 2
+        aliases = {len(args) + 1 + i: i for i in range(3)}
+        in_specs += [pl.BlockSpec(memory_space=pl.ANY)] * 3
         args += list(before)
     return pl.pallas_call(
         partial(
             finish_kernel,
             count=count,
             cd=cd,
+            hd=heads // count,
             inner=inner,
             rows=rows,
             out_part=out_part,
@@ -684,7 +900,9 @@
         out_shape=[
             jax.ShapeDtypeStruct((layers, rows, columns), F32),
             jax.ShapeDtypeStruct((layers, count * out_part, out_cols), F32),
+            jax.ShapeDtypeStruct((layers, heads, rows), F32),
             jax.ShapeDtypeStruct((rows, 1), F32),
+            jax.ShapeDtypeStruct((1, rows), F32),
         ],
         grid_spec=pltpu.PrefetchScalarGridSpec(
             num_scalar_prefetch=1,
@@ -693,12 +911,14 @@
             out_specs=[
                 pl.BlockSpec((1, rows, columns), lambda i, s: (layer, 0, 0)),
                 pl.BlockSpec((1, count * out_part, out_cols), lambda i, s: (layer, 0, 0)),
+                pl.BlockSpec((1, heads, rows), lambda i, s: (layer, 0, 0)),
                 whole((rows, 1)),
+                whole((1, rows)),
             ],
         ),
         input_output_aliases=aliases,
-        compiler_params=pltpu.CompilerParams(vmem_limit_bytes=48 * 2**20),
-        cost_estimate=pl.CostEstimate(flops=10**7, bytes_accessed=2 * 10**7, transcendentals=0),
+        compiler_params=pltpu.CompilerParams(vmem_limit_bytes=40 * 2**20),
+        cost_estimate=pl.CostEstimate(flops=10**6, bytes_accessed=10**5, transcendentals=0),
     )(shift, *args)
 
 
@@ -728,20 +948,28 @@
         return [items[0]] + [swap(items[k], axis, k, size) for k in range(1, size)]
 
 
-def gather_rows(shard, n, what, arrived=None):
+def gather_first(shard, n, what):
     if n != 4:
-        everything = lax.all_gather(shard, "dp")
+        return [lax.all_gather(shard, "dp")]
+    with jax.named_scope(what):
+        return [shard, swap(shard, "dp", 1, n), swap(shard, "dp", 2, n)]
+
+
+def gather_second(state, n, what):
+    if n != 4:
         mine = lax.axis_index("dp")
-        return [pick(everything, mine ^ k) for k in range(n)], arrived
+        return [pick(state[0], mine ^ k) for k in range(n)]
+    shard, first, second = state
     half = shard.shape[0] // 2
     with jax.named_scope(what):
-        first = swap(shard, "dp", 1, n)
-        second = swap(shard, "dp", 2, n)
-        if arrived is not None:
-            first, second, arrived = tie(first, second, arrived)
         low = swap(first[:half], "dp", 2, n)
         high = swap(second[half:], "dp", 1, n)
-    return [shard, first, second, (low, high)], arrived
+    return [shard, first, second, (low, high)]
+
+
+def tie_terms(terms, rest):
+    arrays, rest = tie([array for array, _ in terms], rest)
+    return [(array, kind) for array, (_, kind) in zip(arrays, terms)], rest
 
 
 def joined(shards):
@@ -750,34 +978,48 @@
     ]
 
 
-def reduce_rows(parts, n, what, during=None):
-    with jax.named_scope(what):
-        return reduce_parts(parts, n, during)
-
-
-def reduce_parts(parts, n, during=None):
+def reduce_first(parts, n, what):
     if n != 4:
         mine = lax.axis_index("dp")
-        ordered = jnp.stack([pick(parts, mine ^ j) for j in range(n)])
-        total = lax.psum_scatter(ordered, "dp", scatter_dimension=0, tiled=False).astype(F32)
-        return (total, None if during is None else during[0](*during[1]))
+        ordered = jnp.stack([pick(parts[0], mine ^ j) for j in range(n)])
+        return [lax.psum_scatter(ordered, "dp", scatter_dimension=0, tiled=False)]
+    send_a, keep_a, send_b, keep_b = parts
+    with jax.named_scope(what):
+        return [keep_a, keep_b, swap(send_a, "dp", 1, n), swap(send_b, "dp", 2, n)]
+
+
+def reduce_second(state, n, what):
+    if n != 4:
+        return [(state[0], "all")]
+    keep_a, keep_b, got_a, got_b = state
+    with jax.named_scope(what):
+        on_a = (keep_a[1].astype(F32) + got_a[1].astype(F32)).astype(BF)
+        on_b = (keep_b[1].astype(F32) + got_b[1].astype(F32)).astype(BF)
+        last_a = swap(on_a, "dp", 2, n)
+        last_b = swap(on_b, "dp", 1, n)
+    lower = [(x, "lower") for x in (keep_a, got_a, last_a)]
+    return lower + [(x, "upper") for x in (keep_b, got_b, last_b)]
+
+
+def split_sums(parts, n):
+    if n != 4:
+        return [parts]
     half = parts.shape[1] // 2
-    a, b = parts[:, :half], parts[:, half:]
-    send_a, send_b = tie(jnp.stack([a[1], a[3]]), jnp.stack([b[2], b[3]]))
-    got_a = swap(send_a, "dp", 1, n)
-    got_b = swap(send_b, "dp", 2, n)
-    work = None
-    if during is not None:
-        function, args = during
-        work = function(*after(args, send_a, send_b))
-        got_a, got_b, work = tie(got_a, got_b, work)
-    on_a = (a[2].astype(F32) + got_a[1].astype(F32)).astype(BF)
-    on_b = (b[1].astype(F32) + got_b[1].astype(F32)).astype(BF)
-    last_a = swap(on_a, "dp", 2, n)
-    last_b = swap(on_b, "dp", 1, n)
-    sum_a = a[0].astype(F32) + got_a[0].astype(F32) + last_a.astype(F32)
-    sum_b = b[0].astype(F32) + got_b[0].astype(F32) + last_b.astype(F32)
-    return jnp.concatenate([sum_a, sum_b], axis=0), work
+    out = []
+    for upper in range(2):
+        side = parts[:, upper * half : (upper + 1) * half]
+        out += [jnp.stack([side[k] for k in pair]) for pair in QUARTERS[upper]]
+    return out
+
+
+def add_up(terms):
+    sums = {}
+    for array, kind in terms:
+        part = (array if array.ndim == 3 else array[0]).astype(F32)
+        sums[kind] = part if kind not in sums else sums[kind] + part
+    if "all" in sums:
+        return sums["all"]
+    return jnp.concatenate([sums["lower"], sums["upper"]], axis=0)
 
 
 def both_cores(block, what):
@@ -801,23 +1043,22 @@
     return jnp.stack(moved(sends(groups, z ^ d, z_count), "z", what))
 
 
-def from_groups(groups, n, what):
-    d, z = lax.axis_index("dp"), lax.axis_index("z")
-    return jnp.stack(moved(sends(groups, z ^ d, n), "dp", what))
-
-
-def from_both(parts, what):
-    n = parts.shape[0]
+def from_both(groups, q, what):
+    n = len(groups)
     d, core = lax.axis_index("dp"), lax.axis_index("core")
     half = n // 2
+    parts = jnp.stack([group[:q] for group in groups])
+    sums = jnp.stack([group[q:] for group in groups])
 
     def side(c):
         return jnp.concatenate([pick(parts, (half * c + i) ^ d) for i in range(half)], axis=0)
 
     with jax.named_scope(what):
-        other = lax.ppermute(side(1 - core), "core", [(0, 1), (1, 0)])
+        other, more = lax.ppermute((side(1 - core), sums), "core", [(0, 1), (1, 0)])
     keep = side(core)
-    return jnp.stack([jnp.where(core == 0, keep, other), jnp.where(core == 0, other, keep)])
+    sums = sums.astype(F32) + more.astype(F32)
+    both = jnp.stack([jnp.where(core == 0, keep, other), jnp.where(core == 0, other, keep)])
+    return both, [pick(sums, d ^ j) for j in range(n)]
 
 
 def on_device(
@@ -858,17 +1099,6 @@
     core = lax.axis_index("core")
     shift = jnp.stack([d, z]).astype(jnp.int32)
 
-    small_len = 5 * conv_f + gate_f + 3 * heads_f
-    small_cols = -(-small_len // d_rows)
-
-    def small_split(flat):
-        sizes = (4 * conv_f, conv_f, gate_f, heads_f, heads_f, heads_f)
-        parts, at = [], 0
-        for size in sizes:
-            parts.append(flat[..., at : at + size])
-            at += size
-        return parts
-
     small_lanes = max(-(-max(conv_f, gate_f) // LANES), 3) * LANES
 
     def small_unpack(everything):
@@ -913,6 +1143,29 @@
     def weight_out(parts):
         return place(shift, parts, 1).reshape(cd, width_d)
 
+    every = ("dp", "z", "core")
+
+    def at_device(i, j, c):
+        return (i * z_count + j) * 2 + c
+
+    both_ways = [
+        (at_device(i, g // 2, g % 2), at_device(g % n, i, g // n))
+        for i in range(n)
+        for g in range(2 * n)
+    ]
+
+    def to_slices(own, what):
+        with jax.named_scope(what):
+            return lax.ppermute(own, every, [(b, a) for a, b in both_ways])
+
+    def to_owners(piece, what):
+        with jax.named_scope(what):
+            return lax.ppermute(piece, every, both_ways)
+
+    def grad_out_sum(d_out):
+        pieces = d_out.reshape(owners, out_part, width_d)
+        return lax.psum_scatter(pieces, PLANE, scatter_dimension=0)
+
     def grad_out_sends(d_out):
         return sends(d_out.reshape(2, n, out_part, width_d).transpose(1, 0, 2, 3), d, n)
 
@@ -920,62 +1173,80 @@
         rows_all = place(shift, by_rows, 0).reshape(owners, out_part, width_d)
         return lax.psum_scatter(rows_all, PLANE, scatter_dimension=0)
 
-    def small_out(wide_sums, head_sums):
-        conv_full = jnp.concatenate([jnp.zeros((5, inner), F32), wide_sums[:5, cd:]], axis=1)
-        conv_full = lax.dynamic_update_slice(conv_full, wide_sums[:5, :cd], (0, d * cd))
-        conv_full = conv_full.reshape(5, owners, conv_f).transpose(1, 0, 2).reshape(owners, -1)
-        gain_full = lax.dynamic_update_slice(jnp.zeros((inner,), F32), wide_sums[6, :cd], (d * cd,))
-        skip_sum = jnp.sum(wide_sums[5, :cd].reshape(hd, HEAD_DIM), axis=1)
-        head_full = lax.dynamic_update_slice(
-            jnp.zeros((3, heads), F32),
-            jnp.stack([head_sums[0, :hd], head_sums[1, :hd], skip_sum]),
-            (0, d * hd),
-        )
-        head_full = head_full.reshape(3, owners, heads_f).transpose(1, 0, 2).reshape(owners, -1)
-        small = jnp.concatenate([conv_full, gain_full.reshape(owners, gate_f), head_full], axis=1)
-        small = jnp.pad(small, ((0, 0), (0, small_cols * d_rows - small_len)))
-        return small.reshape(owners * d_rows, small_cols)
-
-    def grad_in(unit_cat, d_mixed, wide_sums, head_sums):
-        small = small_out(wide_sums, head_sums)
-        product = mm_at(flat(unit_cat), flat(d_mixed))
-        return (
-            product + jnp.pad(small, ((0, 0), (step_at + hd, LANES - hd - small_cols)))
-        ).astype(BF)
+    def grad_in(unit_cat, d_mixed):
+        return mm_at(flat(unit_cat), flat(d_mixed)).astype(BF)
 
     out_padded = -(-out_part // 16) * 16
 
-    def owned_parts(own_in, own_out, what):
+    def owned_first(own_in, own_out, what):
         own_out = jnp.pad(own_out, ((0, out_padded - out_part), (0, 0)))
-        if width_in < width_d:
-            return joined(gather_rows(own_in, n, what)[0]), joined(gather_rows(own_out, n, what)[0])
+        if n != 4:
+            return tuple(
+                gather_second(gather_first(x, n, what), n, what) for x in (own_in, own_out)
+            )
         own_out = jnp.pad(own_out, ((0, 0), (0, width_in - width_d)))
-        return joined(gather_rows(jnp.concatenate([own_in, own_out], axis=0), n, what)[0]), None
+        both = jnp.concatenate([own_in, own_out], axis=0)
+        with jax.named_scope(what):
+            return both, swap(both, "dp", 1, n), swap(both, "dp", 2, n)
+
+    def owned_second(state, what, later=None):
+        if n != 4:
+            return state if later is None else (state, later)
+        own, first, second = state
+        half = own.shape[0] // 2
+        with jax.named_scope(what):
+            items = first[:half], second[half:]
+            if later is not None:
+                *items, later = tie(*items, later)
+            low = swap(items[0], "dp", 2, n)
+            high = swap(items[1], "dp", 1, n)
+        out = [own, first, second, jnp.concatenate([low, high], axis=0)], None
+        return out if later is None else (out, later)
 
     def finished_layer(layer, owned, before):
         parts, apart = owned
-        at = slice(step_at + hd, step_at + hd + small_cols)
-        small = sum(part[:d_rows, at].astype(F32) for part in parts)
-        small = small_split(small.reshape(-1)[:small_len])
-        steps = jnp.stack([part[:d_rows, step_at : step_at + hd] for part in parts])
-        steps = jnp.stack([pick(steps, d ^ j) for j in range(n)]).astype(F32)
-        steps = steps.transpose(0, 2, 1).reshape(heads, d_rows)
         gain = norm_gain[layer].astype(F32)
-        in_all, out_all, norm_grad = finish(
-            layer, shift, parts, apart, input_proj, gain, out_part, width_d, before, cd, inner
+        *buffers, norm, norm_row = finish(
+            layer,
+            shift,
+            parts,
+            apart,
+            input_proj,
+            step_proj,
+            gain,
+            out_part,
+            width_d,
+            before,
+            cd,
+            inner,
         )
-        norm_grad = norm_grad[:, 0] + jnp.sum(steps * step_proj[layer].astype(F32), axis=0)
-        rest = (
-            norm_grad,
-            steps * gain[None, :],
-            small[0].reshape(4, conv_f),
-            small[1],
-            small[3],
-            small[4],
-            small[5],
-            small[2],
+        return buffers, norm[:, 0] + norm_row[0]
+
+    def small_rows(*sums):
+        rows = jnp.concatenate(
+            [jnp.concatenate(sums[2 * l : 2 * l + 2], axis=1) for l in range(layers)]
         )
-        return (in_all, out_all), rest
+        return jnp.pad(rows, ((0, 0), (0, width_d - rows.shape[1]))).astype(BF)
+
+    def small_owned(parts):
+        parts = [part.reshape(layers, 8, part.shape[1]) for part in parts]
+        f = 2 * z + core
+
+        def mine(x, width):
+            return lax.dynamic_slice_in_dim(x, f * width, width, x.ndim - 1)
+
+        conv = jnp.concatenate(
+            [part[:, :5, :cd] for part in parts]
+            + [sum(part[:, :5, cd:conv_ch] for part in parts)],
+            axis=2,
+        )
+        conv = mine(conv, conv_f)
+        gain = mine(jnp.concatenate([part[:, 6, :cd] for part in parts], axis=1), gate_f)
+        skip = jnp.concatenate([part[:, 5, :cd] for part in parts], axis=1)
+        skip = mine(jnp.sum(skip.reshape(layers, heads, HEAD_DIM), axis=2), heads_f)
+        at = slice(conv_ch, conv_ch + hd)
+        both = mine(jnp.concatenate([part[:, :2, at] for part in parts], axis=2), heads_f)
+        return conv[:, :4], conv[:, 4], both[:, 0], both[:, 1], skip, gain
 
     both = lax.ppermute(
         doc_lengths,
@@ -1000,12 +1271,6 @@
     def flat(x):
         return x.reshape(-1, x.shape[-1])
 
-    def norm_back(back, resid, inv, normed_grad):
-        u = resid * inv
-        return back + inv * (
-            normed_grad - u * jnp.mean(normed_grad * u, axis=-1, keepdims=True)
-        )
-
     both = both_cores(hidden_in, "hidden_cores")
     small = (
         conv_weight.reshape(layers * 4, conv_f),
@@ -1018,6 +1283,7 @@
     shard0 = weight_shard(
         shift, 0, input_proj, step_proj, norm_gain[0].astype(F32), cd, hd, small
     )
+    column0 = lax.all_gather(shard_out(0), PLANE)
     both, shard0 = tie(both, shard0)
     w_in0 = lax.all_gather(shard0, PLANE)
     groups = to_groups(both, n, "hidden_groups")
@@ -1025,126 +1291,165 @@
     inv0, unit = normalize(resid0)
     unit = unit.astype(BF)
     shard1 = weight_shard(shift, 1, input_proj, step_proj, norm_gain[1].astype(F32), cd, hd)
-    shard_out0, shard1, shard_out1, unit = tie(shard_out(0), shard1, shard_out(1), unit)
-    column0 = lax.all_gather(shard_out0, PLANE)
+    shard1, shard_out1, unit, column0 = tie(shard1, shard_out(1), unit, column0)
     w_in1 = lax.all_gather(shard1, PLANE)
-    column1 = lax.all_gather(shard_out1, PLANE)
-    units0, w_in0 = gather_rows(unit, n, "unit0", w_in0)
+    state = gather_first(unit, n, "unit0")
+    parts = moved(column_sends(column0), "dp", "weight_out0")
+    state, parts, cot = tie(state, parts, cotangent)
+    units0 = gather_second(state, n, "unit0")
+    w_out0 = weight_out(parts)
+    cot_both = both_cores(cot, "cot_cores")
+    cot_groups = moved(sends(cot_both.reshape(n, q, width_d), d, n), "dp", "cot_groups")
     pcs, phs = small_unpack(w_in0[:, d_rows:, :small_lanes])
 
-    items, w_in0 = tie(column_sends(after(column0, *flat_shards(units0))), w_in0)
-    parts = moved(items, "dp", "weight_out0")
-    _, mixed0, gated0, pre0, ssd0, states0, sums0 = layer0 = mixer_forward(
-        shift, units0, w_in0, False, age, pcs[0], phs[0]
+    unit_cat0, mixed0, gated0, pre0, ssd0, states0, *sent = mixer_forward(
+        shift, units0, w_in0, w_out0, age, pcs[0], phs[0]
     )
-    unit_cat0 = layer0[0]
-    parts, gated0 = tie(parts, gated0)
-    w_out0 = weight_out(parts)
-    sent = mm(flat(gated0), w_out0).astype(BF).reshape(n, z_count, q, width_d)
-    sent = jnp.concatenate([sent, sums0], axis=-1)
-    cot_both = both_cores(after(cotangent, sent), "cot_cores")
-    cot_items = sends(cot_both.reshape(n, q, width_d), d, n)
-    cot_groups = moved(cot_items, "dp", "cot_groups")
-    got, _ = reduce_rows(sent, n, "product0")
-    squares = jnp.sum(got[..., width_d:], axis=-1, keepdims=True)
-    ginv0 = lax.rsqrt(squares / inner + EPSILON)
-    branch0 = got[..., :width_d] * ginv0
-    resid1 = resid0 + branch0
-
-    inv1, unit = normalize(resid1)
-    unit, *cot_groups = tie(unit.astype(BF), *cot_groups)
+    sent, cot_groups, shard_out1 = tie(sent, cot_groups, shard_out1)
+    state = reduce_first(sent, n, "product0")
     cot_chunks = moved(sends(jnp.stack(cot_groups), z ^ d, z_count), "z", "cot_chunks")
-    units1, _ = gather_rows(unit, n, "unit1")
-    cot_chunks, units1 = tie(cot_chunks, units1)
+    state, shard_out1 = tie(state, shard_out1)
+    terms = reduce_second(state, n, "product0")
+    piece1 = to_slices(shard_out1, "weight_out1")
+    terms, cot_chunks = tie_terms(terms, cot_chunks)
+    resid1, branch0, ginv0, inv1, unit = settle_forward(terms, resid0, inner)
+
+    state = gather_first(unit, n, "unit1")
+    piece1, state = tie(piece1, state)
+    w_out1 = lax.all_gather(piece1, PLANE).reshape(cd, width_d)
+    units1 = gather_second(state, n, "unit1")
+    cot_chunks, units1, w_in1 = tie(cot_chunks, units1, w_in1)
     upstream = jnp.stack(cot_chunks)
-    items, w_in1 = tie(column_sends(after(column1, *flat_shards(units1))), w_in1)
-    parts = moved(items, "dp", "weight_out1")
+    state = gather_first(upstream, n, "upstream")
     unit_cat1, mixed1, gated1, pre1, ssd1, states1, sums1 = mixer_forward(
-        shift, units1, w_in1, True, age, pcs[1], phs[1]
+        shift, units1, w_in1, None, age, pcs[1], phs[1]
     )
-    upstream_parts, gated1 = gather_rows(upstream, n, "upstream", gated1)
-    parts, gated1 = tie(parts, gated1)
-    upstream_all = place(shift, joined(upstream_parts), 0)
-    w_out1 = weight_out(parts)
+    state, gated1, sums1 = tie(state, gated1, sums1)
+    upstream_parts = gather_second(state, n, "upstream")
+
+    def summed(totals, what):
+        shape = totals.shape
+        totals = totals.reshape(-1, row_len // LANES, LANES)
+        bit = 1
+        while bit < n:
+            with jax.named_scope(what):
+                totals = totals + swap(totals, "dp", bit, n)
+            bit *= 2
+        return totals.reshape(shape)
+
+    s1 = summed(jnp.sum(sums1.astype(F32), axis=-1), "sum1")
+    ginv1 = lax.rsqrt(s1 / inner + EPSILON)
+    upstream_parts = joined(upstream_parts)
+    upstream_all = place(shift, upstream_parts, 0)
     gg1 = mm_bt(flat(upstream_all), w_out1).reshape(n, z_count, q, cd)
-    s1 = jnp.sum(sums1.astype(F32), axis=-1)
     s2 = jnp.sum(gg1 * gated1.astype(F32), axis=-1)
-    totals = jnp.stack([s1, s2]).reshape(2, row_len // LANES, LANES)
-    bit = 1
-    while bit < n:
-        with jax.named_scope("totals"):
-            totals = totals + swap(totals, "dp", bit, n)
-        bit *= 2
-    totals = totals.reshape(2, n, z_count, q)
-    ginv1 = lax.rsqrt(totals[0] / inner + EPSILON)
-    scales = jnp.stack([ginv1, ginv1 * ginv1 * ginv1 * totals[1] / inner], axis=-1)
-    relative1 = jnp.stack([pick(gated1, d ^ k) for k in range(n)])
-    sent1 = mm(flat(relative1), w_out1).astype(BF).reshape(n, z_count, q, width_d)
+    weighted, s2 = tie((gated1.astype(F32) * ginv1[..., None]).astype(BF), s2)
+    d_out1 = mm_at(flat(weighted), flat(upstream_all)).astype(BF)
+    sent1 = mm(flat(after(gated1, s2)), w_out1).astype(BF).reshape(n, z_count, q, width_d)
+    s2, d_out1, sent1 = tie(summed(s2, "sum2"), d_out1, sent1)
+    scales = jnp.stack([ginv1, ginv1 * ginv1 * ginv1 * s2 / inner], axis=-1)
     own = pick(ginv1, d)[..., None]
 
-    weighted = (gated1.astype(F32) * ginv1[..., None]).astype(BF)
-    d_out1 = mm_at(flat(weighted), flat(upstream_all)).astype(BF)
-    items, sent1, gg1 = tie(grad_out_sends(d_out1), sent1, gg1)
-    by_rows = moved(items, "dp", "grad_out1")
-
-    def backward1(gg1):
-        return mixer_backward(
-            shift, gg1, scales, None, w_in1, mixed1, age, pcs[1], phs[1], pre1, ssd1, states1,
-            width_d,
-        )
-
-    total1, (d_mixed, sent, wide_sums, head_sums) = reduce_rows(
-        sent1, n, "product1", (backward1, (gg1,))
+    total1 = lax.psum_scatter(sent1, "dp", scatter_dimension=0)
+    sum_out1 = grad_out_sum(d_out1)
+    d_mixed, wide_sums1, head_sums1, *sent = mixer_backward(
+        shift,
+        gg1,
+        scales,
+        None,
+        w_in1,
+        mixed1,
+        age,
+        pcs[1],
+        phs[1],
+        pre1,
+        ssd1,
+        states1,
+        width_d,
     )
-    by_rows, sent = tie(by_rows, sent)
-    own_out1 = grad_out_owned(by_rows)
-    normed_grad, d_in1 = reduce_rows(
-        sent, n, "back1", (grad_in, (unit_cat1, d_mixed, wide_sums, head_sums))
-    )
+    total1, sent = tie(total1, sent)
+    state = reduce_first(sent, n, "back1")
+    hidden_out = (resid1 + total1.astype(F32) * own).astype(BF)
+    out_chunks = moved([hidden_out[k] for k in range(z_count)], "z", "hidden_out_chunks")
+    d_in1 = grad_in(*after((unit_cat1, d_mixed), sent))
+    state, d_in1 = tie(state, d_in1)
     own_in1 = lax.psum_scatter(d_in1, PLANE, scatter_dimension=0, tiled=True)
-    back1 = norm_back(upstream.astype(F32), resid1, inv1, normed_grad)
-
-    low = back1.astype(BF).astype(F32)
-    mean = jnp.sum(low * branch0, axis=-1, keepdims=True) / inner
-    kappa = ginv0 * ginv0 * mean
-    high = kappa.astype(BF)
-    rest = (kappa - high.astype(F32)).astype(BF)
-    payload = jnp.concatenate(
-        [(low * ginv0).astype(BF), high, rest, jnp.zeros((z_count, q, LANES - 2), BF)], axis=-1
-    )
-    hidden_out = (resid1 + after(total1, payload) * own).astype(BF)
-    out_chunks = moved([hidden_out[k] for k in range(z_count)], "z", "hidden_out_chunks")
-    g_all, _ = gather_rows(payload, n, "branch_grad0")
-    out_chunks, g_all = tie(out_chunks, g_all)
+    terms = reduce_second(state, n, "back1")
+    back1, payload = settle_backward(terms, resid1, inv1, upstream, inner, branch0, ginv0)
+
+    payload, sum_out1 = tie(payload, sum_out1)
+    own_out1 = to_owners(sum_out1, "grad_out1")
+    g_all = gather_second(gather_first(payload, n, "branch_grad0"), n, "branch_grad0")
     d_out0 = mm_at(flat(gated0), flat(jnp.stack(joined(g_all)))[:, :width_d]).astype(BF)
     items, g_all = tie(grad_out_sends(d_out0), g_all)
     by_rows = moved(items, "dp", "grad_out0")
-    d_mixed, sent, wide_sums, head_sums = mixer_backward(
-        shift, g_all, None, w_out0, w_in0, mixed0, age, pcs[0], phs[0], pre0, ssd0, states0,
+    d_mixed, wide_sums0, head_sums0, *sent = mixer_backward(
+        shift,
+        g_all,
+        None,
+        w_out0,
+        w_in0,
+        mixed0,
+        age,
+        pcs[0],
+        phs[0],
+        pre0,
+        ssd0,
+        states0,
         width_d,
     )
-    by_rows, sent = tie(by_rows, sent)
+    own_in1, own_out1, by_rows, sent, out_chunks = tie(
+        own_in1, own_out1, by_rows, sent, out_chunks
+    )
+    state = reduce_first(sent, n, "back0")
     own_out0 = grad_out_owned(by_rows)
-    normed_grad, d_in0 = reduce_rows(
-        sent, n, "back0", (grad_in, (unit_cat0, d_mixed, wide_sums, head_sums))
+    d_in0 = grad_in(*after((unit_cat0, d_mixed), sent))
+    sums = small_rows(wide_sums0, head_sums0, wide_sums1, head_sums1)
+    state, d_in0, sums = tie(state, d_in0, sums)
+    own_in0 = lax.psum_scatter(d_in0, PLANE, scatter_dimension=0, tiled=True)
+    terms = reduce_second(state, n, "back0")
+    terms, (own_in1, own_out1) = tie_terms(terms, (own_in1, own_out1))
+    (back0,) = settle_backward(terms, resid0, inv0, back1, inner)
+
+    items = [jnp.concatenate([back0[k], sums], axis=0) for k in range(z_count)]
+    chunks = moved(items, "z", "back_chunks")
+    first = owned_first(*after((own_in1, own_out1), items), "owned1")
+    chunks, first = tie(chunks, first)
+    sums = sum(chunk[q:].astype(F32) for chunk in chunks).astype(BF)
+    both = jnp.stack(
+        [jnp.concatenate([x[:q], y], axis=1) for x, y in zip(chunks, out_chunks)]
     )
-    own_in0 = lax.psum_scatter(d_in0, PLANE, scatter_dimension=0, tiled=True)
-    back0 = norm_back(back1, resid0, inv0, normed_grad).astype(BF)
-    own_in1, own_out1, back0 = tie(own_in1, own_out1, back0)
-    back_chunks = moved([back0[k] for k in range(z_count)], "z", "back_chunks")
-    owned1 = owned_parts(own_in1, own_out1, "owned1")
-    back_chunks, owned1 = tie(back_chunks, owned1)
-    back_groups = from_groups(jnp.stack(back_chunks), n, "back_groups")
-    buffers, rest1 = finished_layer(1, owned1, None)
-    back_groups, buffers = tie(back_groups, buffers)
-    hidden_grad = from_both(back_groups, "back_cores").astype(F32)
-    out_groups = from_groups(jnp.stack(after(out_chunks, back_groups)), n, "hidden_out_groups")
-    hidden_out = from_both(out_groups, "hidden_out_cores")
-    own_in0, own_out0, buffers, out_groups = tie(own_in0, own_out0, buffers, out_groups)
-    owned0 = owned_parts(own_in0, own_out0, "owned0")
-    buffers, rest0 = finished_layer(0, owned0, buffers)
-    stacked = tuple(jnp.stack([first, second]) for first, second in zip(rest0, rest1))
-    return (hidden_out, hidden_grad, stacked[0], buffers[0], *stacked[1:], buffers[1])
+    sums = jnp.pad(sums, ((0, 0), (0, width_d)))
+    items = [jnp.concatenate([item, sums], axis=0) for item in sends(both, z ^ d, n)]
+    groups = moved(items, "dp", "back_groups")
+    owned1 = owned_second(after(first, items), "owned1")
+    groups, owned1, own_in0, own_out0 = tie(groups, owned1, own_in0, own_out0)
+    buffers, norm1 = finished_layer(1, owned1, None)
+    first = owned_first(own_in0, own_out0, "owned0")
+    results, sums = from_both(groups, q, "back_cores")
+    first, results, buffers = tie(first, results, buffers)
+    owned0, sums = owned_second(first, "owned0", sums)
+    hidden_grad = results[..., :width_d].astype(F32)
+    hidden_out = results[..., width_d:]
+    smalls = small_owned(sums)
+    owned0, hidden_grad, hidden_out, smalls = tie(owned0, hidden_grad, hidden_out, smalls)
+    buffers, norm0 = finished_layer(0, owned0, buffers)
+    norm = jnp.stack([norm0, norm1])
+    conv_grad, conv_bias_grad, bias_grad, decay_grad, skip_grad, gain_grad = smalls
+    return (
+        hidden_out,
+        hidden_grad,
+        norm,
+        buffers[0],
+        buffers[2],
+        conv_grad,
+        conv_bias_grad,
+        bias_grad,
+        decay_grad,
+        skip_grad,
+        gain_grad,
+        buffers[1],
+    )
 
 
 def solution(mesh):

time: 741 us -> 678 us (0.915)
  other arithmetic: 56.9 us -> 32.2 us
  local copies, waits for them, and re-layouts: 84.1 us -> 63.7 us
  waiting for transfers between devices: 276 us -> 261 us
  starting transfers between devices: 111 us -> 102 us
    all_gather x2, waiting for transfers between devices: 23.1 us -> 0.01 us  [the longest x1 0.01 us: on_device(): column0 = lax.all_gather(shard_out(0), PLANE)]
    all_gather x1, waiting for transfers between devices: 17.9 us -> 0.01 us  [on_device(): w_in0 = lax.all_gather(shard0, PLANE)]
    ppermute x78 -> x67, starting transfers between devices: 109 us -> 95.7 us  [swap(): return lax.ppermute(value, axis, [(i, i ^ k) for i in range(size)])]
    ppermute x78 -> x67, waiting for transfers between devices: 234 us -> 245 us  [swap(): return lax.ppermute(value, axis, [(i, i ^ k) for i in range(size)])]
    another operation x24 -> x14, other arithmetic: 13.7 us -> 3.35 us  [the longest x2 1.41 us: on_device(): scales = jnp.stack([ginv1, ginv1 * ginv1 * ginv1 * s2 / inner], axis=-1)]
    another operation x34 -> x9, local copies, waits for them, and re-layouts: 15.8 us -> 6.92 us  [the longest x4 3.17 us: from_both(): parts = jnp.stack([group[:q] for group in groups])]
    reduce_scatter x1, waiting for transfers between devices: 0.01 us -> 8.58 us  [on_device(): own_in0 = lax.psum_scatter(d_in0, PLANE, scatter_dimension=0, tiled=True)]
    pallas_call x2 -> x5, Pallas kernels: 12.4 us -> 18 us  [the longest x2 10.7 us: finish(): pl.pallas_call(partial(finish_kernel, count=count, cd=cd, hd=heads // cou...]
  transfers between devices with their start and end apart: 91 -> 83, of which waited for: 42 -> 44; matrix products, arithmetic and copies ran while one was open for 18% -> 14% of each run, Pallas kernels for 19% -> 21%
where the time goes in v3:
time: 678 us; the launch traced here: 671 us
  waiting for transfers between devices  261 us (38%)
  Pallas kernels  152 us (22%)
  starting transfers between devices  102 us (15%)
  local copies, waits for them, and re-layouts  63.7 us (9%)
  matrix products  43.9 us (6%)
  other arithmetic  32.2 us (5%)
  between operations  15.9 us (2%)
    ppermute x67, waiting for transfers between devices, swap(): return lax.ppermute(value, axis, [(i, i ^ k) for i in range(size)])  245 us
    ppermute x67, starting transfers between devices, swap(): return lax.ppermute(value, axis, [(i, i ^ k) for i in range(size)])  95.7 us
    pallas_call x2, Pallas kernels, mixer_backward(): pl.pallas_call(partial(backward_kernel, count=count, cd=cd, own_scales=sc...  81.3 us
    pallas_call x2, Pallas kernels, mixer_forward(): pl.pallas_call(partial(forward_kernel, count=count, cd=cd, ordered=ordere...  45.8 us
    dot_general x4, matrix products, mm_at(): lax.dot_general(a, b, (((0,), (0,)), ((), ())), preferred_element_type=F32)  31.7 us
    unnamed x229, local copies, waits for them, and re-layouts  27.4 us
  transfers between devices with their start and end apart: 83, of which 44 were waited for; matrix products, arithmetic and copies ran while one was open for 14% of the time, Pallas kernels for 21%

profile of v3, /device:TPU:0, one launch (start us, length us, event | category | flops | bytes accessed | tf_op | source)
XLA Modules:
  0.0 670.8 jit_solution(8937203048790528428)
XLA Ops:
  36.8 8.6 %collective-permute-done.6 = bf16[64,1536]{1,0:T(8,128)(2,1)S(1)} collective-permute-done((bf16[64,1536]{1,0:T(8,128)(2,1)S(1)}, bf16[64,1536]{1,0:T(8,128)(2,1)S(1)}, u32[]{:S(2)}, u32[]{:S(2)}) %collective-permute-start.6) | collective-permute-done | bytes 196640 | tf_op jit(solution)/shard_map/hidden_chunks/ppermute | solution.py:926
  45.4 14.7 %collective-permute-done.5 = bf16[64,1536]{1,0:T(8,128)(2,1)S(1)} collective-permute-done((bf16[64,1536]{1,0:T(8,128)(2,1)S(1)}, bf16[64,1536]{1,0:T(8,128)(2,1)S(1)}, u32[]{:S(2)}, u32[]{:S(2)}) %collective-permute-start.5) | collective-permute-done | bytes 196640 | tf_op jit(solution)/shard_map/hidden_chunks/ppermute | solution.py:926
  70.8 24.6 %collective-permute-done.9.refs_1_ = bf16[2,96,1536]{2,1,0:T(8,128)(2,1)S(1)} collective-permute-done((bf16[2,96,1536]{2,1,0:T(8,128)(2,1)S(1)}, bf16[2,96,1536]{2,1,0:T(8,128)(2,1)S(1)}, u32[]{:S(2)}, u32[]{:S(2)}) %collective-permute-start.9) | collective-permute-done | bytes 589856 | tf_op jit(solution)/shard_map/weight_out0/ppermute | solution.py:926
  95.5 12.8 %collective-permute-done.10.refs_2_ = bf16[2,96,1536]{2,1,0:T(8,128)(2,1)S(1)} collective-permute-done((bf16[2,96,1536]{2,1,0:T(8,128)(2,1)S(1)}, bf16[2,96,1536]{2,1,0:T(8,128)(2,1)S(1)}, u32[]{:S(2)}, u32[]{:S(2)}) %collective-permute-start.10) | collective-permute-done | bytes 589856 | tf_op jit(solution)/shard_map/weight_out0/ppermute | solution.py:926
  113.4 7.9 %collective-permute-start.12 = (bf16[2,64,1536]{2,1,0:T(8,128)(2,1)}, bf16[2,64,1536]{2,1,0:T(8,128)(2,1)S(1)}, u32[]{:S(2)}, u32[]{:S(2)}) collective-permute-start(bf16[2,64,1536]{2,1,0:T(8,128)(2,1)} %slice.294), channel_id=1, source_target_pairs={{0,16},{8,24},{16,0},{24,8},{1,17},{9,25},{17,1},{25,9},{2,18},{10... | collective-permute-start | bytes 1179656 | tf_op jit(solution)/shard_map/unit0/ppermute | solution.py:926
  135.8 26.0 %shard_map.223 = (bf16[4,256,1536]{2,1,0:T(8,128)(2,1)}, f32[4,256,1920]{2,1,0:T(8,128)}, bf16[4,4,64,768]{3,2,1,0:T(8,128)(2,1)}, f32[4,256,1024]{2,1,0:T(8,128...) custom-call(s32[2]{0:T(128)S(1)} %pad_add_fusion.1.at_ref.shift_ref,, ...), custom_call_target="tpu_custom_call" | custom-call | flops 1000000 | bytes 100000 | tf_op jit(solution)/shard_map/pallas_call | solution.py:496
  164.1 15.7 %collective-permute-done.19.refs_1_ = bf16[2,2,64,1664]{3,2,1,0:T(8,128)(2,1)S(1)} collective-permute-done((bf16[2,2,64,1664]{3,2,1,0:T(8,128)(2,1)}, bf16[2,2,64,1664]{3,2,1,0:T(8,128)(2,1)S(1)}, u32[]{:S(2)}, u32[]{:S(2)}) %collective-permute-start.19) | collective-permute-done | bytes 852000 | tf_op jit(solution)/shard_map/product0/ppermute | solution.py:926
  206.0 15.0 %collective-permute-done.27.refs_1_ = bf16[4,64,1536]{2,1,0:T(8,128)(2,1)} collective-permute-done((bf16[4,64,1536]{2,1,0:T(8,128)(2,1)S(1)}, bf16[4,64,1536]{2,1,0:T(8,128)(2,1)}, u32[]{:S(2)}, u32[]{:S(2)}) %collective-permute-start.27) | collective-permute-done | bytes 786464 | tf_op jit(solution)/shard_map/unit1/ppermute | solution.py:926
  241.7 19.8 %shard_map.225 = (bf16[4,256,1536]{2,1,0:T(8,128)(2,1)}, f32[4,256,1920]{2,1,0:T(8,128)}, bf16[4,4,64,768]{3,2,1,0:T(8,128)(2,1)}, f32[4,256,1024]{2,1,0:T(8,128...) custom-call(s32[2]{0:T(128)S(1)} %pad_add_fusion.1.at_ref.shift_ref, ...), custom_call_target="tpu_custom_call" | custom-call | flops 1000000 | bytes 100000 | tf_op jit(solution)/shard_map/pallas_call | solution.py:496
  279.6 8.2 %fusion.1 = (f32[4,4,64]{2,1,0:T(4,128)S(1)}, bf16[4,4,64,768]{3,2,1,0:T(8,128)(2,1)}, f32[4,4,64,768]{3,2,1,0:T(8,128)}) fusion(bf16[4,4,64,768]{3,2,1,0:T(8,128)(2,1)} %get-tuple-element.289, f32[4,4,64]{2,1,0:T(4,128)S(1)} %rsqrt.24, bf16[4,4,64,1536]{3,2,1,0:T(8,128)(2,1)} %copy-done.7, bf16[768,1536]{1,0:T(8,128)(2,1)} %all-gather.14.cloned.1.call-done), kind=kOutput, calls=%fused_computation.9 | convolution fusion | flops 2419850240 | bytes 11804672 | tf_op jit(solution)/shard_map/dot_general | solution.py:29
  289.5 6.4 bitcast_convert_fusion.2
  306.6 39.3 %shard_map.227 = (bf16[4,256,1920]{2,1,0:T(8,128)(2,1)}, f32[8,1024]{1,0:T(8,128)S(1)}, f32[8,128]{1,0:T(8,128)S(1)}, bf16[2,2,64,1536]{3,2,1,0:T(8,128)(2,1)S(1...) custom-call(s32[2]{0:T(128)S(1)} %copy-done.41, ...), custom_call_target="tpu_custom_call" | custom-call | flops 40000000000 | bytes 50000000 | tf_op jit(solution)/shard_map/pallas_call | solution.py:579
  351.9 11.2 %bitcast_convert_fusion.1 = bf16[1536,1920]{1,0:T(8,128)(2,1)} fusion(bf16[4,256,1536]{2,1,0:T(8,128)(2,1)} %get-tuple-element.306, bf16[4,256,1920]{2,1,0:T(8,128)(2,1)} %get-tuple-element.307), kind=kOutput, calls=%fused_computation.1 | convolution fusion | flops 6042746880 | bytes 12976128 | tf_op jit(solution)/shard_map/dot_general | solution.py:33
  363.2 6.4 collective-permute-done.39.refs_1_
  393.9 14.5 %collective-permute-done.45.refs_2_ = bf16[4,64,1664]{2,1,0:T(8,128)(2,1)S(1)} collective-permute-done((bf16[4,64,1664]{2,1,0:T(8,128)(2,1)}, bf16[4,64,1664]{2,1,0:T(8,128)(2,1)S(1)}, u32[]{:S(2)}, u32[]{:S(2)}) %collective-permute-start.45) | collective-permute-done | bytes 852000 | tf_op jit(solution)/shard_map/branch_grad0/ppermute | solution.py:926
  436.2 42.0 %shard_map.229 = (bf16[4,256,1920]{2,1,0:T(8,128)(2,1)}, f32[8,1024]{1,0:T(8,128)S(1)}, f32[8,128]{1,0:T(8,128)S(1)}, bf16[2,2,64,1536]{3,2,1,0:T(8,128)(2,1)}, ...) custom-call(s32[2]{0:T(128)S(1)} %copy-done.42, ...), custom_call_target="tpu_custom_call" | custom-call | flops 40000000000 | bytes 50000000 | tf_op jit(solution)/shard_map/pallas_call | solution.py:579
  492.5 11.1 %bitcast_convert_fusion = bf16[1536,1920]{1,0:T(8,128)(2,1)} fusion(bf16[4,256,1536]{2,1,0:T(8,128)(2,1)} %get-tuple-element.346, bf16[4,256,1920]{2,1,0:T(8,128)(2,1)} %get-tuple-element.347), kind=kOutput, calls=%fused_computation | convolution fusion | flops 6042746880 | bytes 12976128 | tf_op jit(solution)/shard_map/dot_general | solution.py:33
  513.8 7.4 %collective-permute-done.56.refs_2_ = bf16[2,64,1536]{2,1,0:T(8,128)(2,1)S(1)} collective-permute-done((bf16[2,64,1536]{2,1,0:T(8,128)(2,1)}, bf16[2,64,1536]{2,1,0:T(8,128)(2,1)S(1)}, u32[]{:S(2)}, u32[]{:S(2)}) %collective-permute-start.56) | collective-permute-done | bytes 393248 | tf_op jit(solution)/shard_map/back0/ppermute | solution.py:926
  535.9 13.3 %collective-permute-done.58 = bf16[80,1536]{1,0:T(8,128)(2,1)S(1)} collective-permute-done((bf16[80,1536]{1,0:T(8,128)(2,1)S(1)}, bf16[80,1536]{1,0:T(8,128)(2,1)S(1)}, u32[]{:S(2)}, u32[]{:S(2)}) %collective-permute-start.58) | collective-permute-done | bytes 245792 | tf_op jit(solution)/shard_map/back_chunks/ppermute | solution.py:926
  551.7 13.5 %collective-permute-done.60 = bf16[80,1536]{1,0:T(8,128)(2,1)S(1)} collective-permute-done((bf16[80,1536]{1,0:T(8,128)(2,1)S(1)}, bf16[80,1536]{1,0:T(8,128)(2,1)S(1)}, u32[]{:S(2)}, u32[]{:S(2)}) %collective-permute-start.60) | collective-permute-done | bytes 245792 | tf_op jit(solution)/shard_map/back_chunks/ppermute | solution.py:926
  571.5 11.3 %collective-permute-done.67 = bf16[144,1920]{1,0:T(8,128)(2,1)S(1)} collective-permute-done((bf16[144,1920]{1,0:T(8,128)(2,1)S(1)}, bf16[144,1920]{1,0:T(8,128)(2,1)S(1)}, u32[]{:S(2)}, u32[]{:S(2)}) %collective-permute-start.67) | collective-permute-done | bytes 552992 | tf_op jit(solution)/shard_map/owned1/ppermute | solution.py:926
  582.9 8.4 %collective-permute-done.63 = bf16[80,3072]{1,0:T(8,128)(2,1)} collective-permute-done((bf16[80,3072]{1,0:T(8,128)(2,1)}, bf16[80,3072]{1,0:T(8,128)(2,1)}, u32[]{:S(2)}, u32[]{:S(2)}) %collective-permute-start.63) | collective-permute-done | bytes 491552 | tf_op jit(solution)/shard_map/back_groups/ppermute | solution.py:926
  596.8 8.6 %reduce-scatter.12.cloned.1.call-done = bf16[192,1920]{1,0:T(8,128)(2,1)} async-done(((bf16[1536,1920]{1,0:T(8,128)(2,1)}), bf16[192,1920]{1,0:T(8,128)(2,1)}) %reduce-scatter.12.cloned.1.call-update) | async-done | bytes 737296 | tf_op jit(solution)/shard_map/reduce_scatter | solution.py:1409
  645.4 7.5 %collective-permute-done.73 = bf16[144,1920]{1,0:T(8,128)(2,1)} collective-permute-done((bf16[144,1920]{1,0:T(8,128)(2,1)}, bf16[144,1920]{1,0:T(8,128)(2,1)}, u32[]{:S(2)}, u32[]{:S(2)}) %collective-permute-start.73) | collective-permute-done | bytes 552992 | tf_op jit(solution)/shard_map/owned0/ppermute | solution.py:926
  (565 shorter events, 300.7 us)
Async XLA Ops:
  7.2 54.9 %all-gather.8.cloned.1.call-start = ((), (), s32[]{:S(2)}) async-start(), calls=%async_computation.5 | async-start | bytes 2654208 | tf_op jit(solution)/shard_map/all_gather | solution.py:1286
  9.9 121.3 %all-gather.10.cloned.1.call-start = ((), (), s32[]{:S(2)}) async-start(), calls=%async_computation.10 | async-start | bytes 7188480 | tf_op jit(solution)/shard_map/all_gather | solution.py:1288
  17.7 218.9 %all-gather.12.cloned.1.call-start = ((), (), s32[]{:S(2)}) async-start(), calls=%async_computation.11 | async-start | bytes 6635520 | tf_op jit(solution)/shard_map/all_gather | solution.py:1295
  62.1 217.5 %all-gather.14.cloned.1.call-start = ((), (), s32[]{:S(2)}) async-start(), calls=%async_computation.12 | async-start | bytes 2654208 | tf_op jit(solution)/shard_map/all_gather | solution.py:1319
  62.1 46.1 %collective-permute-start.7 = (bf16[4,64,1536]{2,1,0:T(8,128)(2,1)}, bf16[4,64,1536]{2,1,0:T(8,128)(2,1)}, u32[]{:S(2)}, u32[]{:S(2)}) collective-permute-start(bf16[4,64,1536]{2,1,0:T(8,128)(2,1)} %multiply_convert_fusion.refs_0_), channel_id=1, source_target_pairs={{0,8},{8,0},{16,24},{24,16},{1,9},{9,1},{17,25},{25,17},{2,10},{10... | collective-permute-start | bytes 2359304 | tf_op jit(solution)/shard_map/unit0/ppermute | solution.py:926
  63.7 44.6 %collective-permute-start.8 = (bf16[4,64,1536]{2,1,0:T(8,128)(2,1)}, bf16[4,64,1536]{2,1,0:T(8,128)(2,1)}, u32[]{:S(2)}, u32[]{:S(2)}) collective-permute-start(bf16[4,64,1536]{2,1,0:T(8,128)(2,1)} %multiply_convert_fusion.refs_0_), channel_id=1, source_target_pairs={{0,16},{8,24},{16,0},{24,8},{1,17},{9,25},{17,1},{25,9},{2,18},{10... | collective-permute-start | bytes 2359304 | tf_op jit(solution)/shard_map/unit0/ppermute | solution.py:926
  67.9 40.4 %collective-permute-start.10 = (bf16[2,96,1536]{2,1,0:T(8,128)(2,1)S(1)}, bf16[2,96,1536]{2,1,0:T(8,128)(2,1)S(1)}, u32[]{:S(2)}, u32[]{:S(2)}) collective-permute-start(bf16[2,96,1536]{2,1,0:T(8,128)(2,1)S(1)} %get-tuple-element.451), channel_id=1, source_target_pairs={{0,16},{8,24},{16,0},{24,8},{1,17},{9,25},{17,1},{25,9},{2,18},{10... | collective-permute-start | bytes 1769480 | tf_op jit(solution)/shard_map/weight_out0/ppermute | solution.py:926
  68.3 40.0 %collective-permute-start.11 = (bf16[2,96,1536]{2,1,0:T(8,128)(2,1)S(1)}, bf16[2,96,1536]{2,1,0:T(8,128)(2,1)S(1)}, u32[]{:S(2)}, u32[]{:S(2)}) collective-permute-start(bf16[2,96,1536]{2,1,0:T(8,128)(2,1)S(1)} %get-tuple-element.450), channel_id=1, source_target_pairs={{0,24},{8,16},{16,8},{24,0},{1,25},{9,17},{17,9},{25,1},{2,26},{10... | collective-permute-start | bytes 1769480 | tf_op jit(solution)/shard_map/weight_out0/ppermute | solution.py:926
  127.7 34.1 %collective-permute-start.16 = (bf16[64,1536]{1,0:T(8,128)(2,1)S(1)}, bf16[64,1536]{1,0:T(8,128)(2,1)S(1)}, u32[]{:S(2)}, u32[]{:S(2)}) collective-permute-start(bf16[64,1536]{1,0:T(8,128)(2,1)S(1)} %get-tuple-element.492), channel_id=1, source_target_pairs={{0,8},{8,0},{16,24},{24,16},{1,9},{9,1},{17,25},{25,17},{2,10},{10... | collective-permute-start | bytes 589832 | tf_op jit(solution)/shard_map/cot_groups/ppermute | solution.py:926
  128.1 33.7 %collective-permute-start.17 = (bf16[64,1536]{1,0:T(8,128)(2,1)S(1)}, bf16[64,1536]{1,0:T(8,128)(2,1)S(1)}, u32[]{:S(2)}, u32[]{:S(2)}) collective-permute-start(bf16[64,1536]{1,0:T(8,128)(2,1)S(1)} %get-tuple-element.491), channel_id=1, source_target_pairs={{0,16},{8,24},{16,0},{24,8},{1,17},{9,25},{17,1},{25,9},{2,18},{10... | collective-permute-start | bytes 589832 | tf_op jit(solution)/shard_map/cot_groups/ppermute | solution.py:926
  128.2 33.6 %collective-permute-start.18 = (bf16[64,1536]{1,0:T(8,128)(2,1)S(1)}, bf16[64,1536]{1,0:T(8,128)(2,1)S(1)}, u32[]{:S(2)}, u32[]{:S(2)}) collective-permute-start(bf16[64,1536]{1,0:T(8,128)(2,1)S(1)} %get-tuple-element.490), channel_id=1, source_target_pairs={{0,24},{8,16},{16,8},{24,0},{1,25},{9,17},{17,9},{25,1},{2,26},{10... | collective-permute-start | bytes 589832 | tf_op jit(solution)/shard_map/cot_groups/ppermute | solution.py:926
  223.0 126.9 %reduce-scatter.16.cloned.1.call-start = ((), (), s32[]{:S(2)}) async-start(), calls=%async_computation.13 | async-start | bytes 3932160
  300.4 89.4 %reduce-scatter.10.cloned.1.call-start = ((), (), s32[]{:S(2)}) async-start(), calls=%async_computation.7 | async-start | bytes 2654208 | tf_op jit(solution)/shard_map/reduce_scatter | solution.py:1167
  304.1 180.3 %reduce-scatter.8.cloned.1.call-start = ((), (), s32[]{:S(2)}) async-start(), calls=%async_computation.6 | async-start | bytes 6635520 | tf_op jit(solution)/shard_map/reduce_scatter | solution.py:1376
  370.7 226.1 %reduce-scatter.14.cloned.1.call-start = ((), (), s32[]{:S(2)}) async-start(), calls=%async_computation.9 | async-start | bytes 2654208 | tf_op jit(solution)/shard_map/reduce_scatter | solution.py:1174
  415.9 62.2 %collective-permute-start.53 = (bf16[64,1536]{1,0:T(8,128)(2,1)S(1)}, bf16[64,1536]{1,0:T(8,128)(2,1)S(1)}, u32[]{:S(2)}, u32[]{:S(2)}) collective-permute-start(bf16[64,1536]{1,0:T(8,128)(2,1)S(1)} %get-tuple-element.482), channel_id=1, source_target_pairs={{0,6},{2,4},{4,2},{6,0},{1,7},{3,5},{5,3},{7,1},{8,14},{10,12},{12... | collective-permute-start | bytes 589832 | tf_op jit(solution)/shard_map/hidden_out_chunks/ppermute | solution.py:926
  418.6 59.6 %collective-permute-start.43 = (bf16[96,1536]{1,0:T(8,128)(2,1)}, bf16[96,1536]{1,0:T(8,128)(2,1)S(1)}, u32[]{:S(2)}, u32[]{:S(2)}) collective-permute-start(bf16[96,1536]{1,0:T(8,128)(2,1)} %bitcast.77), channel_id=1, source_target_pairs={{0,0},{1,8},{2,16},{3,24},{4,1},{5,9},{6,17},{7,25},{8,2},{9,10},{... | collective-permute-start | bytes 884744 | tf_op jit(solution)/shard_map/grad_out1/ppermute | solution.py:1163
  424.9 53.2 %collective-permute-start.48 = (bf16[2,96,1536]{2,1,0:T(8,128)(2,1)S(1)}, bf16[2,96,1536]{2,1,0:T(8,128)(2,1)S(1)}, u32[]{:S(2)}, u32[]{:S(2)}) collective-permute-start(bf16[2,96,1536]{2,1,0:T(8,128)(2,1)S(1)} %get-tuple-element.323), channel_id=1, source_target_pairs={{0,8},{8,0},{16,24},{24,16},{1,9},{9,1},{17,25},{25,17},{2,10},{10... | collective-permute-start | bytes 1769480 | tf_op jit(solution)/shard_map/grad_out0/ppermute | solution.py:926
  428.2 49.9 %collective-permute-start.49 = (bf16[2,96,1536]{2,1,0:T(8,128)(2,1)S(1)}, bf16[2,96,1536]{2,1,0:T(8,128)(2,1)S(1)}, u32[]{:S(2)}, u32[]{:S(2)}) collective-permute-start(bf16[2,96,1536]{2,1,0:T(8,128)(2,1)S(1)} %get-tuple-element.324), channel_id=1, source_target_pairs={{0,16},{8,24},{16,0},{24,8},{1,17},{9,25},{17,1},{25,9},{2,18},{10... | collective-permute-start | bytes 1769480 | tf_op jit(solution)/shard_map/grad_out0/ppermute | solution.py:926
  433.9 44.9 %collective-permute-start.50 = (bf16[2,96,1536]{2,1,0:T(8,128)(2,1)S(1)}, bf16[2,96,1536]{2,1,0:T(8,128)(2,1)S(1)}, u32[]{:S(2)}, u32[]{:S(2)}) collective-permute-start(bf16[2,96,1536]{2,1,0:T(8,128)(2,1)S(1)} %get-tuple-element.325), channel_id=1, source_target_pairs={{0,24},{8,16},{16,8},{24,0},{1,25},{9,17},{17,9},{25,1},{2,26},{10... | collective-permute-start | bytes 1769480 | tf_op jit(solution)/shard_map/grad_out0/ppermute | solution.py:926
  486.5 118.9 %reduce-scatter.12.cloned.1.call-start = ((), (), s32[]{:S(2)}) async-start(), calls=%async_computation.8 | async-start | bytes 6635520 | tf_op jit(solution)/shard_map/reduce_scatter | solution.py:1409
  528.0 37.2 %collective-permute-start.61 = (bf16[288,1920]{1,0:T(8,128)(2,1)S(1)}, bf16[288,1920]{1,0:T(8,128)(2,1)S(1)}, u32[]{:S(2)}, u32[]{:S(2)}) collective-permute-start(bf16[288,1920]{1,0:T(8,128)(2,1)S(1)} %fusion.7.refs_0_), channel_id=1, source_target_pairs={{0,8},{8,0},{16,24},{24,16},{1,9},{9,1},{17,25},{25,17},{2,10},{10... | collective-permute-start | bytes 3317768 | tf_op jit(solution)/shard_map/owned1/ppermute | solution.py:926
  530.0 35.2 %collective-permute-start.62 = (bf16[288,1920]{1,0:T(8,128)(2,1)S(1)}, bf16[288,1920]{1,0:T(8,128)(2,1)S(1)}, u32[]{:S(2)}, u32[]{:S(2)}) collective-permute-start(bf16[288,1920]{1,0:T(8,128)(2,1)S(1)} %fusion.7.refs_0_), channel_id=1, source_target_pairs={{0,16},{8,24},{16,0},{24,8},{1,17},{9,25},{17,1},{25,9},{2,18},{10... | collective-permute-start | bytes 3317768 | tf_op jit(solution)/shard_map/owned1/ppermute | solution.py:926
  534.2 30.9 %collective-permute-start.60 = (bf16[80,1536]{1,0:T(8,128)(2,1)S(1)}, bf16[80,1536]{1,0:T(8,128)(2,1)S(1)}, u32[]{:S(2)}, u32[]{:S(2)}) collective-permute-start(bf16[80,1536]{1,0:T(8,128)(2,1)S(1)} %get-tuple-element.519), channel_id=1, source_target_pairs={{0,6},{2,4},{4,2},{6,0},{1,7},{3,5},{5,3},{7,1},{8,14},{10,12},{12... | collective-permute-start | bytes 737288 | tf_op jit(solution)/shard_map/back_chunks/ppermute | solution.py:926
  (169 other events, 2320.5 us)
Sparse Core Ops, SparseCore 0:
  10.2 46.8 all-gather.7
  59.3 64.4 all-gather.9
  125.4 60.1 all-gather.11
  223.1 35.9 all-gather.13
  300.5 49.3 reduce-scatter.15
  352.1 36.2 reduce-scatter.9
  390.7 93.5 reduce-scatter.7
  487.4 39.3 reduce-scatter.13
  529.8 75.5 reduce-scatter.11
